TPU v7x, 256 devices: a whole 4x4x8 slice. The times are simulated.
256 devices in a mesh: exp: 32 (over z_hi, x, y), tp: 8 (over z_lo, core).
Axes of the slice: x: 4, y: 4, z: 8 (z_hi: 2, z_lo: 4; z = z_hi * 4 + z_lo), core: 2. Of those that a mesh axis runs over, the one named last changes fastest.
Arguments:
- tokens: bfloat16 [1536, 6144], P(('exp', 'tp')), may hold values from -6 to 6
- routes: int32 [1536, 4], P(('exp', 'tp')), may hold values from 0 to 15, all different within a row; in each aligned block of 6 rows (0 to 5, 6 to 11, ...) at most 2 rows name the same one
- up_weight: bfloat16 [32, 6144, 2688], P('exp', None, 'tp'), may hold values from -0.078125 to 0.078125
- gate_pre: bfloat16 [32, 512, 2688], P('exp', None, 'tp'), may hold values from -6 to 6
- grad_hidden: bfloat16 [32, 512, 2688], P('exp', None, 'tp'), may hold values from -4 to 4
Outputs:
- grad_tokens: bfloat16 [1536, 6144], P(('exp', 'tp'))
- grad_weight: bfloat16 [32, 6144, 2688], P('exp', None, 'tp')
Inputs may be any that keep to these rules, and one draw needn't show every extreme that they name: `routes`: each token names 4 different experts; among the 6 tokens of one device no expert is named more than 2 times, a bound that some block reaches.
All inputs are finite; a program needn't handle non-finite values.
Results may differ from a plain program's by a relative error of at most 0.02.
Values may be sent and summed in bfloat16 or wider, within the bound.
No kernel may reach another device: no remote copies, remote signals or barrier semaphores. Data moves between devices by JAX's collectives and lax.ppermute only.
A program may use at most 128 MiB of HBM per device.

v0:
```python
from functools import partial

import jax
import jax.numpy as jnp
from jax import lax
from jax.sharding import PartitionSpec as P

EXPERTS = 16
CAP = 2


def place_table(routes, experts, capacity):
    named_by = jnp.sum(
        (routes[:, :, None] == jnp.arange(experts, dtype=jnp.int32)[None, None, :]).astype(
            jnp.int32
        ),
        axis=1,
    )
    before = jnp.cumsum(named_by, axis=0) - named_by
    placed = (before[:, :, None] == jnp.arange(capacity, dtype=jnp.int32)[None, None, :]) & (
        named_by[:, :, None] > 0
    )
    return placed.astype(jnp.bfloat16)


def body(tokens, routes, up_weight, gate_pre, grad_hidden):
    experts = EXPERTS
    capacity = CAP
    part_count = lax.axis_size("exp")
    slices = lax.axis_size("tp")
    copies_per = part_count // experts
    model_width = tokens.shape[1]
    weight = up_weight[0]
    hidden_units = weight.shape[1]
    scaled = (
        grad_hidden[0].astype(jnp.float32) * jax.nn.silu(gate_pre[0].astype(jnp.float32))
    ).astype(jnp.bfloat16)
    up_grads = scaled.reshape(part_count, slices, capacity, hidden_units)
    per_device = tokens.shape[0]
    every_token = lax.all_gather(tokens, "tp", axis=0, tiled=True)
    every_route = lax.all_gather(routes, "tp", axis=0, tiled=True)
    placed_all = jax.vmap(partial(place_table, experts=experts, capacity=capacity))(
        every_route.reshape(slices, per_device, routes.shape[1])
    )
    outgoing = jnp.einsum(
        "tnec,tnd->etcd",
        placed_all,
        every_token.reshape(slices, per_device, model_width),
        preferred_element_type=jnp.float32,
    ).astype(jnp.bfloat16)
    outgoing = jnp.repeat(outgoing, copies_per, axis=0)
    arrived = lax.all_to_all(outgoing, "exp", split_axis=0, concat_axis=0, tiled=True)
    grad_part = jnp.einsum("qtcd,qtch->dh", arrived, up_grads, preferred_element_type=jnp.float32)
    partial_terms = jnp.einsum(
        "qtch,dh->qtcd", up_grads, weight, preferred_element_type=jnp.float32
    ).astype(jnp.bfloat16)
    returned = lax.all_to_all(partial_terms, "exp", split_axis=0, concat_axis=0, tiled=True)
    spread = returned.reshape(experts, copies_per, slices, capacity, model_width)
    column_terms = jnp.einsum(
        "tnec,estcd->tnd", placed_all, spread, preferred_element_type=jnp.float32
    )
    grad_rows = lax.psum_scatter(
        column_terms.astype(jnp.bfloat16), "tp", scatter_dimension=0, tiled=True
    ).astype(jnp.float32)[0]
    return (grad_rows.astype(jnp.bfloat16), grad_part.astype(jnp.bfloat16)[None])


def solution(mesh):
    in_specs = (
        P(("exp", "tp"), None),
        P(("exp", "tp"), None),
        P("exp", None, "tp"),
        P("exp", None, "tp"),
        P("exp", None, "tp"),
    )
    out_specs = (P(("exp", "tp"), None), P("exp", None, "tp"))
    return jax.shard_map(body, mesh=mesh, in_specs=in_specs, out_specs=out_specs, check_vma=False)
```

profile of v0, /device:TPU:124, one launch (start us, length us, event | category | flops | bytes accessed | tf_op | source)
XLA Modules:
  0.0 395.2 jit_solution(11667610836380514478)
XLA Ops:
  7.2 1.3 multiply_convert_fusion
  8.5 0.2 copy.43
  8.7 0.2 convert_element_type.63
  8.9 7.4 %convolution_convert_fusion = bf16[32,8,2,6144]{3,1,2,0:T(8,128)(2,1)} fusion(bf16[1,6144,336]{1,2,0:T(8,128)(2,1)} %param.7, bf16[32,8,2,336]{3,2,1,0:T(2,128)(2,1)S(1)} %convert_element_type.63), kind=kOutput, calls=%fused_computation.1 | convolution fusion | flops 2117074944 | bytes 10764288 | tf_op jit(solution)/shard_map/qtch,dh->qtcd/dot_general | solution.py:54
  16.3 0.0 copy-start.3
  16.3 0.0 copy-start.2
  16.3 11.4 %all-to-all-start = ((bf16[32,8,2,6144]{3,1,2,0:T(8,128)(2,1)}), bf16[32,8,2,6144]{3,1,2,0:T(8,128)(2,1)}, u32[]{:S(2)}, u32[]{:S(2)}) async-start(bf16[32,8,2,6144]{3,1,2,0:T(8,128)(2,1)} %convolution_convert_fusion), calls=%async_computation | async-start | bytes 12582912 | tf_op jit(solution)/shard_map/all_to_all | solution.py:57
  27.7 0.0 copy-done.3
  27.7 146.4 %all-gather = s32[8,6,4]{1,2,0:T(4,128)S(1)} all-gather(s32[1,6,4]{1,2,0:T(4,128)S(1)} %bitcast.39), channel_id=1, replica_groups=mesh['exp'=32,'tp'=8] {'tp'}, dimensions={0}, use_global_device_ids=true | all-gather | bytes 864 | tf_op jit(solution)/shard_map/all_gather | solution.py:41
  174.1 0.1 copy.40
  174.2 0.1 convert_reduce_fusion.1
  174.3 0.2 reduce-window_subtract_fusion
  174.5 0.0 copy-done.2
  174.6 16.4 %all-gather.1 = bf16[8,6,6144]{2,1,0:T(8,128)(2,1)S(1)} all-gather(bf16[1,6,6144]{2,1,0:T(8,128)(2,1)S(1)} %bitcast.38), channel_id=1, replica_groups=mesh['exp'=32,'tp'=8] {'tp'}, dimensions={0}, use_global_device_ids=true | all-gather | bytes 663552 | tf_op jit(solution)/shard_map/all_gather | solution.py:40
  190.9 1.3 fusion.2
  192.3 1.7 copy.46
  194.0 0.0 all-to-all-done
  194.0 3.7 broadcast_in_dim.4
  197.7 19.9 %all-to-all-start.1 = ((bf16[32,8,2,6144]{3,1,2,0:T(8,128)(2,1)}), bf16[32,8,2,6144]{3,1,2,0:T(8,128)(2,1)}, u32[]{:S(2)}, u32[]{:S(2)}) async-start(bf16[32,8,2,6144]{3,1,2,0:T(8,128)(2,1)} %bitcast.37), calls=%async_computation.2 | async-start | bytes 12582912 | tf_op jit(solution)/shard_map/all_to_all | solution.py:52
  217.6 0.2 reduce-scatter.2.cloned.1.call-start
  217.8 4.4 %convert_reduce_fusion = bf16[16,8,2,6144]{3,1,2,0:T(8,128)(2,1)S(1)} fusion(bf16[32,8,2,6144]{3,1,2,0:T(8,128)(2,1)} %all-to-all-done), kind=kLoop, calls=%fused_computation | loop fusion | flops 4718592 | bytes 9437184 | tf_op jit(solution)/shard_map/tnec,estcd->tnd/reduce_sum | solution.py:59
  222.2 0.0 copy-start
  222.3 0.0 copy-start.1
  222.3 4.4 %fusion.3 = bf16[8,6,6144]{2,1,0:T(8,128)(2,1)} fusion(bf16[16,8,2,6144]{3,1,2,0:T(8,128)(2,1)S(1)} %convert_reduce_fusion, s32[8,6,16]{2,1,0:T(8,128)S(1)} %copy.41, pred[8,6,16]{2,1,0:T(8,128)(4,1)S(1)} %copy.42), kind=kOutput, calls=%fused_computation.8 | convolution fusion | flops 18877440 | bytes 3739392 | tf_op jit(solution)/shard_map/tnec,estcd->tnd/dot_general | solution.py:59
  226.6 0.0 reduce-scatter.2.cloned.1.call-update
  226.7 0.0 copy-done
  226.7 0.2 copy.47
  226.8 0.0 copy-done.1
  226.9 0.2 copy.48
  227.0 0.5 reshape.39
  227.5 0.5 reshape.40
  228.0 153.2 %all-to-all-done.1 = bf16[32,8,2,6144]{3,1,2,0:T(8,128)(2,1)} async-done(((bf16[32,8,2,6144]{3,1,2,0:T(8,128)(2,1)}), bf16[32,8,2,6144]{3,1,2,0:T(8,128)(2,1)}, u32[]{:S(2)}, u32[]{:S(2)}) %all-to-all-start.1) | async-done | bytes 6291488 | tf_op jit(solution)/shard_map/all_to_all | solution.py:52
  381.2 7.2 %fusion.1 = bf16[1,6144,336]{1,2,0:T(8,128)(2,1)} fusion(bf16[32,8,2,6144]{3,1,2,0:T(8,128)(2,1)} %all-to-all-done.1, f32[32,8,2,336]{3,2,1,0:T(2,128)S(1)} %reshape.39, f32[32,8,2,336]{3,2,1,0:T(2,128)S(1)} %reshape.40), kind=kOutput, calls=%fused_computation.5 | convolution fusion | flops 2117025792 | bytes 11796480 | tf_op jit(solution)/shard_map/qtcd,qtch->dh/dot_general | solution.py:53
  388.4 0.0 reduce-scatter.2.cloned.1.call-done
  (3 shorter events, 0.0 us)
Async XLA Ops:
  16.3 11.4 %copy-start.3 = (s32[6,4]{0,1:T(4,128)S(1)}, s32[6,4]{0,1:T(4,128)}, u32[]{:S(2)}) copy-start(s32[6,4]{0,1:T(4,128)} %param.6) | copy-start | bytes 292
  16.3 158.2 %copy-start.2 = (bf16[6,6144]{1,0:T(8,128)(2,1)S(1)}, bf16[6,6144]{1,0:T(8,128)(2,1)}, u32[]{:S(2)}) copy-start(bf16[6,6144]{1,0:T(8,128)(2,1)} %param.5) | copy-start | bytes 221188
  16.3 177.7 %all-to-all-start = ((bf16[32,8,2,6144]{3,1,2,0:T(8,128)(2,1)}), bf16[32,8,2,6144]{3,1,2,0:T(8,128)(2,1)}, u32[]{:S(2)}, u32[]{:S(2)}) async-start(bf16[32,8,2,6144]{3,1,2,0:T(8,128)(2,1)} %convolution_convert_fusion), calls=%async_computation | async-start | bytes 12582912 | tf_op jit(solution)/shard_map/all_to_all | solution.py:57
  197.7 183.5 %all-to-all-start.1 = ((bf16[32,8,2,6144]{3,1,2,0:T(8,128)(2,1)}), bf16[32,8,2,6144]{3,1,2,0:T(8,128)(2,1)}, u32[]{:S(2)}, u32[]{:S(2)}) async-start(bf16[32,8,2,6144]{3,1,2,0:T(8,128)(2,1)} %bitcast.37), calls=%async_computation.2 | async-start | bytes 12582912 | tf_op jit(solution)/shard_map/all_to_all | solution.py:52
  217.6 170.8 %reduce-scatter.2.cloned.1.call-start = ((), (), s32[]{:S(2)}) async-start(), calls=%async_computation.3 | async-start | bytes 884736 | tf_op jit(solution)/shard_map/reduce_scatter | solution.py:62
  222.2 4.4 %copy-start = (bf16[1,512,336]{1,2,0:T(8,128)(2,1)S(1)}, bf16[1,512,336]{1,2,0:T(8,128)(2,1)}, u32[]{:S(2)}) copy-start(bf16[1,512,336]{1,2,0:T(8,128)(2,1)} %param.9) | copy-start | bytes 1032196
  222.3 4.6 %copy-start.1 = (bf16[1,512,336]{1,2,0:T(8,128)(2,1)S(1)}, bf16[1,512,336]{1,2,0:T(8,128)(2,1)}, u32[]{:S(2)}) copy-start(bf16[1,512,336]{1,2,0:T(8,128)(2,1)} %param.8) | copy-start | bytes 1032196
Sparse Core Ops, SparseCore 0:
  226.8 81.4 reduce-scatter.1
where the time goes:
time: 396 us; the launch traced here: 395 us
  blocking collectives  163 us (41%)
  waiting for transfers between devices  153 us (39%)
  starting transfers between devices  31.5 us (8%)
  matrix products  20.3 us (5%)
  between operations  14.2 us (4%)
  local copies, waits for them, and re-layouts  7.21 us (2%)
  other arithmetic  5.97 us (2%)
    all_to_all x1, waiting for transfers between devices, body(): lax.all_to_all(outgoing, 'exp', split_axis=0, concat_axis=0, tiled=True)  153 us
    all_gather x1, blocking collectives, body(): every_route = lax.all_gather(routes, 'tp', axis=0, tiled=True)  146 us
    all_to_all x1, starting transfers between devices, body(): lax.all_to_all(outgoing, 'exp', split_axis=0, concat_axis=0, tiled=True)  19.9 us
    all_gather x1, blocking collectives, body(): every_token = lax.all_gather(tokens, 'tp', axis=0, tiled=True)  16.4 us
    all_to_all x1, starting transfers between devices, body(): lax.all_to_all(partial_terms, 'exp', split_axis=0, concat_axis=0, tiled=T...  11.4 us
  transfers between devices with their start and end apart: 3, of which 1 were waited for; matrix products, arithmetic and copies ran while one was open for 5% of the time, Pallas kernels for 0%

commit v1 on v0

v1 whole, which is shorter than its diff:
```python
import jax
import jax.numpy as jnp
from jax import lax
from jax.sharding import Mesh, PartitionSpec as P

EXPERTS = 16
CAP = 2
FAR = ("zh", "x", "yp")
NEAR = ("yi", "zl", "c")
AXES = FAR + NEAR
SIZES = (2, 4, 2, 2, 4, 2)


def place_table(routes):
    named_by = jnp.sum(
        (routes[:, :, None] == jnp.arange(EXPERTS, dtype=jnp.int32)[None, None, :]).astype(jnp.int32),
        axis=1,
    )
    before = jnp.cumsum(named_by, axis=0) - named_by
    placed = (before[:, :, None] == jnp.arange(CAP, dtype=jnp.int32)[None, None, :]) & (
        named_by[:, :, None] > 0
    )
    return placed.astype(jnp.bfloat16)


def body(tokens, routes, up_weight, gate_pre, grad_hidden):
    weight = up_weight[0]
    width, hidden = weight.shape
    placed = place_table(routes)
    up_grads = (
        grad_hidden[0].astype(jnp.float32) * jax.nn.silu(gate_pre[0].astype(jnp.float32))
    ).astype(jnp.bfloat16)
    up_grads = up_grads.reshape(16, 16, CAP, hidden).transpose(1, 0, 2, 3)
    outgoing = jnp.einsum(
        "tec,td->ecd", placed, tokens, preferred_element_type=jnp.float32
    ).astype(jnp.bfloat16)
    arrived = lax.all_to_all(outgoing, FAR, split_axis=0, concat_axis=0, tiled=True)
    terms = jnp.einsum(
        "gsch,dh->gscd", up_grads, weight, preferred_element_type=jnp.float32
    ).astype(jnp.bfloat16)
    summed = lax.psum_scatter(terms, NEAR, scatter_dimension=0, tiled=False)
    rows = lax.all_gather(arrived, NEAR, axis=0, tiled=False)
    returned = lax.all_to_all(summed, FAR, split_axis=0, concat_axis=0, tiled=True)
    grad_part = jnp.einsum("gscd,gsch->dh", rows, up_grads, preferred_element_type=jnp.float32)
    grad_rows = jnp.einsum("tec,ecd->td", placed, returned, preferred_element_type=jnp.float32)
    return (grad_rows.astype(jnp.bfloat16), grad_part.astype(jnp.bfloat16)[None])


def solution(mesh):
    fine = Mesh(mesh.devices.reshape(SIZES), AXES)
    whole = FAR + NEAR
    part, column = ("zh", "x", "yp", "yi"), ("zl", "c")
    in_specs = (
        P(whole, None),
        P(whole, None),
        P(part, None, column),
        P(part, None, column),
        P(part, None, column),
    )
    out_specs = (P(whole, None), P(part, None, column))
    return jax.shard_map(body, mesh=fine, in_specs=in_specs, out_specs=out_specs, check_vma=False)
```

time: 396 us -> 184 us (0.46)
  the two profiles are of different devices: /device:TPU:124 before, /device:TPU:1 now
where the time goes in v1:
time: 184 us; the launch traced here: 183 us
  waiting for transfers between devices  98.2 us (53%)
  blocking collectives  33.2 us (18%)
  between operations  14.1 us (8%)
  matrix products  13.3 us (7%)
  local copies, waits for them, and re-layouts  11.9 us (6%)
  starting transfers between devices  11.5 us (6%)
    reduce_scatter x1, waiting for transfers between devices, body(): summed = lax.psum_scatter(terms, NEAR, scatter_dimension=0, tiled=False)  56.9 us
    all_gather x1, waiting for transfers between devices, body(): rows = lax.all_gather(arrived, NEAR, axis=0, tiled=False)  41.3 us
    all_to_all x1, blocking collectives, body(): lax.all_to_all(outgoing, FAR, split_axis=0, concat_axis=0, tiled=True)  33.2 us
    all_to_all x1, starting transfers between devices, body(): lax.all_to_all(summed, FAR, split_axis=0, concat_axis=0, tiled=True)  11.5 us
    dot_general x1, matrix products, body(): jnp.einsum('gsch,dh->gscd', up_grads, weight, preferred_element_type=jnp....  7.47 us
    all_gather x1, local copies, waits for them, and re-layouts, body(): rows = lax.all_gather(arrived, NEAR, axis=0, tiled=False)  5.4 us
    dot_general x1, matrix products, body(): jnp.einsum('gscd,gsch->dh', rows, up_grads, preferred_element_type=jnp.fl...  4.56 us
  transfers between devices with their start and end apart: 3, of which 2 were waited for; matrix products, arithmetic and copies ran while one was open for 7% of the time, Pallas kernels for 0%

profile of v1, /device:TPU:1, one launch (start us, length us, event | category | flops | bytes accessed | tf_op | source)
XLA Modules:
  0.0 183.2 jit_solution(9827374931005797331)
XLA Ops:
  7.2 0.0 copy-start
  7.2 0.0 reduce-scatter.2.cloned.1.call-start
  7.2 1.1 copy.37
  8.4 0.5 reshape.26
  8.8 1.1 copy.36
  10.0 0.5 reshape.25
  10.5 0.8 fusion.9
  11.3 7.5 %convolution_convert_fusion = bf16[16,16,2,6144]{3,1,2,0:T(8,128)(2,1)} fusion(bf16[1,6144,336]{1,2,0:T(8,128)(2,1)} %param.7, bf16[16,16,2,336]{3,2,0,1:T(2,128)(2,1)S(1)} %fusion.9), kind=kOutput, calls=%fused_computation | convolution fusion | flops 2117074944 | bytes 10764288 | tf_op jit(solution)/shard_map/gsch,dh->gscd/dot_general | solution.py:38
  18.8 0.0 copy-start.1
  18.8 0.0 reduce-scatter.2.cloned.1.call-update
  18.8 0.0 all-gather.3.cloned.1.call-start
  18.9 0.6 copy-done.1
  19.5 0.1 copy.35
  19.6 0.1 convert_reduce_fusion
  19.7 0.0 copy-done
  19.7 0.4 convolution_convert_fusion.1
  20.1 0.4 copy.41
  20.5 33.2 %all_to_all.10 = bf16[16,2,6144]{2,1,0:T(2,128)(2,1)} all-to-all(bf16[16,2,6144]{2,1,0:T(2,128)(2,1)S(1)} %copy.41), channel_id=1, replica_groups=mesh['zh'=2,'x'=4,'yp'=2,'yi'=2,'zl'=4,'c'=2] {'zh','x','yp'}, dimensions={0} | all-to-all | bytes 786432 | tf_op jit(solution)/shard_map/all_to_all | solution.py:37
  53.7 0.0 all-gather.3.cloned.1.call-update
  53.7 56.9 %reduce-scatter.2.cloned.1.call-done = bf16[1,16,2,6144]{3,1,2,0:T(8,128)(2,1)} async-done(((bf16[16,16,2,6144]{3,1,2,0:T(8,128)(2,1)}), bf16[1,16,2,6144]{3,1,2,0:T(8,128)(2,1)}) %reduce-scatter.2.cloned.1.call-update) | async-done | bytes 393232 | tf_op jit(solution)/shard_map/reduce_scatter | solution.py:41
  110.6 2.2 %copy.39 = bf16[16,2,6144]{2,1,0:T(2,128)(2,1)} copy(bf16[16,2,6144]{2,0,1:T(8,128)(2,1)} %bitcast.30) | data formatting | bytes 786432 | tf_op jit(solution)/shard_map/reduce_scatter | solution.py:41
  112.8 11.5 %all-to-all-start = ((bf16[16,2,6144]{2,1,0:T(2,128)(2,1)}), bf16[16,2,6144]{2,1,0:T(2,128)(2,1)S(1)}, u32[]{:S(2)}, u32[]{:S(2)}) async-start(bf16[16,2,6144]{2,1,0:T(2,128)(2,1)} %copy.39), calls=%async_computation.1 | async-start | bytes 786432 | tf_op jit(solution)/shard_map/all_to_all | solution.py:43
  124.2 41.3 %all-gather.3.cloned.1.call-done = bf16[256,2,6144]{2,1,0:T(2,128)(2,1)} async-done(((bf16[16,2,6144]{2,1,0:T(2,128)(2,1)}), bf16[256,2,6144]{2,1,0:T(2,128)(2,1)}) %all-gather.3.cloned.1.call-update) | async-done | bytes 6291472 | tf_op jit(solution)/shard_map/all_gather | solution.py:42
  165.5 5.4 %copy.42 = bf16[256,2,6144]{2,0,1:T(8,128)(2,1)S(1)} copy(bf16[256,2,6144]{2,1,0:T(2,128)(2,1)} %all-gather.3.cloned.1.call-done) | data formatting | bytes 12582912 | tf_op jit(solution)/shard_map/all_gather | solution.py:42
  170.9 4.6 %fusion.1 = bf16[1,6144,336]{1,2,0:T(8,128)(2,1)} fusion(bf16[16,16,2,6144]{3,1,0,2:T(8,128)(2,1)S(1)} %bitcast.29, bf16[16,16,2,336]{3,2,0,1:T(2,128)(2,1)S(1)} %fusion.9), kind=kOutput, calls=%fused_computation.3 | convolution fusion | flops 2115993600 | bytes 10764288 | tf_op jit(solution)/shard_map/gscd,gsch->dh/dot_general | solution.py:44
  175.5 0.0 all-to-all-done
  175.5 0.9 fusion.2
  (3 shorter events, 0.0 us)
Async XLA Ops:
  7.2 12.5 %copy-start = (bf16[6,6144]{1,0:T(8,128)(2,1)S(1)}, bf16[6,6144]{1,0:T(8,128)(2,1)}, u32[]{:S(2)}) copy-start(bf16[6,6144]{1,0:T(8,128)(2,1)} %param.5) | copy-start | bytes 221188
  7.2 103.4 %reduce-scatter.2.cloned.1.call-start = ((), (), s32[]{:S(2)}) async-start(), calls=%async_computation.3 | async-start | bytes 6684672 | tf_op jit(solution)/shard_map/reduce_scatter | solution.py:41
  18.8 0.7 copy-start.1
  18.8 146.7 %all-gather.3.cloned.1.call-start = ((), (), s32[]{:S(2)}) async-start(), calls=%async_computation.4 | async-start | bytes 6684672 | tf_op jit(solution)/shard_map/all_gather | solution.py:42
  112.8 62.7 %all-to-all-start = ((bf16[16,2,6144]{2,1,0:T(2,128)(2,1)}), bf16[16,2,6144]{2,1,0:T(2,128)(2,1)S(1)}, u32[]{:S(2)}, u32[]{:S(2)}) async-start(bf16[16,2,6144]{2,1,0:T(2,128)(2,1)} %copy.39), calls=%async_computation.1 | async-start | bytes 786432 | tf_op jit(solution)/shard_map/all_to_all | solution.py:43
Sparse Core Ops, SparseCore 0:
  18.9 91.6 reduce-scatter.1
  112.5 53.0 all-gather.2

commit v2 on v1

v2 whole, which is shorter than its diff:
```python
import jax
import jax.numpy as jnp
from jax import lax
from jax.sharding import Mesh, PartitionSpec as P

EXPERTS = 16
CAP = 2
AXES = ("zh", "x", "yp", "yi", "zl", "c")
SIZES = (2, 4, 2, 2, 4, 2)
PLANE = ("x", "yp", "yi")
RING = ("zh", "zl")
TOK = 6
PAD = 8


def place_table(routes):
    named_by = jnp.sum(
        (routes[..., None] == jnp.arange(EXPERTS, dtype=jnp.int32)).astype(jnp.int32), axis=-2
    )
    tri = jnp.tril(jnp.ones((PAD, PAD), jnp.int32), -1)
    before = jnp.einsum("ij,...je->...ie", tri, named_by)
    return (before[..., None] == jnp.arange(CAP, dtype=jnp.int32)) & (named_by[..., None] > 0)


def swap(value):
    return lax.ppermute(value, "c", [(0, 1), (1, 0)])


def body(tokens, routes, up_weight, gate_pre, grad_hidden):
    zh, zl, core = lax.axis_index("zh"), lax.axis_index("zl"), lax.axis_index("c")
    z = zh * 4 + zl
    weight = up_weight[0]
    width, hidden = weight.shape
    half = width // 2

    up_grads = (
        grad_hidden[0].astype(jnp.float32) * jax.nn.silu(gate_pre[0].astype(jnp.float32))
    ).astype(jnp.bfloat16)
    give = lax.dynamic_slice(weight, ((1 - core) * half, 0), (half, hidden))
    keep = lax.dynamic_slice(weight, (core * half, 0), (half, hidden))
    other_weight = swap(give)
    other_grads = swap(up_grads)
    by_dest = up_grads.reshape(2, 16, 16, hidden).transpose(1, 0, 2, 3).reshape(16, 32, hidden)
    other_by_dest = other_grads.reshape(2, 16, 16, hidden).transpose(1, 0, 2, 3).reshape(16, 32, hidden)
    terms = (
        jnp.einsum("grh,dh->grd", by_dest, keep, preferred_element_type=jnp.float32)
        + jnp.einsum("grh,dh->grd", other_by_dest, other_weight, preferred_element_type=jnp.float32)
    ).astype(jnp.bfloat16)
    came_back = lax.all_to_all(terms, PLANE, split_axis=0, concat_axis=0, tiled=True)

    packed = jnp.concatenate(
        [tokens, jnp.pad(routes.astype(jnp.bfloat16), ((0, 0), (0, 124)))], axis=1
    )
    packed = jnp.pad(packed, ((0, PAD - TOK), (0, 0)))
    ring = [packed]
    for shift in range(1, 8):
        ring.append(lax.ppermute(packed, RING, [(i, (i + shift) % 8) for i in range(8)]))
    ring = jnp.stack(ring)
    ring_tokens = ring[:, :, :width]
    real = (jnp.arange(PAD) < TOK)[None, :, None]
    ring_routes = jnp.where(real, ring[:, :, width : width + 4].astype(jnp.int32), -1)
    place = place_table(ring_routes)
    source = (z - jnp.arange(8, dtype=jnp.int32)) % 8
    at = source[:, None] == jnp.arange(8, dtype=jnp.int32)[None, :]
    mine = lax.dynamic_slice(place, (0, 0, zh * 8, 0), (8, PAD, 8, CAP))
    mine = jnp.repeat(mine, 2, axis=2)
    select = (mine[:, :, :, None, :] & at[:, None, None, :, None]).astype(jnp.bfloat16)
    outgoing = jnp.einsum(
        "ktpzs,ktd->pzsd", select, ring_tokens, preferred_element_type=jnp.float32
    ).astype(jnp.bfloat16).reshape(16, 16, width)
    arrived = lax.all_to_all(outgoing, PLANE, split_axis=0, concat_axis=0, tiled=True)
    other_arrived = swap(arrived)
    by_core = up_grads.reshape(2, 16, 4, 2, CAP, hidden).transpose(3, 1, 0, 2, 4, 5)
    by_core = by_core.reshape(2, 256, hidden)
    mine_rows = lax.dynamic_index_in_dim(by_core, core, 0, keepdims=False)
    other_rows = lax.dynamic_index_in_dim(by_core, 1 - core, 0, keepdims=False)
    grad_part = jnp.einsum(
        "rd,rh->dh", arrived.reshape(256, width), mine_rows, preferred_element_type=jnp.float32
    ) + jnp.einsum(
        "rd,rh->dh", other_arrived.reshape(256, width), other_rows, preferred_element_type=jnp.float32
    )

    both_routes = jnp.stack([ring_routes, swap(ring_routes.astype(jnp.bfloat16)).astype(jnp.int32)])
    both_place = place_table(both_routes)
    both = lax.dynamic_slice(both_place, (0, 0, 0, zh * 8, 0), (2, 8, PAD, 8, CAP))
    both = jnp.repeat(both, 2, axis=3).astype(jnp.bfloat16)
    same = (jnp.arange(2)[:, None] ^ core == jnp.arange(2)[None, :]).astype(jnp.bfloat16)
    gather = jnp.einsum(
        "qktps,kz,qc->zctps", both, at.astype(jnp.bfloat16), same
    )
    eye = jnp.eye(16, dtype=jnp.bfloat16).reshape(8, 2, 8, 2)
    gather = jnp.einsum("zctps,zcyb->zctpybs", gather, eye)
    ring_sums = jnp.einsum(
        "zctpybs,pybsd->zctd",
        gather,
        came_back.reshape(16, 8, 2, CAP, half),
        preferred_element_type=jnp.float32,
    ).astype(jnp.bfloat16)
    ring_parts = lax.all_to_all(
        ring_sums.reshape(8, 2 * PAD, half), RING, split_axis=0, concat_axis=0, tiled=True
    )
    total = jnp.sum(ring_parts.astype(jnp.float32), axis=0).astype(jnp.bfloat16).reshape(2, PAD, half)
    own = lax.dynamic_index_in_dim(total, core, 0, keepdims=False)
    other = swap(lax.dynamic_index_in_dim(total, 1 - core, 0, keepdims=False))
    low, high = jnp.where(core == 0, own, other), jnp.where(core == 0, other, own)
    grad_rows = jnp.concatenate([low, high], axis=1)[:TOK]
    return (grad_rows, grad_part.astype(jnp.bfloat16)[None])


def solution(mesh):
    fine = Mesh(mesh.devices.reshape(SIZES), AXES)
    part, column = AXES[:4], AXES[4:]
    in_specs = (
        P(AXES, None),
        P(AXES, None),
        P(part, None, column),
        P(part, None, column),
        P(part, None, column),
    )
    out_specs = (P(AXES, None), P(part, None, column))
    return jax.shard_map(body, mesh=fine, in_specs=in_specs, out_specs=out_specs, check_vma=False)
```

time: 184 us -> 187 us (1.016)
  waiting for transfers between devices: 98.2 us -> 50.1 us
  starting transfers between devices: 11.5 us -> 50 us
  blocking collectives: 33.2 us -> 0 us
  local copies, waits for them, and re-layouts: 11.9 us -> 34.9 us
  matrix products: 13.3 us -> 32.3 us
  other arithmetic: 0.95 us -> 17.4 us
  between operations: 14.1 us -> 0.95 us
    reduce_scatter x1 -> x0, waiting for transfers between devices: 56.9 us -> none  [body(): summed = lax.psum_scatter(terms, NEAR, scatter_dimension=0, tiled=False)]
    all_gather x1 -> x0, waiting for transfers between devices: 41.3 us -> none  [body(): rows = lax.all_gather(arrived, NEAR, axis=0, tiled=False)]
    all_to_all x1 -> x3, waiting for transfers between devices: 0.01 us -> 37.7 us  [the longest x1 17.3 us: body(): lax.all_to_all(outgoing, PLANE, split_axis=0, concat_axis=0, tiled=True)]
    all_to_all x1 -> x0, blocking collectives: 33.2 us -> none  [body(): lax.all_to_all(outgoing, FAR, split_axis=0, concat_axis=0, tiled=True)]
    ppermute x0 -> x12, starting transfers between devices: none -> 28 us  [the longest x7 17.5 us: body(): lax.ppermute(packed, RING, [(i, (i + shift) % 8) for i in range(8)])]
    dot_general x4 -> x10, matrix products: 13.3 us -> 32.3 us  [the longest x1 7.54 us: body(): jnp.einsum('rd,rh->dh', other_arrived.reshape(256, width), other_rows, pr...]
    ppermute x0 -> x12, waiting for transfers between devices: none -> 12.3 us  [the longest x7 12 us: body(): lax.ppermute(packed, RING, [(i, (i + shift) % 8) for i in range(8)])]
    all_to_all x1 -> x3, starting transfers between devices: 11.5 us -> 22 us  [the longest x1 9.05 us: body(): lax.all_to_all(terms, PLANE, split_axis=0, concat_axis=0, tiled=True)]
  transfers between devices with their start and end apart: 3 -> 15, of which waited for: 2 -> 9; matrix products, arithmetic and copies ran while one was open for 7% -> 38% of each run, Pallas kernels for 0% -> 0%
where the time goes in v2:
time: 187 us; the launch traced here: 186 us
  waiting for transfers between devices  50.1 us (27%)
  starting transfers between devices  50 us (27%)
  local copies, waits for them, and re-layouts  34.9 us (19%)
  matrix products  32.3 us (17%)
  other arithmetic  17.4 us (9%)
    ppermute x7, starting transfers between devices, body(): lax.ppermute(packed, RING, [(i, (i + shift) % 8) for i in range(8)])  17.5 us
    all_to_all x1, waiting for transfers between devices, body(): lax.all_to_all(outgoing, PLANE, split_axis=0, concat_axis=0, tiled=True)  17.3 us
    all_to_all x1, waiting for transfers between devices, body(): lax.all_to_all(terms, PLANE, split_axis=0, concat_axis=0, tiled=True)  17.1 us
    ppermute x7, waiting for transfers between devices, body(): lax.ppermute(packed, RING, [(i, (i + shift) % 8) for i in range(8)])  12 us
    ppermute x5, starting transfers between devices, swap(): return lax.ppermute(value, 'c', [(0, 1), (1, 0)])  10.5 us
    all_to_all x1, starting transfers between devices, body(): lax.all_to_all(terms, PLANE, split_axis=0, concat_axis=0, tiled=True)  9.05 us
    dot_general x1, matrix products, body(): jnp.einsum('rd,rh->dh', other_arrived.reshape(256, width), other_rows, pr...  7.54 us
    all_to_all x1, starting transfers between devices, body(): lax.all_to_all(outgoing, PLANE, split_axis=0, concat_axis=0, tiled=True)  6.76 us
  transfers between devices with their start and end apart: 15, of which 9 were waited for; matrix products, arithmetic and copies ran while one was open for 38% of the time, Pallas kernels for 0%

profile of v2, /device:TPU:1, one launch (start us, length us, event | category | flops | bytes accessed | tf_op | source)
XLA Modules:
  0.0 185.6 jit_solution(2686002574855989841)
XLA Ops:
  2.4 2.5 %collective-permute-start = (bf16[8,6272]{1,0:T(8,128)(2,1)S(1)}, bf16[8,6272]{1,0:T(8,128)(2,1)S(1)}, u32[]{:S(2)}, u32[]{:S(2)}) collective-permute-start(bf16[8,6272]{1,0:T(8,128)(2,1)S(1)} %pad.9), channel_id=1, source_target_pairs={{0,2},{2,4},{4,6},{6,128},{128,130},{130,132},{132,134},{134,0},{1... | collective-permute-start | bytes 301064 | tf_op jit(solution)/shard_map/ppermute | solution.py:57
  4.9 3.0 %collective-permute-start.1 = (bf16[8,6272]{1,0:T(8,128)(2,1)S(1)}, bf16[8,6272]{1,0:T(8,128)(2,1)S(1)}, u32[]{:S(2)}, u32[]{:S(2)}) collective-permute-start(bf16[8,6272]{1,0:T(8,128)(2,1)S(1)} %pad.9), channel_id=1, source_target_pairs={{0,4},{2,6},{4,128},{6,130},{128,132},{130,134},{132,0},{134,2},{1... | collective-permute-start | bytes 301064 | tf_op jit(solution)/shard_map/ppermute | solution.py:57
  7.9 3.8 %collective-permute-start.2 = (bf16[8,6272]{1,0:T(8,128)(2,1)S(1)}, bf16[8,6272]{1,0:T(8,128)(2,1)S(1)}, u32[]{:S(2)}, u32[]{:S(2)}) collective-permute-start(bf16[8,6272]{1,0:T(8,128)(2,1)S(1)} %pad.9), channel_id=1, source_target_pairs={{0,6},{2,128},{4,130},{6,132},{128,134},{130,0},{132,2},{134,4},{1... | collective-permute-start | bytes 301064 | tf_op jit(solution)/shard_map/ppermute | solution.py:57
  12.1 4.5 %collective-permute-start.4 = (bf16[8,6272]{1,0:T(8,128)(2,1)S(1)}, bf16[8,6272]{1,0:T(8,128)(2,1)S(1)}, u32[]{:S(2)}, u32[]{:S(2)}) collective-permute-start(bf16[8,6272]{1,0:T(8,128)(2,1)S(1)} %pad.9), channel_id=1, source_target_pairs={{0,130},{2,132},{4,134},{6,0},{128,2},{130,4},{132,6},{134,128},{1... | collective-permute-start | bytes 301064 | tf_op jit(solution)/shard_map/ppermute | solution.py:57
  17.3 2.5 %collective-permute-start.5 = (bf16[8,6272]{1,0:T(8,128)(2,1)S(1)}, bf16[8,6272]{1,0:T(8,128)(2,1)S(1)}, u32[]{:S(2)}, u32[]{:S(2)}) collective-permute-start(bf16[8,6272]{1,0:T(8,128)(2,1)S(1)} %pad.9), channel_id=1, source_target_pairs={{0,132},{2,134},{4,0},{6,2},{128,4},{130,6},{132,128},{134,130},{1... | collective-permute-start | bytes 301064 | tf_op jit(solution)/shard_map/ppermute | solution.py:57
  20.6 1.4 collective-permute-done.2
  22.1 2.0 %collective-permute-done.3 = bf16[8,6272]{1,0:T(8,128)(2,1)S(1)} collective-permute-done((bf16[8,6272]{1,0:T(8,128)(2,1)S(1)}, bf16[8,6272]{1,0:T(8,128)(2,1)S(1)}, u32[]{:S(2)}, u32[]{:S(2)}) %collective-permute-start.3) | collective-permute-done | bytes 100384 | tf_op jit(solution)/shard_map/ppermute | solution.py:57
  24.9 6.9 %collective-permute-done.5 = bf16[8,6272]{1,0:T(8,128)(2,1)S(1)} collective-permute-done((bf16[8,6272]{1,0:T(8,128)(2,1)S(1)}, bf16[8,6272]{1,0:T(8,128)(2,1)S(1)}, u32[]{:S(2)}, u32[]{:S(2)}) %collective-permute-start.5) | collective-permute-done | bytes 100384 | tf_op jit(solution)/shard_map/ppermute | solution.py:57
  34.2 2.0 %fusion.1 = bf16[16,8,2,6144]{3,1,2,0:T(8,128)(2,1)S(1)} fusion(bf16[8,8,6272]{2,1,0:T(8,128)(2,1)S(1)} %bitcast_dynamic-update-slice_fusion, pred[8,8]{1,0:T(8,128)(4,1)S(1)} %copy.125, pred[8,8,16,2]{1,0,3,2:T(8,128)(4,1)S(1)} %bitcast.142), kind=kOutput, calls=%fused_computation.3 | convolution fusion | flops 202915840 | bytes 3965952 | tf_op jit(solution)/shard_map/ktpzs,ktd->pzsd/dot_general | solution.py:68
  36.1 1.7 copy.126
  37.9 3.4 %copy.127 = bf16[16,16,6144]{2,1,0:T(8,128)(2,1)} copy(bf16[16,16,6144]{2,0,1:T(8,128)(2,1)S(1)} %bitcast.131) | data formatting | bytes 6291456 | tf_op jit(solution)/shard_map/reshape | solution.py:70
  41.3 6.8 %all-to-all-start.2 = ((bf16[16,16,6144]{2,1,0:T(8,128)(2,1)}), bf16[16,16,6144]{2,1,0:T(8,128)(2,1)S(1)}, u32[]{:S(2)}, u32[]{:S(2)}) async-start(bf16[16,16,6144]{2,1,0:T(8,128)(2,1)} %copy.127), calls=%async_computation.2 | async-start | bytes 6291456 | tf_op jit(solution)/shard_map/all_to_all | solution.py:71
  48.0 3.1 %dynamic-slice_bitcast_fusion = bf16[3072,336]{0,1:T(8,128)(2,1)} fusion(bf16[1,6144,336]{1,2,0:T(8,128)(2,1)} %param.7, s32[]{:T(128)S(6)} %select_n.60), kind=kLoop, calls=%fused_computation.11 | loop fusion | bytes 4128772 | tf_op jit(solution)/shard_map/dynamic_slice | solution.py:39
  51.1 0.9 collective-permute-start.9
  52.0 0.9 copy.116
  52.9 1.2 copy.117
  54.1 2.0 %fusion.16 = bf16[512,336]{1,0:T(8,128)(2,1)} fusion(bf16[1,512,336]{2,1,0:T(8,128)(2,1)S(1)} %copy.117, bf16[1,512,336]{2,1,0:T(8,128)(2,1)} %copy.116), kind=kLoop, calls=%fused_computation.31 | loop fusion | flops 1376256 | bytes 1032192 | tf_op jit(solution)/shard_map/convert_element_type | solution.py:38
  56.1 2.0 %convert_element_type.108 = f32[1,512,336]{2,1,0:T(8,128)} convert(bf16[1,512,336]{2,1,0:T(8,128)(2,1)} %copy.116) | non-fusion elementwise | flops 172032 | bytes 1032192 | tf_op jit(solution)/shard_map/convert_element_type | solution.py:37
  58.1 0.9 convert_element_type.109
  59.0 1.6 fusion.20
  61.5 3.5 %fusion.6 = f32[16,32,3072]{2,1,0:T(8,128)S(1)} fusion(bf16[16,32,336]{2,1,0:T(8,128)(2,1)} %bitcast.137, bf16[1,6144,336]{1,2,0:T(8,128)(2,1)} %param.7, s32[]{:T(128)S(6)} %select_n.59), kind=kOutput, calls=%fused_computation.9 | convolution fusion | flops 1056964608 | bytes 8749060 | tf_op jit(solution)/shard_map/grh,dh->grd/dot_general | solution.py:46
  65.0 1.0 copy.119
  66.0 5.0 %add_convert_fusion = bf16[16,32,3072]{2,1,0:T(8,128)(2,1)} fusion(f32[16,32,3072]{2,1,0:T(8,128)S(1)} %fusion.6, bf16[16,32,336]{2,1,0:T(8,128)(2,1)S(1)} %bitcast.138, bf16[3072,336]{0,1:T(8,128)(2,1)} %collective-permute-done.9), kind=kOutput, calls=%fused_computation.5 | convolution fusion | flops 1060110336 | bytes 11845632 | tf_op jit(solution)/shard_map/grh,dh->grd/dot_general | solution.py:47
  71.1 17.3 %all-to-all-done.2 = bf16[16,16,6144]{2,1,0:T(8,128)(2,1)S(1)} async-done(((bf16[16,16,6144]{2,1,0:T(8,128)(2,1)}), bf16[16,16,6144]{2,1,0:T(8,128)(2,1)S(1)}, u32[]{:S(2)}, u32[]{:S(2)}) %all-to-all-start.2) | async-done | bytes 3145760 | tf_op jit(solution)/shard_map/all_to_all | solution.py:71
  88.3 1.7 copy-done
  90.1 9.0 %all-to-all-start = ((bf16[16,32,3072]{2,1,0:T(8,128)(2,1)}), bf16[16,32,3072]{2,1,0:T(8,128)(2,1)S(1)}, u32[]{:S(2)}, u32[]{:S(2)}) async-start(bf16[16,32,3072]{2,1,0:T(8,128)(2,1)} %add_convert_fusion), calls=%async_computation | async-start | bytes 6291456 | tf_op jit(solution)/shard_map/all_to_all | solution.py:49
  99.8 2.2 %collective-permute-start.7 = (bf16[8,8,4]{2,1,0:T(8,128)(2,1)S(1)}, bf16[8,8,4]{2,1,0:T(8,128)(2,1)S(1)}, u32[]{:S(2)}, u32[]{:S(2)}) collective-permute-start(bf16[8,8,4]{2,1,0:T(8,128)(2,1)S(1)} %get-tuple-element.4), channel_id=1, source_target_pairs={{0,1},{1,0},{2,3},{3,2},{4,5},{5,4},{6,7},{7,6},{8,9},{9,8},{10,11... | collective-permute-start | bytes 1544 | tf_op jit(solution)/shard_map/ppermute | solution.py:26
  102.8 1.4 pad_add_fusion
  104.2 1.6 copy.110
  107.3 1.6 convolution_bitcast_fusion.2
  108.9 1.6 copy.111
  114.4 1.6 copy.113
  118.7 17.1 %all-to-all-done = bf16[16,32,3072]{2,1,0:T(8,128)(2,1)S(1)} async-done(((bf16[16,32,3072]{2,1,0:T(8,128)(2,1)}), bf16[16,32,3072]{2,1,0:T(8,128)(2,1)S(1)}, u32[]{:S(2)}, u32[]{:S(2)}) %all-to-all-start) | async-done | bytes 3145760 | tf_op jit(solution)/shard_map/all_to_all | solution.py:49
  135.7 2.7 %reshape.137 = bf16[16,8,2,2,3072]{4,3,2,1,0:T(2,128)(2,1)} reshape(bf16[16,32,3072]{2,1,0:T(8,128)(2,1)S(1)} %all-to-all-done) | data formatting | bytes 6291456 | tf_op jit(solution)/shard_map/reshape | solution.py:96
  138.4 6.3 %fusion.3 = bf16[8,2,8,3072,1,1,1]{3,2,6,5,1,0,4:T(8,128)(2,1)S(1)} fusion(bf16[16,8,2,2,3072,1,1]{4,3,2,1,0,6,5:T(2,128)(2,1)} %bitcast.134, bf16[8,2,8,16,2]{3,2,4,0,1:T(8,128)(2,1)} %copy.115, bf16[8,2,8,2]{2,0,1,3:T(8,128)(2,1)S(1)} %copy-done.5), kind=kOutput, calls=%fused_computation.6 | convolution fusion | flops 402718720 | bytes 3940864 | tf_op jit(solution)/shard_map/zctpybs,pybsd->zctd/dot_general | solution.py:93
  144.7 0.9 copy_bitcast_fusion
  145.6 6.2 %all-to-all-start.1 = ((bf16[8,16,3072]{2,1,0:T(8,128)(2,1)}), bf16[8,16,3072]{2,1,0:T(8,128)(2,1)}, u32[]{:S(2)}, u32[]{:S(2)}) async-start(bf16[8,16,3072]{2,1,0:T(8,128)(2,1)} %copy_bitcast_fusion), calls=%async_computation.1 | async-start | bytes 1572864 | tf_op jit(solution)/shard_map/all_to_all | solution.py:99
  151.9 1.3 reshape.149
  153.2 1.3 reshape.150
  154.5 2.2 %fusion.21 = bf16[2,16,2,4,2,336]{5,4,0,3,1,2:T(2,128)(2,1)S(1)} fusion(f32[2,16,4,2,2,336]{5,4,3,2,1,0:T(2,128)} %reshape.149, f32[2,16,4,2,2,336]{5,4,3,2,1,0:T(2,128)} %reshape.150), kind=kLoop, calls=%fused_computation.36 | loop fusion | flops 1032192 | bytes 1720320 | tf_op jit(solution)/shard_map/transpose | solution.py:73
  157.0 1.7 constant_dynamic-slice_fusion.2
  158.7 1.2 copy.129
  159.9 1.2 copy.130
  161.2 4.4 %fusion.24 = f32[6144,336]{0,1:T(8,128)} fusion(bf16[256,6144]{1,0:T(8,128)(2,1)S(1)} %bitcast.132, bf16[1,256,336]{1,2,0:T(8,128)(2,1)S(1)} %copy.129), kind=kOutput, calls=%fused_computation.42 | convolution fusion | flops 1056964608 | bytes 11575296 | tf_op jit(solution)/shard_map/rd,rh->dh/dot_general | solution.py:77
  165.6 3.4 %all-to-all-done.1 = bf16[8,16,3072]{2,1,0:T(8,128)(2,1)} async-done(((bf16[8,16,3072]{2,1,0:T(8,128)(2,1)}), bf16[8,16,3072]{2,1,0:T(8,128)(2,1)}, u32[]{:S(2)}, u32[]{:S(2)}) %all-to-all-start.1) | async-done | bytes 786464 | tf_op jit(solution)/shard_map/all_to_all | solution.py:99
  169.0 1.2 reduce_sum.31
  170.3 7.1 %collective-permute-start.10 = (bf16[8,3072]{1,0:T(8,128)(2,1)S(1)}, bf16[8,3072]{1,0:T(8,128)(2,1)S(1)}, u32[]{:S(2)}, u32[]{:S(2)}) collective-permute-start(bf16[8,3072]{1,0:T(8,128)(2,1)S(1)} %dynamic-slice_bitcast_fusion.1), channel_id=1, source_target_pairs={{0,1},{1,0},{2,3},{3,2},{4,5},{5,4},{6,7},{7,6},{8,9},{9,8},{10,11... | collective-permute-start | bytes 147464 | tf_op jit(solution)/shard_map/ppermute | solution.py:26
  177.4 7.5 %fusion.2 = bf16[1,6144,336]{1,2,0:T(8,128)(2,1)} fusion(f32[6144,336]{0,1:T(8,128)} %fusion.24, bf16[256,6144]{1,0:T(8,128)(2,1)} %bitcast.51, bf16[1,256,336]{1,2,0:T(8,128)(2,1)S(1)} %copy.130), kind=kOutput, calls=%fused_computation.4 | convolution fusion | flops 1061093376 | bytes 15704064 | tf_op jit(solution)/shard_map/rd,rh->dh/dot_general | solution.py:79
  (75 shorter events, 18.2 us)
Async XLA Ops:
  2.4 15.0 %collective-permute-start = (bf16[8,6272]{1,0:T(8,128)(2,1)S(1)}, bf16[8,6272]{1,0:T(8,128)(2,1)S(1)}, u32[]{:S(2)}, u32[]{:S(2)}) collective-permute-start(bf16[8,6272]{1,0:T(8,128)(2,1)S(1)} %pad.9), channel_id=1, source_target_pairs={{0,2},{2,4},{4,6},{6,128},{128,130},{130,132},{132,134},{134,0},{1... | collective-permute-start | bytes 301064 | tf_op jit(solution)/shard_map/ppermute | solution.py:57
  4.9 14.9 %collective-permute-start.1 = (bf16[8,6272]{1,0:T(8,128)(2,1)S(1)}, bf16[8,6272]{1,0:T(8,128)(2,1)S(1)}, u32[]{:S(2)}, u32[]{:S(2)}) collective-permute-start(bf16[8,6272]{1,0:T(8,128)(2,1)S(1)} %pad.9), channel_id=1, source_target_pairs={{0,4},{2,6},{4,128},{6,130},{128,132},{130,134},{132,0},{134,2},{1... | collective-permute-start | bytes 301064 | tf_op jit(solution)/shard_map/ppermute | solution.py:57
  7.9 14.2 %collective-permute-start.2 = (bf16[8,6272]{1,0:T(8,128)(2,1)S(1)}, bf16[8,6272]{1,0:T(8,128)(2,1)S(1)}, u32[]{:S(2)}, u32[]{:S(2)}) collective-permute-start(bf16[8,6272]{1,0:T(8,128)(2,1)S(1)} %pad.9), channel_id=1, source_target_pairs={{0,6},{2,128},{4,130},{6,132},{128,134},{130,0},{132,2},{134,4},{1... | collective-permute-start | bytes 301064 | tf_op jit(solution)/shard_map/ppermute | solution.py:57
  11.7 12.5 %collective-permute-start.3 = (bf16[8,6272]{1,0:T(8,128)(2,1)S(1)}, bf16[8,6272]{1,0:T(8,128)(2,1)S(1)}, u32[]{:S(2)}, u32[]{:S(2)}) collective-permute-start(bf16[8,6272]{1,0:T(8,128)(2,1)S(1)} %pad.9), channel_id=1, source_target_pairs={{0,128},{2,130},{4,132},{6,134},{128,0},{130,2},{132,4},{134,6},{1... | collective-permute-start | bytes 301064 | tf_op jit(solution)/shard_map/ppermute | solution.py:57
  12.1 12.8 %collective-permute-start.4 = (bf16[8,6272]{1,0:T(8,128)(2,1)S(1)}, bf16[8,6272]{1,0:T(8,128)(2,1)S(1)}, u32[]{:S(2)}, u32[]{:S(2)}) collective-permute-start(bf16[8,6272]{1,0:T(8,128)(2,1)S(1)} %pad.9), channel_id=1, source_target_pairs={{0,130},{2,132},{4,134},{6,0},{128,2},{130,4},{132,6},{134,128},{1... | collective-permute-start | bytes 301064 | tf_op jit(solution)/shard_map/ppermute | solution.py:57
  16.7 0.6 copy-start.7
  17.3 18.8 %copy-start.6 = (s32[8]{0:T(128)}, s32[8]{0:T(128)S(1)}, u32[]{:S(2)}) copy-start(s32[8]{0:T(128)S(1)} %iota_add_fusion) | copy-start | bytes 100
  17.3 14.5 %collective-permute-start.5 = (bf16[8,6272]{1,0:T(8,128)(2,1)S(1)}, bf16[8,6272]{1,0:T(8,128)(2,1)S(1)}, u32[]{:S(2)}, u32[]{:S(2)}) collective-permute-start(bf16[8,6272]{1,0:T(8,128)(2,1)S(1)} %pad.9), channel_id=1, source_target_pairs={{0,132},{2,134},{4,0},{6,2},{128,4},{130,6},{132,128},{134,130},{1... | collective-permute-start | bytes 301064 | tf_op jit(solution)/shard_map/ppermute | solution.py:57
  19.8 12.8 %collective-permute-start.6 = (bf16[8,6272]{1,0:T(8,128)(2,1)S(1)}, bf16[8,6272]{1,0:T(8,128)(2,1)S(1)}, u32[]{:S(2)}, u32[]{:S(2)}) collective-permute-start(bf16[8,6272]{1,0:T(8,128)(2,1)S(1)} %pad.9), channel_id=1, source_target_pairs={{0,134},{2,0},{4,2},{6,4},{128,6},{130,128},{132,130},{134,132},{1... | collective-permute-start | bytes 301064 | tf_op jit(solution)/shard_map/ppermute | solution.py:57
  41.3 47.1 %all-to-all-start.2 = ((bf16[16,16,6144]{2,1,0:T(8,128)(2,1)}), bf16[16,16,6144]{2,1,0:T(8,128)(2,1)S(1)}, u32[]{:S(2)}, u32[]{:S(2)}) async-start(bf16[16,16,6144]{2,1,0:T(8,128)(2,1)} %copy.127), calls=%async_computation.2 | async-start | bytes 6291456 | tf_op jit(solution)/shard_map/all_to_all | solution.py:71
  48.0 4.0 %copy-start.4 = (bf16[1,512,336]{1,2,0:T(8,128)(2,1)S(1)}, bf16[1,512,336]{1,2,0:T(8,128)(2,1)}, u32[]{:S(2)}) copy-start(bf16[1,512,336]{1,2,0:T(8,128)(2,1)} %param.9) | copy-start | bytes 1032196
  51.1 14.9 %collective-permute-start.9 = (bf16[3072,336]{0,1:T(8,128)(2,1)}, bf16[3072,336]{0,1:T(8,128)(2,1)}, u32[]{:S(2)}, u32[]{:S(2)}) collective-permute-start(bf16[3072,336]{0,1:T(8,128)(2,1)} %dynamic-slice_bitcast_fusion), channel_id=1, source_target_pairs={{0,1},{1,0},{2,3},{3,2},{4,5},{5,4},{6,7},{7,6},{8,9},{9,8},{10,11... | collective-permute-start | bytes 6193160 | tf_op jit(solution)/shard_map/ppermute | solution.py:26
  56.1 8.9 %collective-permute-start.8 = (bf16[512,336]{1,0:T(8,128)(2,1)}, bf16[512,336]{1,0:T(8,128)(2,1)}, u32[]{:S(2)}, u32[]{:S(2)}) collective-permute-start(bf16[512,336]{1,0:T(8,128)(2,1)} %fusion.16), channel_id=1, source_target_pairs={{0,1},{1,0},{2,3},{3,2},{4,5},{5,4},{6,7},{7,6},{8,9},{9,8},{10,11... | collective-permute-start | bytes 1032200 | tf_op jit(solution)/shard_map/ppermute | solution.py:26
  88.3 1.7 copy-start
  90.1 45.7 %all-to-all-start = ((bf16[16,32,3072]{2,1,0:T(8,128)(2,1)}), bf16[16,32,3072]{2,1,0:T(8,128)(2,1)S(1)}, u32[]{:S(2)}, u32[]{:S(2)}) async-start(bf16[16,32,3072]{2,1,0:T(8,128)(2,1)} %add_convert_fusion), calls=%async_computation | async-start | bytes 6291456 | tf_op jit(solution)/shard_map/all_to_all | solution.py:49
  99.8 3.0 %collective-permute-start.7 = (bf16[8,8,4]{2,1,0:T(8,128)(2,1)S(1)}, bf16[8,8,4]{2,1,0:T(8,128)(2,1)S(1)}, u32[]{:S(2)}, u32[]{:S(2)}) collective-permute-start(bf16[8,8,4]{2,1,0:T(8,128)(2,1)S(1)} %get-tuple-element.4), channel_id=1, source_target_pairs={{0,1},{1,0},{2,3},{3,2},{4,5},{5,4},{6,7},{7,6},{8,9},{9,8},{10,11... | collective-permute-start | bytes 1544 | tf_op jit(solution)/shard_map/ppermute | solution.py:26
  106.7 0.6 copy-start.3
  118.3 20.1 %copy-start.5 = (bf16[8,2,8,2]{2,0,1,3:T(8,128)(2,1)S(1)}, bf16[8,2,8,2]{2,0,1,3:T(8,128)(2,1)}, u32[]{:S(2)}) copy-start(bf16[8,2,8,2]{2,0,1,3:T(8,128)(2,1)} %compare_convert_fusion) | copy-start | bytes 1540
  118.3 59.1 %collective-permute-start.11 = (bf16[16,16,6144]{2,1,0:T(8,128)(2,1)}, bf16[16,16,6144]{2,1,0:T(8,128)(2,1)}, u32[]{:S(2)}, u32[]{:S(2)}) collective-permute-start(bf16[16,16,6144]{2,1,0:T(8,128)(2,1)} %copy-done), channel_id=1, source_target_pairs={{0,1},{1,0},{2,3},{3,2},{4,5},{5,4},{6,7},{7,6},{8,9},{9,8},{10,11... | collective-permute-start | bytes 9437192 | tf_op jit(solution)/shard_map/ppermute | solution.py:26
  144.7 7.2 %copy-start.2 = (bf16[1,512,336]{2,1,0:T(8,128)(2,1)S(1)}, bf16[1,512,336]{2,1,0:T(8,128)(2,1)}, u32[]{:S(2)}) copy-start(bf16[1,512,336]{2,1,0:T(8,128)(2,1)} %copy.116) | copy-start | bytes 1032196
  145.6 23.4 %all-to-all-start.1 = ((bf16[8,16,3072]{2,1,0:T(8,128)(2,1)}), bf16[8,16,3072]{2,1,0:T(8,128)(2,1)}, u32[]{:S(2)}, u32[]{:S(2)}) async-start(bf16[8,16,3072]{2,1,0:T(8,128)(2,1)} %copy_bitcast_fusion), calls=%async_computation.1 | async-start | bytes 1572864 | tf_op jit(solution)/shard_map/all_to_all | solution.py:99
  153.2 8.0 %copy-start.1 = (bf16[16,16,6144]{2,1,0:T(8,128)(2,1)S(1)}, bf16[16,16,6144]{2,1,0:T(8,128)(2,1)}, u32[]{:S(2)}) copy-start(bf16[16,16,6144]{2,1,0:T(8,128)(2,1)} %copy-done) | copy-start | bytes 9437188
  170.3 14.6 %collective-permute-start.10 = (bf16[8,3072]{1,0:T(8,128)(2,1)S(1)}, bf16[8,3072]{1,0:T(8,128)(2,1)S(1)}, u32[]{:S(2)}, u32[]{:S(2)}) collective-permute-start(bf16[8,3072]{1,0:T(8,128)(2,1)S(1)} %dynamic-slice_bitcast_fusion.1), channel_id=1, source_target_pairs={{0,1},{1,0},{2,3},{3,2},{4,5},{5,4},{6,7},{7,6},{8,9},{9,8},{10,11... | collective-permute-start | bytes 147464 | tf_op jit(solution)/shard_map/ppermute | solution.py:26

commit v3 on v1

v3 whole, which is shorter than its diff:
```python
import functools

import jax
import jax.numpy as jnp
from jax import lax
from jax.experimental import pallas as pl
from jax.experimental.pallas import tpu as pltpu
from jax.sharding import Mesh, PartitionSpec as P

EXPERTS = 16
CAP = 2
AXES = ("zh", "x", "yp", "yi", "zl", "c")
SIZES = (2, 4, 2, 2, 4, 2)
FAR = ("zh", "x", "yp")
PLANE = ("x", "yp", "yi")
RING = ("zh", "zl")
TOK = 6
PAD = 8
CUT = 2048
MIB = 1 << 20
BF, F32, I32 = jnp.bfloat16, jnp.float32, jnp.int32


def params(mib=40):
    return pltpu.CompilerParams(vmem_limit_bytes=mib * MIB)


def iota(shape, dim):
    return lax.broadcasted_iota(I32, shape, dim)


def gate_kernel(gate_ref, grad_ref, ut_ref, u_ref):
    gate = gate_ref[...].astype(F32)
    value = (grad_ref[...].astype(F32) * (gate / (1.0 + jnp.exp(-gate)))).astype(BF)
    ut_ref[...] = value
    u_ref[...] = value.T


def gated(gate_t, grad_t):
    hidden, rows = gate_t.shape
    return pl.pallas_call(
        gate_kernel,
        out_shape=(
            jax.ShapeDtypeStruct((hidden, rows), BF),
            jax.ShapeDtypeStruct((rows, hidden), BF),
        ),
        compiler_params=params(),
        cost_estimate=pl.CostEstimate(flops=10**6, bytes_accessed=1400000, transcendentals=172032),
    )(gate_t, grad_t)


def copy_kernel(core_ref, in_ref, out_ref):
    out_ref[...] = in_ref[...]


def other_half(core, weight_t):
    hidden, width = weight_t.shape
    block = 1024
    steps = width // 2 // block
    return pl.pallas_call(
        copy_kernel,
        grid_spec=pltpu.PrefetchScalarGridSpec(
            num_scalar_prefetch=1,
            grid=(steps,),
            in_specs=[pl.BlockSpec((hidden, block), lambda i, core: (0, (1 - core[0]) * steps + i))],
            out_specs=pl.BlockSpec((hidden, block), lambda i, core: (0, i)),
        ),
        out_shape=jax.ShapeDtypeStruct((hidden, width // 2), BF),
        compiler_params=params(),
        cost_estimate=pl.CostEstimate(flops=0, bytes_accessed=4200000, transcendentals=0),
    )(core, weight_t)


def terms_kernel(core_ref, u_ref, v_ref, w_ref, x_ref, out_ref):
    for zh in range(2):
        rows = pl.ds(zh * 256, 256)
        term = jnp.dot(u_ref[rows, :], w_ref[...], preferred_element_type=F32)
        term += jnp.dot(v_ref[rows, :], x_ref[...], preferred_element_type=F32)
        out_ref[:, zh, :, :] = term.astype(BF).reshape(16, 16, term.shape[1])


def terms_of(core, u, v, weight_t, other_t):
    rows, hidden = u.shape
    half = other_t.shape[1]
    block = 512
    steps = half // block
    return pl.pallas_call(
        terms_kernel,
        grid_spec=pltpu.PrefetchScalarGridSpec(
            num_scalar_prefetch=1,
            grid=(steps,),
            in_specs=[
                pl.BlockSpec((rows, hidden), lambda i, core: (0, 0)),
                pl.BlockSpec((rows, hidden), lambda i, core: (0, 0)),
                pl.BlockSpec((hidden, block), lambda i, core: (0, core[0] * steps + i)),
                pl.BlockSpec((hidden, block), lambda i, core: (0, i)),
            ],
            out_specs=pl.BlockSpec((16, 2, 16, block), lambda i, core: (0, 0, 0, i)),
        ),
        out_shape=jax.ShapeDtypeStruct((16, 2, 16, half), BF),
        compiler_params=params(),
        cost_estimate=pl.CostEstimate(flops=4 * rows * hidden * half, bytes_accessed=8000000, transcendentals=0),
    )(core, u, v, weight_t, other_t)


def named_mask(routes, expert):
    named = jnp.zeros(expert.shape, F32)
    for k in range(4):
        named += jnp.where(routes[:, k : k + 1] == expert, 1.0, 0.0)
    return named


def place_kernel(routes_ref, tokens_ref, out_ref):
    rows = 2 * EXPERTS
    column = iota((PAD, rows), 1)
    named = named_mask(routes_ref[...].astype(F32), (column // 2).astype(F32))
    lower = jnp.where(iota((PAD, PAD), 0) > iota((PAD, PAD), 1), 1.0, 0.0)
    before = jnp.dot(lower, named, preferred_element_type=F32)
    chosen = jnp.where(before == (column % 2).astype(F32), named, 0.0).astype(BF)
    out_ref[...] = lax.dot_general(
        chosen, tokens_ref[...], (((0,), (0,)), ((), ())), preferred_element_type=F32
    ).astype(BF)


def placed_rows(routes, tokens):
    return pl.pallas_call(
        place_kernel,
        out_shape=jax.ShapeDtypeStruct((2 * EXPERTS, tokens.shape[1]), BF),
        compiler_params=params(),
        cost_estimate=pl.CostEstimate(flops=10**6, bytes_accessed=500000, transcendentals=0),
    )(routes, tokens)


def choose_kernel(zh_ref, routes_ref, out_ref):
    shape = (8 * 2 * PAD, 512)
    row, column = iota(shape, 0), iota(shape, 1)
    expert = zh_ref[0] * 8 + column // 64
    named = named_mask(routes_ref[...].astype(F32), expert.astype(F32))
    square = (shape[0], shape[0])
    r, s = iota(square, 0), iota(square, 1)
    lower = jnp.where((r // PAD == s // PAD) & (r > s), 1.0, 0.0)
    before = jnp.dot(lower.astype(BF), named.astype(BF), preferred_element_type=F32)
    fits = (before == (column % 2).astype(F32)) & (row // PAD == (column // 2) % 16)
    out_ref[...] = jnp.where(fits, named, 0.0).astype(BF)


def chooser(zh, routes):
    return pl.pallas_call(
        choose_kernel,
        in_specs=[pl.BlockSpec(memory_space=pltpu.SMEM), pl.BlockSpec(memory_space=pltpu.VMEM)],
        out_shape=jax.ShapeDtypeStruct((8 * 2 * PAD, 512), BF),
        compiler_params=params(),
        cost_estimate=pl.CostEstimate(flops=10**6, bytes_accessed=200000, transcendentals=0),
    )(zh, routes)


def combine_kernel(choice_ref, back_ref, out_ref):
    out_ref[...] = jnp.dot(choice_ref[...], back_ref[...], preferred_element_type=F32).astype(BF)


def combined(choice, back):
    rows, width = back.shape
    block = 1024
    return pl.pallas_call(
        combine_kernel,
        grid=(width // block,),
        in_specs=[
            pl.BlockSpec(choice.shape, lambda i: (0, 0)),
            pl.BlockSpec((rows, block), lambda i: (0, i)),
        ],
        out_specs=pl.BlockSpec((choice.shape[0], block), lambda i: (0, i)),
        out_shape=jax.ShapeDtypeStruct((choice.shape[0], width), BF),
        compiler_params=params(),
        cost_estimate=pl.CostEstimate(flops=2 * 128 * rows * width, bytes_accessed=4000000, transcendentals=0),
    )(choice, back)


def order_kernel(own_ref, ut_ref, first_ref, second_ref):
    own = own_ref[0]
    row, column = iota((512, 512), 0), iota((512, 512), 1)
    origin, slot = (column % 32) // 2 * 32, column % 2
    cc = column // 256
    for ref, yr, k in (
        (first_ref, (column // 32) % 2, (column // 64) % 4),
        (second_ref, (column // 128) % 2, (column // 32) % 4),
    ):
        near = jnp.bitwise_xor(own, yr * 16 + k * 4 + cc * 2)
        move = jnp.where(row == origin + near + slot, 1.0, 0.0).astype(BF)
        ref[...] = jnp.dot(ut_ref[...], move, preferred_element_type=F32).astype(BF)


def ordered(own, ut):
    like = jax.ShapeDtypeStruct(ut.shape, BF)
    return pl.pallas_call(
        order_kernel,
        in_specs=[pl.BlockSpec(memory_space=pltpu.SMEM), pl.BlockSpec(memory_space=pltpu.VMEM)],
        out_shape=(like, like),
        compiler_params=params(),
        cost_estimate=pl.CostEstimate(flops=4 * 336 * 512 * 512, bytes_accessed=1000000, transcendentals=0),
    )(own, ut)


def weight_kernel(count, u_ref, *refs):
    rows = jnp.concatenate([ref[...] for ref in refs[:count]], axis=0)
    refs[-1][...] = jnp.dot(u_ref[...], rows, preferred_element_type=F32).astype(BF)


def weight_grad(u, blocks, width, first, block, base=None):
    hidden = u.shape[0]
    rows, columns = blocks[0].shape
    start = first // block
    specs = [pl.BlockSpec(u.shape, lambda i: (0, 0))]
    specs += [pl.BlockSpec((rows, block), lambda i: (0, i)) for _ in blocks]
    operands = [u, *blocks]
    aliases = {}
    if base is not None:
        specs.append(pl.BlockSpec(memory_space=pl.ANY))
        operands.append(base)
        aliases = {len(operands) - 1: 0}
    return pl.pallas_call(
        functools.partial(weight_kernel, len(blocks)),
        grid=(columns // block,),
        in_specs=specs,
        out_specs=pl.BlockSpec((hidden, block), lambda i: (0, start + i)),
        out_shape=jax.ShapeDtypeStruct((hidden, width), BF),
        input_output_aliases=aliases,
        compiler_params=params(),
        cost_estimate=pl.CostEstimate(
            flops=2 * hidden * 512 * columns, bytes_accessed=2 * (512 + hidden) * columns, transcendentals=0
        ),
    )(*operands)


def swap(value, axis):
    return lax.ppermute(value, axis, [(0, 1), (1, 0)])


def cross(value, mask):
    return lax.ppermute(value, "zl", [(i, i ^ mask) for i in range(4)])


def body(tokens, routes, up_weight, gate_pre, grad_hidden):
    place = {name: lax.axis_index(name).astype(I32) for name in AXES}
    core = place["c"]
    core_arg, zh_arg = core[None], place["zh"][None]
    own_arg = (place["yi"] * 16 + place["zl"] * 4 + core * 2)[None]
    weight_t = jnp.swapaxes(up_weight, 1, 2)[0]
    hidden, width = weight_t.shape
    half = width // 2

    give = other_half(core_arg, weight_t)
    other_t = swap(give, "c")
    ut, u = gated(jnp.swapaxes(gate_pre, 1, 2)[0], jnp.swapaxes(grad_hidden, 1, 2)[0])
    other_u = swap(u, "c")

    route_rows = jnp.pad(routes.astype(BF), ((0, PAD - TOK), (0, 124)), constant_values=-1)
    rows = placed_rows(route_rows, jnp.pad(tokens, ((0, PAD - TOK), (0, 0))))
    far = lax.all_to_all(
        rows.reshape(EXPERTS, CAP, width), FAR, split_axis=0, concat_axis=0, tiled=True
    ).reshape(2 * EXPERTS, width)

    terms = terms_of(core_arg, u, other_u, weight_t, other_t)
    back = lax.all_to_all(
        terms.reshape(16, 32, half), PLANE, split_axis=0, concat_axis=0, tiled=True
    ).reshape(512, half)

    one, two = far[:, :CUT], far[:, CUT:]
    run = jnp.concatenate([two] + [cross(two, k) for k in (1, 2, 3)], axis=0)
    pair = jnp.concatenate([one, swap(one, "yi")], axis=0)
    first = [pair] + [cross(pair, k) for k in (1, 2, 3)]
    second = [run, swap(run, "yi")]
    first += [swap(value, "c") for value in first]
    second += [swap(value, "c") for value in second]
    u_first, u_second = ordered(own_arg, ut)
    grad = weight_grad(u_first, first, width, 0, 1024)
    grad = weight_grad(u_second, second, width, CUT, 1024, grad)

    swapped = swap(route_rows, "c")
    low, high = jnp.where(core == 0, route_rows, swapped), jnp.where(core == 0, swapped, route_rows)
    ring_routes = lax.all_to_all(
        jnp.broadcast_to(jnp.concatenate([low, high], axis=0)[None], (8, 2 * PAD, 128)),
        RING, split_axis=0, concat_axis=0, tiled=True,
    ).reshape(8 * 2 * PAD, 128)
    choice = chooser(zh_arg, ring_routes)
    sums = combined(choice, back)
    parts = lax.all_to_all(
        sums.reshape(8, 2 * PAD, half), RING, split_axis=0, concat_axis=0, tiled=True
    )
    total = jnp.sum(parts.astype(F32), axis=0).astype(BF).reshape(2, PAD, half)
    mine = lax.dynamic_index_in_dim(total, core, 0, keepdims=False)
    other = swap(lax.dynamic_index_in_dim(total, 1 - core, 0, keepdims=False), "c")
    left, right = jnp.where(core == 0, mine, other), jnp.where(core == 0, other, mine)
    grad_rows = jnp.concatenate([left, right], axis=1)[:TOK]
    return (grad_rows, jnp.swapaxes(grad[None], 1, 2))


def solution(mesh):
    fine = Mesh(mesh.devices.reshape(SIZES), AXES)
    part, column = AXES[:4], AXES[4:]
    in_specs = (
        P(AXES, None),
        P(AXES, None),
        P(part, None, column),
        P(part, None, column),
        P(part, None, column),
    )
    out_specs = (P(AXES, None), P(part, None, column))
    return jax.shard_map(body, mesh=fine, in_specs=in_specs, out_specs=out_specs, check_vma=False)
```

time: 184 us -> 161 us (0.88)
  the two profiles are of different devices: /device:TPU:1 before, /device:TPU:61 now
where the time goes in v3:
time: 161 us; the launch traced here: 160 us
  waiting for transfers between devices  66.5 us (41%)
  starting transfers between devices  57.3 us (36%)
  Pallas kernels  18.1 us (11%)
  local copies, waits for them, and re-layouts  14.3 us (9%)
  other arithmetic  3.01 us (2%)
    ppermute x6, waiting for transfers between devices, cross(): return lax.ppermute(value, 'zl', [(i, i ^ mask) for i in range(4)])  41.5 us
    all_to_all x1, starting transfers between devices, body(): lax.all_to_all(sums.reshape(8, 2 * PAD, half), RING, split_axis=0, concat...  15.6 us
    ppermute x12, waiting for transfers between devices, swap(): return lax.ppermute(value, axis, [(0, 1), (1, 0)])  14.6 us
    ppermute x6, starting transfers between devices, cross(): return lax.ppermute(value, 'zl', [(i, i ^ mask) for i in range(4)])  9.29 us
    ppermute x12, starting transfers between devices, swap(): return lax.ppermute(value, axis, [(0, 1), (1, 0)])  9 us
    unnamed x28, local copies, waits for them, and re-layouts  8.72 us
    all_to_all x1, starting transfers between devices, body(): lax.all_to_all(jnp.broadcast_to(jnp.concatenate([low, high], axis=0)[None...  8.01 us
    pallas_call x2, Pallas kernels, weight_grad(): pl.pallas_call(functools.partial(weight_kernel, len(blocks)), grid=(colum...  7.89 us
  transfers between devices with their start and end apart: 22, of which 12 were waited for; matrix products, arithmetic and copies ran while one was open for 5% of the time, Pallas kernels for 10%

profile of v3, /device:TPU:61, one launch (start us, length us, event | category | flops | bytes accessed | tf_op | source)
XLA Modules:
  0.0 160.0 jit_solution(13513573485931091434)
XLA Ops:
  0.6 2.2 %copy-done = bf16[1,6144,336]{1,2,0:T(8,128)(2,1)S(1)} copy-done((bf16[1,6144,336]{1,2,0:T(8,128)(2,1)S(1)}, bf16[1,6144,336]{1,2,0:T(8,128)(2,1)}, u32[]{:S(2)}) %copy-start) | copy-done | bytes 4128792
  2.8 1.9 %shard_map.70 = bf16[336,3072]{1,0:T(8,128)(2,1)} custom-call(s32[1]{0:T(128)} %bitcast.2.core_ref, bf16[336,6144]{1,0:T(8,128)(2,1)S(1)} %bitcast.25), custom_call_target="tpu_custom_call" | custom-call | bytes 4200000 | tf_op jit(solution)/shard_map/pallas_call | solution.py:60
  4.7 0.7 collective-permute-start.2
  5.6 3.4 %collective-permute-done = bf16[8,128]{1,0:T(8,128)(2,1)S(1)} collective-permute-done((bf16[8,128]{1,0:T(8,128)(2,1)S(1)}, bf16[8,128]{1,0:T(8,128)(2,1)S(1)}, u32[]{:S(2)}, u32[]{:S(2)}) %collective-permute-start) | collective-permute-done | bytes 2080 | tf_op jit(solution)/shard_map/ppermute | solution.py:235
  9.0 0.6 broadcast_in_dim.19
  9.6 8.0 %all-to-all-start = ((bf16[8,16,128]{2,1,0:T(8,128)(2,1)}), bf16[8,16,128]{2,1,0:T(8,128)(2,1)S(1)}, u32[]{:S(2)}, u32[]{:S(2)}) async-start(bf16[8,16,128]{2,1,0:T(8,128)(2,1)} %broadcast_in_dim.19), calls=%async_computation | async-start | bytes 65536 | tf_op jit(solution)/shard_map/all_to_all | solution.py:280
  17.7 0.5 shard_map.74
  18.1 1.0 reshape.31
  19.2 4.2 %all-to-all-done = bf16[8,16,128]{2,1,0:T(8,128)(2,1)S(1)} async-done(((bf16[8,16,128]{2,1,0:T(8,128)(2,1)}), bf16[8,16,128]{2,1,0:T(8,128)(2,1)S(1)}, u32[]{:S(2)}, u32[]{:S(2)}) %all-to-all-start) | async-done | bytes 32800 | tf_op jit(solution)/shard_map/all_to_all | solution.py:280
  23.3 7.6 %all-to-all-start.3 = ((bf16[16,2,6144]{2,1,0:T(2,128)(2,1)}), bf16[16,2,6144]{2,1,0:T(2,128)(2,1)S(1)}, u32[]{:S(2)}, u32[]{:S(2)}) async-start(bf16[16,2,6144]{2,1,0:T(2,128)(2,1)} %reshape.31), calls=%async_computation.3 | async-start | bytes 786432 | tf_op jit(solution)/shard_map/all_to_all | solution.py:258
  31.3 2.1 %collective-permute-start.1 = (bf16[512,336]{1,0:T(8,128)(2,1)S(1)}, bf16[512,336]{1,0:T(8,128)(2,1)S(1)}, u32[]{:S(2)}, u32[]{:S(2)}) collective-permute-start(bf16[512,336]{1,0:T(8,128)(2,1)S(1)} %get-tuple-element.6.u_ref), channel_id=1, source_target_pairs={{0,1},{1,0},{2,3},{3,2},{4,5},{5,4},{6,7},{7,6},{8,9},{9,8},{10,11... | collective-permute-start | bytes 1032200 | tf_op jit(solution)/shard_map/ppermute | solution.py:235
  33.4 1.3 collective-permute-done.1.v_ref
  34.8 2.2 %copy-done.1 = bf16[1,6144,336]{1,2,0:T(8,128)(2,1)S(1)} copy-done((bf16[1,6144,336]{1,2,0:T(8,128)(2,1)S(1)}, bf16[1,6144,336]{1,2,0:T(8,128)(2,1)}, u32[]{:S(2)}) %copy-start.1) | copy-done | bytes 4128792
  36.9 5.4 %shard_map.71 = bf16[16,2,16,3072]{3,2,1,0:T(8,128)(2,1)} custom-call(s32[1]{0:T(128)} %bitcast.2.core_ref, bf16[512,336]{1,0:T(8,128)(2,1)S(1)} %get-tuple-element.6.u_ref, bf16[512,336]{1,0:T(8,128)(2,1)S(1)} %collective-permute-done.1.v_ref, bf16[336,6144]{1,0:T(8,128)(2,1)S(1)} %bitcast.26, bf16[336,3072]{1,0:T(8,128)(2,1)S(1)} %collective-permute-done.2.x_ref), custom_call_target="tpu_custom_call" | custom-call | flops 2113929216 | bytes 8000000 | tf_op jit(solution)/shard_map/pallas_call | solution.py:87
  42.4 0.7 copy-done.9
  43.2 7.8 %all-to-all-start.1 = ((bf16[16,32,3072]{2,1,0:T(8,128)(2,1)}), bf16[16,32,3072]{2,1,0:T(8,128)(2,1)S(1)}, u32[]{:S(2)}, u32[]{:S(2)}) async-start(bf16[16,32,3072]{2,1,0:T(8,128)(2,1)} %bitcast.10), calls=%async_computation.1 | async-start | bytes 6291456 | tf_op jit(solution)/shard_map/all_to_all | solution.py:263
  50.9 1.9 %reshape.32 = bf16[32,6144]{1,0:T(8,128)(2,1)} reshape(bf16[16,2,6144]{2,1,0:T(2,128)(2,1)} %copy-done.9) | data formatting | bytes 786432 | tf_op jit(solution)/shard_map/reshape | solution.py:260
  52.8 1.0 slice.12
  53.8 3.9 %collective-permute-start.6 = (bf16[32,4096]{1,0:T(8,128)(2,1)S(1)}, bf16[32,4096]{1,0:T(8,128)(2,1)S(1)}, u32[]{:S(2)}, u32[]{:S(2)}) collective-permute-start(bf16[32,4096]{1,0:T(8,128)(2,1)S(1)} %slice.12), channel_id=1, source_target_pairs={{0,6},{2,4},{4,2},{6,0},{1,7},{3,5},{5,3},{7,1},{8,14},{10,12},{12... | collective-permute-start | bytes 786440 | tf_op jit(solution)/shard_map/ppermute | solution.py:239
  57.7 1.3 collective-permute-start.4
  59.0 13.4 %collective-permute-done.6 = bf16[32,4096]{1,0:T(8,128)(2,1)S(1)} collective-permute-done((bf16[32,4096]{1,0:T(8,128)(2,1)S(1)}, bf16[32,4096]{1,0:T(8,128)(2,1)S(1)}, u32[]{:S(2)}, u32[]{:S(2)}) %collective-permute-start.6) | collective-permute-done | bytes 262176 | tf_op jit(solution)/shard_map/ppermute | solution.py:239
  72.4 5.6 %collective-permute-done.5 = bf16[32,4096]{1,0:T(8,128)(2,1)S(1)} collective-permute-done((bf16[32,4096]{1,0:T(8,128)(2,1)S(1)}, bf16[32,4096]{1,0:T(8,128)(2,1)S(1)}, u32[]{:S(2)}, u32[]{:S(2)}) %collective-permute-start.5) | collective-permute-done | bytes 262176 | tf_op jit(solution)/shard_map/ppermute | solution.py:239
  78.0 1.1 pad_maximum_fusion.refs_0_
  79.0 0.6 collective-permute-start.7
  79.6 0.3 shard_map.68.choice_ref
  80.0 6.1 %all-to-all-done.1 = bf16[16,32,3072]{2,1,0:T(8,128)(2,1)S(1)} async-done(((bf16[16,32,3072]{2,1,0:T(8,128)(2,1)}), bf16[16,32,3072]{2,1,0:T(8,128)(2,1)S(1)}, u32[]{:S(2)}, u32[]{:S(2)}) %all-to-all-start.1) | async-done | bytes 3145760 | tf_op jit(solution)/shard_map/all_to_all | solution.py:263
  86.1 1.2 shard_map.72
  87.3 0.9 copy-done.2
  88.2 15.6 %all-to-all-start.2 = ((bf16[8,16,3072]{2,1,0:T(8,128)(2,1)}), bf16[8,16,3072]{2,1,0:T(8,128)(2,1)}, u32[]{:S(2)}, u32[]{:S(2)}) async-start(bf16[8,16,3072]{2,1,0:T(8,128)(2,1)} %bitcast.28), calls=%async_computation.2 | async-start | bytes 1572864 | tf_op jit(solution)/shard_map/all_to_all | solution.py:286
  103.8 0.9 slice.13
  104.9 9.8 %collective-permute-done.10 = bf16[32,2048]{1,0:T(8,128)(2,1)S(1)} collective-permute-done((bf16[32,2048]{1,0:T(8,128)(2,1)S(1)}, bf16[32,2048]{1,0:T(8,128)(2,1)S(1)}, u32[]{:S(2)}, u32[]{:S(2)}) %collective-permute-start.10) | collective-permute-done | bytes 131104 | tf_op jit(solution)/shard_map/ppermute | solution.py:235
  114.7 0.4 collective-permute-start.8
  115.4 4.1 %collective-permute-start.12 = (bf16[64,2048]{1,0:T(8,128)(2,1)S(1)}, bf16[64,2048]{1,0:T(8,128)(2,1)S(1)}, u32[]{:S(2)}, u32[]{:S(2)}) collective-permute-start(bf16[64,2048]{1,0:T(8,128)(2,1)S(1)} %pad_maximum_fusion.1.refs_0_), channel_id=1, source_target_pairs={{0,4},{2,6},{4,0},{6,2},{1,5},{3,7},{5,1},{7,3},{8,12},{10,14},{12... | collective-permute-start | bytes 786440 | tf_op jit(solution)/shard_map/ppermute | solution.py:239
  119.4 11.1 %collective-permute-done.11.refs_1_ = bf16[64,2048]{1,0:T(8,128)(2,1)S(1)} collective-permute-done((bf16[64,2048]{1,0:T(8,128)(2,1)S(1)}, bf16[64,2048]{1,0:T(8,128)(2,1)S(1)}, u32[]{:S(2)}, u32[]{:S(2)}) %collective-permute-start.11) | collective-permute-done | bytes 262176 | tf_op jit(solution)/shard_map/ppermute | solution.py:239
  130.5 2.5 %collective-permute-start.14 = (bf16[64,2048]{1,0:T(8,128)(2,1)S(1)}, bf16[64,2048]{1,0:T(8,128)(2,1)S(1)}, u32[]{:S(2)}, u32[]{:S(2)}) collective-permute-start(bf16[64,2048]{1,0:T(8,128)(2,1)S(1)} %pad_maximum_fusion.1.refs_0_), channel_id=1, source_target_pairs={{0,1},{1,0},{2,3},{3,2},{4,5},{5,4},{6,7},{7,6},{8,9},{9,8},{10,11... | collective-permute-start | bytes 786440 | tf_op jit(solution)/shard_map/ppermute | solution.py:235
  133.0 5.7 %collective-permute-done.12.refs_2_ = bf16[64,2048]{1,0:T(8,128)(2,1)S(1)} collective-permute-done((bf16[64,2048]{1,0:T(8,128)(2,1)S(1)}, bf16[64,2048]{1,0:T(8,128)(2,1)S(1)}, u32[]{:S(2)}, u32[]{:S(2)}) %collective-permute-start.12) | collective-permute-done | bytes 262176 | tf_op jit(solution)/shard_map/ppermute | solution.py:239
  138.8 1.1 collective-permute-start.15
  139.9 5.6 %collective-permute-done.13.refs_3_ = bf16[64,2048]{1,0:T(8,128)(2,1)S(1)} collective-permute-done((bf16[64,2048]{1,0:T(8,128)(2,1)S(1)}, bf16[64,2048]{1,0:T(8,128)(2,1)S(1)}, u32[]{:S(2)}, u32[]{:S(2)}) %collective-permute-start.13) | collective-permute-done | bytes 262176 | tf_op jit(solution)/shard_map/ppermute | solution.py:239
  145.4 0.8 collective-permute-start.16
  146.3 0.7 copy-done.5
  147.0 1.0 copy-done.8
  147.9 0.5 shard_map.73
  148.6 0.9 copy-done.6
  149.6 3.0 %shard_map.75.refs_4_ = bf16[336,6144]{1,0:T(8,128)(2,1)} custom-call(bf16[336,512]{1,0:T(8,128)(2,1)S(1)} %get-tuple-element.9.u_ref, bf16[64,2048]{1,0:T(8,128)(2,1)S(1)} %pad_maximum_fusion.1.refs_0_, bf16[64,2048]{1,0:T(8,128)(2,1)S(1)} %collective-permute-done.11.refs_1_, bf16[64,2048]{1,0:T(8,128)(2,1)S(1)} %collective-permute-done.12.refs_2_, ...), custom_call_target="tpu_custom_call" | custom-call | flops 704643072 | bytes 3473408 | tf_op jit(solution)/shard_map/pallas_call | solution.py:220
  152.6 1.2 reduce_sum.12
  153.9 0.5 collective-permute-start.3
  154.5 4.9 %shard_map.76 = bf16[336,6144]{1,0:T(8,128)(2,1)} custom-call(bf16[336,512]{1,0:T(8,128)(2,1)S(1)} %get-tuple-element.8.u_ref, bf16[128,4096]{1,0:T(8,128)(2,1)} %pad_maximum_fusion.refs_0_, bf16[128,4096]{1,0:T(8,128)(2,1)} %collective-permute-done.7.refs_1_, bf16[128,4096]{1,0:T(8,128)(2,1)S(1)} %collective-permute-done.8.refs_2_, ...), custom_call_target="tpu_custom_call", output_to_operand_aliasing={{}: (5, {})} | custom-call | flops 1409286144 | bytes 6946816 | tf_op jit(solution)/shard_map/pallas_call | solution.py:220
  159.4 0.6 pad_maximum_fusion.2
  (50 shorter events, 1.3 us)
Async XLA Ops:
  0.6 2.2 %copy-start = (bf16[1,6144,336]{1,2,0:T(8,128)(2,1)S(1)}, bf16[1,6144,336]{1,2,0:T(8,128)(2,1)}, u32[]{:S(2)}) copy-start(bf16[1,6144,336]{1,2,0:T(8,128)(2,1)} %param.7) | copy-start | bytes 12386308
  2.8 2.6 %copy-start.13 = (s32[6,4]{0,1:T(4,128)S(1)}, s32[6,4]{0,1:T(4,128)}, u32[]{:S(2)}) copy-start(s32[6,4]{0,1:T(4,128)} %param.6) | copy-start | bytes 292
  2.8 14.8 %copy-start.12 = (bf16[6,6144]{1,0:T(8,128)(2,1)S(1)}, bf16[6,6144]{1,0:T(8,128)(2,1)}, u32[]{:S(2)}) copy-start(bf16[6,6144]{1,0:T(8,128)(2,1)} %param.5) | copy-start | bytes 221188
  4.7 26.3 %copy-start.3 = (bf16[1,512,336]{1,2,0:T(8,128)(2,1)S(1)}, bf16[1,512,336]{1,2,0:T(8,128)(2,1)}, u32[]{:S(2)}) copy-start(bf16[1,512,336]{1,2,0:T(8,128)(2,1)} %param.8) | copy-start | bytes 1032196
  4.7 26.3 %copy-start.4 = (bf16[1,512,336]{1,2,0:T(8,128)(2,1)S(1)}, bf16[1,512,336]{1,2,0:T(8,128)(2,1)}, u32[]{:S(2)}) copy-start(bf16[1,512,336]{1,2,0:T(8,128)(2,1)} %param.9) | copy-start | bytes 1032196
  4.7 30.0 %collective-permute-start.2 = (bf16[336,3072]{1,0:T(8,128)(2,1)}, bf16[336,3072]{1,0:T(8,128)(2,1)S(1)}, u32[]{:S(2)}, u32[]{:S(2)}) collective-permute-start(bf16[336,3072]{1,0:T(8,128)(2,1)} %shard_map.70), channel_id=1, source_target_pairs={{0,1},{1,0},{2,3},{3,2},{4,5},{5,4},{6,7},{7,6},{8,9},{9,8},{10,11... | collective-permute-start | bytes 6193160 | tf_op jit(solution)/shard_map/ppermute | solution.py:235
  5.5 3.5 %collective-permute-start = (bf16[8,128]{1,0:T(8,128)(2,1)S(1)}, bf16[8,128]{1,0:T(8,128)(2,1)S(1)}, u32[]{:S(2)}, u32[]{:S(2)}) collective-permute-start(bf16[8,128]{1,0:T(8,128)(2,1)S(1)} %pad.8.routes_ref), channel_id=1, source_target_pairs={{0,1},{1,0},{2,3},{3,2},{4,5},{5,4},{6,7},{7,6},{8,9},{9,8},{10,11... | collective-permute-start | bytes 6152 | tf_op jit(solution)/shard_map/ppermute | solution.py:235
  9.6 13.7 %all-to-all-start = ((bf16[8,16,128]{2,1,0:T(8,128)(2,1)}), bf16[8,16,128]{2,1,0:T(8,128)(2,1)S(1)}, u32[]{:S(2)}, u32[]{:S(2)}) async-start(bf16[8,16,128]{2,1,0:T(8,128)(2,1)} %broadcast_in_dim.19), calls=%async_computation | async-start | bytes 65536 | tf_op jit(solution)/shard_map/all_to_all | solution.py:280
  23.3 19.1 %all-to-all-start.3 = ((bf16[16,2,6144]{2,1,0:T(2,128)(2,1)}), bf16[16,2,6144]{2,1,0:T(2,128)(2,1)S(1)}, u32[]{:S(2)}, u32[]{:S(2)}) async-start(bf16[16,2,6144]{2,1,0:T(2,128)(2,1)} %reshape.31), calls=%async_computation.3 | async-start | bytes 786432 | tf_op jit(solution)/shard_map/all_to_all | solution.py:258
  31.3 11.0 %copy-start.7 = (bf16[336,512]{1,0:T(8,128)(2,1)}, bf16[336,512]{1,0:T(8,128)(2,1)S(1)}, u32[]{:S(2)}) copy-start(bf16[336,512]{1,0:T(8,128)(2,1)S(1)} %get-tuple-element.7.ut_ref) | copy-start | bytes 1032196
  31.3 3.4 %collective-permute-start.1 = (bf16[512,336]{1,0:T(8,128)(2,1)S(1)}, bf16[512,336]{1,0:T(8,128)(2,1)S(1)}, u32[]{:S(2)}, u32[]{:S(2)}) collective-permute-start(bf16[512,336]{1,0:T(8,128)(2,1)S(1)} %get-tuple-element.6.u_ref), channel_id=1, source_target_pairs={{0,1},{1,0},{2,3},{3,2},{4,5},{5,4},{6,7},{7,6},{8,9},{9,8},{10,11... | collective-permute-start | bytes 1032200 | tf_op jit(solution)/shard_map/ppermute | solution.py:235
  34.7 2.2 %copy-start.1 = (bf16[1,6144,336]{1,2,0:T(8,128)(2,1)S(1)}, bf16[1,6144,336]{1,2,0:T(8,128)(2,1)}, u32[]{:S(2)}) copy-start(bf16[1,6144,336]{1,2,0:T(8,128)(2,1)} %param.7) | copy-start | bytes 12386308
  42.4 0.7 copy-start.9
  43.2 42.9 %all-to-all-start.1 = ((bf16[16,32,3072]{2,1,0:T(8,128)(2,1)}), bf16[16,32,3072]{2,1,0:T(8,128)(2,1)S(1)}, u32[]{:S(2)}, u32[]{:S(2)}) async-start(bf16[16,32,3072]{2,1,0:T(8,128)(2,1)} %bitcast.10), calls=%async_computation.1 | async-start | bytes 6291456 | tf_op jit(solution)/shard_map/all_to_all | solution.py:263
  53.8 18.5 %collective-permute-start.6 = (bf16[32,4096]{1,0:T(8,128)(2,1)S(1)}, bf16[32,4096]{1,0:T(8,128)(2,1)S(1)}, u32[]{:S(2)}, u32[]{:S(2)}) collective-permute-start(bf16[32,4096]{1,0:T(8,128)(2,1)S(1)} %slice.12), channel_id=1, source_target_pairs={{0,6},{2,4},{4,2},{6,0},{1,7},{3,5},{5,3},{7,1},{8,14},{10,12},{12... | collective-permute-start | bytes 786440 | tf_op jit(solution)/shard_map/ppermute | solution.py:239
  57.7 20.3 %collective-permute-start.5 = (bf16[32,4096]{1,0:T(8,128)(2,1)S(1)}, bf16[32,4096]{1,0:T(8,128)(2,1)S(1)}, u32[]{:S(2)}, u32[]{:S(2)}) collective-permute-start(bf16[32,4096]{1,0:T(8,128)(2,1)S(1)} %slice.12), channel_id=1, source_target_pairs={{0,4},{2,6},{4,0},{6,2},{1,5},{3,7},{5,1},{7,3},{8,12},{10,14},{12... | collective-permute-start | bytes 786440 | tf_op jit(solution)/shard_map/ppermute | solution.py:239
  57.7 20.3 %collective-permute-start.4 = (bf16[32,4096]{1,0:T(8,128)(2,1)S(1)}, bf16[32,4096]{1,0:T(8,128)(2,1)S(1)}, u32[]{:S(2)}, u32[]{:S(2)}) collective-permute-start(bf16[32,4096]{1,0:T(8,128)(2,1)S(1)} %slice.12), channel_id=1, source_target_pairs={{0,2},{2,0},{4,6},{6,4},{1,3},{3,1},{5,7},{7,5},{8,10},{10,8},{12,... | collective-permute-start | bytes 786440 | tf_op jit(solution)/shard_map/ppermute | solution.py:239
  79.0 36.1 %collective-permute-start.7 = (bf16[128,4096]{1,0:T(8,128)(2,1)}, bf16[128,4096]{1,0:T(8,128)(2,1)}, u32[]{:S(2)}, u32[]{:S(2)}) collective-permute-start(bf16[128,4096]{1,0:T(8,128)(2,1)} %pad_maximum_fusion.refs_0_), channel_id=1, source_target_pairs={{0,8},{8,0},{1,9},{9,1},{2,10},{10,2},{3,11},{11,3},{4,12},{12,4},... | collective-permute-start | bytes 3145736 | tf_op jit(solution)/shard_map/ppermute | solution.py:235
  87.3 0.9 copy-start.2
  88.2 64.4 %all-to-all-start.2 = ((bf16[8,16,3072]{2,1,0:T(8,128)(2,1)}), bf16[8,16,3072]{2,1,0:T(8,128)(2,1)}, u32[]{:S(2)}, u32[]{:S(2)}) async-start(bf16[8,16,3072]{2,1,0:T(8,128)(2,1)} %bitcast.28), calls=%async_computation.2 | async-start | bytes 1572864 | tf_op jit(solution)/shard_map/all_to_all | solution.py:286
  104.8 9.9 %collective-permute-start.10 = (bf16[32,2048]{1,0:T(8,128)(2,1)S(1)}, bf16[32,2048]{1,0:T(8,128)(2,1)S(1)}, u32[]{:S(2)}, u32[]{:S(2)}) collective-permute-start(bf16[32,2048]{1,0:T(8,128)(2,1)S(1)} %slice.13), channel_id=1, source_target_pairs={{0,8},{8,0},{1,9},{9,1},{2,10},{10,2},{3,11},{11,3},{4,12},{12,4},... | collective-permute-start | bytes 393224 | tf_op jit(solution)/shard_map/ppermute | solution.py:235
  114.6 15.9 %collective-permute-start.11 = (bf16[64,2048]{1,0:T(8,128)(2,1)S(1)}, bf16[64,2048]{1,0:T(8,128)(2,1)S(1)}, u32[]{:S(2)}, u32[]{:S(2)}) collective-permute-start(bf16[64,2048]{1,0:T(8,128)(2,1)S(1)} %pad_maximum_fusion.1.refs_0_), channel_id=1, source_target_pairs={{0,2},{2,0},{4,6},{6,4},{1,3},{3,1},{5,7},{7,5},{8,10},{10,8},{12,... | collective-permute-start | bytes 786440 | tf_op jit(solution)/shard_map/ppermute | solution.py:239
  114.7 39.6 %collective-permute-start.8 = (bf16[128,4096]{1,0:T(8,128)(2,1)}, bf16[128,4096]{1,0:T(8,128)(2,1)S(1)}, u32[]{:S(2)}, u32[]{:S(2)}) collective-permute-start(bf16[128,4096]{1,0:T(8,128)(2,1)} %pad_maximum_fusion.refs_0_), channel_id=1, source_target_pairs={{0,1},{1,0},{2,3},{3,2},{4,5},{5,4},{6,7},{7,6},{8,9},{9,8},{10,11... | collective-permute-start | bytes 3145736 | tf_op jit(solution)/shard_map/ppermute | solution.py:235
  115.2 39.2 %collective-permute-start.9 = (bf16[128,4096]{1,0:T(8,128)(2,1)}, bf16[128,4096]{1,0:T(8,128)(2,1)S(1)}, u32[]{:S(2)}, u32[]{:S(2)}) collective-permute-start(bf16[128,4096]{1,0:T(8,128)(2,1)} %collective-permute-done.7.refs_1_), channel_id=1, source_target_pairs={{0,1},{1,0},{2,3},{3,2},{4,5},{5,4},{6,7},{7,6},{8,9},{9,8},{10,11... | collective-permute-start | bytes 3145736 | tf_op jit(solution)/shard_map/ppermute | solution.py:235
  115.4 23.4 %collective-permute-start.12 = (bf16[64,2048]{1,0:T(8,128)(2,1)S(1)}, bf16[64,2048]{1,0:T(8,128)(2,1)S(1)}, u32[]{:S(2)}, u32[]{:S(2)}) collective-permute-start(bf16[64,2048]{1,0:T(8,128)(2,1)S(1)} %pad_maximum_fusion.1.refs_0_), channel_id=1, source_target_pairs={{0,4},{2,6},{4,0},{6,2},{1,5},{3,7},{5,1},{7,3},{8,12},{10,14},{12... | collective-permute-start | bytes 786440 | tf_op jit(solution)/shard_map/ppermute | solution.py:239
  119.4 26.0 %collective-permute-start.13 = (bf16[64,2048]{1,0:T(8,128)(2,1)S(1)}, bf16[64,2048]{1,0:T(8,128)(2,1)S(1)}, u32[]{:S(2)}, u32[]{:S(2)}) collective-permute-start(bf16[64,2048]{1,0:T(8,128)(2,1)S(1)} %pad_maximum_fusion.1.refs_0_), channel_id=1, source_target_pairs={{0,6},{2,4},{4,2},{6,0},{1,7},{3,5},{5,3},{7,1},{8,14},{10,12},{12... | collective-permute-start | bytes 786440 | tf_op jit(solution)/shard_map/ppermute | solution.py:239
  130.5 15.7 %collective-permute-start.14 = (bf16[64,2048]{1,0:T(8,128)(2,1)S(1)}, bf16[64,2048]{1,0:T(8,128)(2,1)S(1)}, u32[]{:S(2)}, u32[]{:S(2)}) collective-permute-start(bf16[64,2048]{1,0:T(8,128)(2,1)S(1)} %pad_maximum_fusion.1.refs_0_), channel_id=1, source_target_pairs={{0,1},{1,0},{2,3},{3,2},{4,5},{5,4},{6,7},{7,6},{8,9},{9,8},{10,11... | collective-permute-start | bytes 786440 | tf_op jit(solution)/shard_map/ppermute | solution.py:235
  138.8 9.7 %collective-permute-start.15 = (bf16[64,2048]{1,0:T(8,128)(2,1)S(1)}, bf16[64,2048]{1,0:T(8,128)(2,1)}, u32[]{:S(2)}, u32[]{:S(2)}) collective-permute-start(bf16[64,2048]{1,0:T(8,128)(2,1)S(1)} %collective-permute-done.11.refs_1_), channel_id=1, source_target_pairs={{0,1},{1,0},{2,3},{3,2},{4,5},{5,4},{6,7},{7,6},{8,9},{9,8},{10,11... | collective-permute-start | bytes 786440 | tf_op jit(solution)/shard_map/ppermute | solution.py:235
  145.4 3.1 %collective-permute-start.16 = (bf16[64,2048]{1,0:T(8,128)(2,1)S(1)}, bf16[64,2048]{1,0:T(8,128)(2,1)}, u32[]{:S(2)}, u32[]{:S(2)}) collective-permute-start(bf16[64,2048]{1,0:T(8,128)(2,1)S(1)} %collective-permute-done.12.refs_2_), channel_id=1, source_target_pairs={{0,1},{1,0},{2,3},{3,2},{4,5},{5,4},{6,7},{7,6},{8,9},{9,8},{10,11... | collective-permute-start | bytes 786440 | tf_op jit(solution)/shard_map/ppermute | solution.py:235
  146.3 0.7 copy-start.5
  147.0 1.7 %collective-permute-start.17 = (bf16[64,2048]{1,0:T(8,128)(2,1)S(1)}, bf16[64,2048]{1,0:T(8,128)(2,1)}, u32[]{:S(2)}, u32[]{:S(2)}) collective-permute-start(bf16[64,2048]{1,0:T(8,128)(2,1)S(1)} %collective-permute-done.13.refs_3_), channel_id=1, source_target_pairs={{0,1},{1,0},{2,3},{3,2},{4,5},{5,4},{6,7},{7,6},{8,9},{9,8},{10,11... | collective-permute-start | bytes 786440 | tf_op jit(solution)/shard_map/ppermute | solution.py:235
  147.0 1.0 copy-start.8
  148.6 1.0 copy-start.6
  153.8 0.6 copy-start.10
  153.9 5.5 %collective-permute-start.3 = (bf16[8,3072]{1,0:T(8,128)(2,1)S(1)}, bf16[8,3072]{1,0:T(8,128)(2,1)S(1)}, u32[]{:S(2)}, u32[]{:S(2)}) collective-permute-start(bf16[8,3072]{1,0:T(8,128)(2,1)S(1)} %dynamic-slice_bitcast_fusion), channel_id=1, source_target_pairs={{0,1},{1,0},{2,3},{3,2},{4,5},{5,4},{6,7},{7,6},{8,9},{9,8},{10,11... | collective-permute-start | bytes 147464 | tf_op jit(solution)/shard_map/ppermute | solution.py:235
  154.5 4.9 %copy-start.11 = (bf16[16,3072]{1,0:T(8,128)(2,1)S(1)}, bf16[16,3072]{1,0:T(8,128)(2,1)}, u32[]{:S(2)}) copy-start(bf16[16,3072]{1,0:T(8,128)(2,1)} %copy-done.10) | copy-start | bytes 294916

commit v4 on v3

v4 whole, which is shorter than its diff:
```python
import functools

import jax
import jax.numpy as jnp
from jax import lax
from jax.experimental import pallas as pl
from jax.experimental.pallas import tpu as pltpu
from jax.sharding import Mesh, PartitionSpec as P

EXPERTS = 16
CAP = 2
AXES = ("zh", "x", "yp", "yi", "zl", "c")
SIZES = (2, 4, 2, 2, 4, 2)
FAR = ("zh", "x", "yp")
PLANE = ("x", "yp", "yi")
RING = ("zh", "zl")
TOK = 6
PAD = 8
FOLD = 768
EXTRA = 128
MIB = 1 << 20
BF, F32, I32 = jnp.bfloat16, jnp.float32, jnp.int32


def params(mib=24):
    return pltpu.CompilerParams(vmem_limit_bytes=mib * MIB)


def iota(shape, dim):
    return lax.broadcasted_iota(I32, shape, dim)


def gate_kernel(gate_ref, grad_ref, ut_ref, u_ref):
    gate = gate_ref[...].astype(F32)
    value = (grad_ref[...].astype(F32) * (gate / (1.0 + jnp.exp(-gate)))).astype(BF)
    ut_ref[...] = value
    u_ref[...] = value.T


def gated(gate_t, grad_t):
    hidden, rows = gate_t.shape
    return pl.pallas_call(
        gate_kernel,
        out_shape=(
            jax.ShapeDtypeStruct((hidden, rows), BF),
            jax.ShapeDtypeStruct((rows, hidden), BF),
        ),
        compiler_params=params(60),
        cost_estimate=pl.CostEstimate(flops=10**6, bytes_accessed=1400000, transcendentals=172032),
    )(gate_t, grad_t)


def copy_kernel(core_ref, in_ref, out_ref):
    out_ref[...] = in_ref[...]


def other_half(core, weight_t):
    hidden, width = weight_t.shape
    block = 1024
    steps = width // 2 // block
    return pl.pallas_call(
        copy_kernel,
        grid_spec=pltpu.PrefetchScalarGridSpec(
            num_scalar_prefetch=1,
            grid=(steps,),
            in_specs=[pl.BlockSpec((hidden, block), lambda i, core: (0, (1 - core[0]) * steps + i))],
            out_specs=pl.BlockSpec((hidden, block), lambda i, core: (0, i)),
        ),
        out_shape=jax.ShapeDtypeStruct((hidden, width // 2), BF),
        compiler_params=params(60),
        cost_estimate=pl.CostEstimate(flops=0, bytes_accessed=4200000, transcendentals=0),
    )(core, weight_t)


def terms_kernel(core_ref, u_ref, v_ref, w_ref, x_ref, out_ref):
    term = jnp.dot(u_ref[...], w_ref[...], preferred_element_type=F32)
    term += jnp.dot(v_ref[...], x_ref[...], preferred_element_type=F32)
    term = term.astype(BF).reshape(2, 16, 16, term.shape[1])
    out_ref[:, 0, :, :] = term[0]
    out_ref[:, 1, :, :] = term[1]


def terms_of(core, u, v, weight_t, other_t):
    rows, hidden = u.shape
    half = other_t.shape[1]
    block = 512
    steps = half // block
    return pl.pallas_call(
        terms_kernel,
        grid_spec=pltpu.PrefetchScalarGridSpec(
            num_scalar_prefetch=1,
            grid=(steps,),
            in_specs=[
                pl.BlockSpec((rows, hidden), lambda i, core: (0, 0)),
                pl.BlockSpec((rows, hidden), lambda i, core: (0, 0)),
                pl.BlockSpec((hidden, block), lambda i, core: (0, core[0] * steps + i)),
                pl.BlockSpec((hidden, block), lambda i, core: (0, i)),
            ],
            out_specs=pl.BlockSpec((16, 2, 16, block), lambda i, core: (0, 0, 0, i)),
        ),
        out_shape=jax.ShapeDtypeStruct((16, 2, 16, half), BF),
        compiler_params=params(),
        cost_estimate=pl.CostEstimate(flops=4 * rows * hidden * half, bytes_accessed=8000000, transcendentals=0),
    )(core, u, v, weight_t, other_t)


def named_mask(routes, expert):
    named = jnp.zeros(expert.shape, F32)
    for k in range(4):
        named += jnp.where(routes[:, k : k + 1] == expert, 1.0, 0.0)
    return named


def place_kernel(tokens_ref, routes_ref, out_ref, held_ref, named_ref):
    count, width = tokens_ref.shape
    held_ref[...] = jnp.zeros(held_ref.shape, F32)
    held_ref[:count, :] = tokens_ref[...].astype(F32)
    named_ref[...] = jnp.full(named_ref.shape, -1.0, F32)
    named_ref[:count, :4] = routes_ref[...].astype(F32).T
    routes = named_ref[...]
    column = iota((PAD, 256), 1)
    named = named_mask(routes, (column // 16).astype(F32))
    lower = jnp.where(iota((PAD, PAD), 0) > iota((PAD, PAD), 1), 1.0, 0.0)
    before = jnp.dot(lower, named, preferred_element_type=F32)
    chosen = jnp.where(before == (column // 8 % 2).astype(F32), named, 0.0)
    total = jnp.zeros((256, FOLD), F32)
    for fold in range(width // FOLD):
        pick = jnp.where(column % 8 == fold, chosen, 0.0).T.astype(BF)
        piece = held_ref[:, fold * FOLD : fold * FOLD + FOLD].astype(BF)
        total += jnp.dot(pick, piece, preferred_element_type=F32)
    out_ref[:, :FOLD] = total.astype(BF)
    spread = jnp.where(iota((256, PAD), 0) % PAD == iota((256, PAD), 1), 1.0, 0.0).astype(BF)
    out_ref[:, FOLD:] = jnp.dot(spread, routes.astype(BF), preferred_element_type=F32).astype(BF)


def placed_rows(tokens, routes):
    return pl.pallas_call(
        place_kernel,
        out_shape=jax.ShapeDtypeStruct((256, FOLD + EXTRA), BF),
        scratch_shapes=[pltpu.VMEM((PAD, tokens.shape[1]), F32), pltpu.VMEM((PAD, EXTRA), F32)],
        compiler_params=params(60),
        cost_estimate=pl.CostEstimate(flops=10**6, bytes_accessed=500000, transcendentals=0),
    )(tokens, routes)


def unfold_kernel(at_ref, rows_ref, out_ref):
    width = out_ref.shape[1] - EXTRA
    rows = rows_ref[...]
    r, s = iota((32, 256), 0), iota((32, 256), 1)
    for fold in range(width // FOLD):
        move = jnp.where(s == r * 8 + fold, 1.0, 0.0).astype(BF)
        piece = jnp.dot(move, rows[:, :FOLD], preferred_element_type=F32)
        out_ref[:, fold * FOLD : fold * FOLD + FOLD] = piece.astype(BF)
    move = jnp.where((s == r // 8 * 128 + at_ref[0] * 16 + r % 8) & (r < 16), 1.0, 0.0).astype(BF)
    out_ref[:, width:] = jnp.dot(move, rows[:, FOLD:], preferred_element_type=F32).astype(BF)


def unfold(at, rows, width):
    return pl.pallas_call(
        unfold_kernel,
        in_specs=[pl.BlockSpec(memory_space=pltpu.SMEM), pl.BlockSpec(memory_space=pltpu.VMEM)],
        out_shape=jax.ShapeDtypeStruct((32, width + EXTRA), BF),
        compiler_params=params(),
        cost_estimate=pl.CostEstimate(flops=10**6, bytes_accessed=1000000, transcendentals=0),
    )(at, rows)


def choose_kernel(at_ref, mine_ref, other_ref, out_ref):
    shape = (8 * 2 * PAD, 512)
    row, column = iota(shape, 0), iota(shape, 1)
    expert = at_ref[0] * 8 + column // 64
    routes = jnp.concatenate([mine_ref[...], other_ref[...]], axis=0)
    r, s = iota((128, 256), 0), iota((128, 256), 1)
    came = (r // 8) % 2 * 128 + jnp.bitwise_xor((r // 16) % 4, at_ref[1]) * 32 + r // 64 * 8 + r % 8
    move = jnp.where(came == s, 1.0, 0.0).astype(BF)
    named = named_mask(jnp.dot(move, routes, preferred_element_type=F32), expert.astype(F32))
    r, s = iota((128, 128), 0), iota((128, 128), 1)
    lower = jnp.where((r // PAD == s // PAD) & (r > s), 1.0, 0.0)
    before = jnp.dot(lower.astype(BF), named.astype(BF), preferred_element_type=F32)
    device = row // 16 * 2 + jnp.bitwise_xor((row // 8) % 2, at_ref[2])
    fits = (before == (column % 2).astype(F32)) & (device == (column // 2) % 16)
    out_ref[...] = jnp.where(fits, named, 0.0).astype(BF)


def chooser(at, mine, other):
    return pl.pallas_call(
        choose_kernel,
        in_specs=[pl.BlockSpec(memory_space=pltpu.SMEM)] + [pl.BlockSpec(memory_space=pltpu.VMEM)] * 2,
        out_shape=jax.ShapeDtypeStruct((8 * 2 * PAD, 512), BF),
        compiler_params=params(),
        cost_estimate=pl.CostEstimate(flops=10**6, bytes_accessed=200000, transcendentals=0),
    )(at, mine, other)


def combine_kernel(choice_ref, back_ref, out_ref):
    out_ref[...] = jnp.dot(choice_ref[...], back_ref[...], preferred_element_type=F32).astype(BF)


def combined(choice, back):
    rows, width = back.shape
    block = 1024
    return pl.pallas_call(
        combine_kernel,
        grid=(width // block,),
        in_specs=[
            pl.BlockSpec(choice.shape, lambda i: (0, 0)),
            pl.BlockSpec((rows, block), lambda i: (0, i)),
        ],
        out_specs=pl.BlockSpec((choice.shape[0], block), lambda i: (0, i)),
        out_shape=jax.ShapeDtypeStruct((choice.shape[0], width), BF),
        compiler_params=params(),
        cost_estimate=pl.CostEstimate(flops=2 * 128 * rows * width, bytes_accessed=4000000, transcendentals=0),
    )(choice, back)


def order_kernel(own_ref, ut_ref, out_ref):
    row, column = iota((512, 512), 0), iota((512, 512), 1)
    near = (column // 128) % 2 * 16 + (column // 32) % 4 * 4 + column // 256 * 2
    origin = column % 32 // 2 * 32 + jnp.bitwise_xor(own_ref[0], near) + column % 2
    move = jnp.where(row == origin, 1.0, 0.0).astype(BF)
    out_ref[...] = jnp.dot(ut_ref[...], move, preferred_element_type=F32).astype(BF)


def ordered(own, ut):
    return pl.pallas_call(
        order_kernel,
        in_specs=[pl.BlockSpec(memory_space=pltpu.SMEM), pl.BlockSpec(memory_space=pltpu.VMEM)],
        out_shape=jax.ShapeDtypeStruct(ut.shape, BF),
        compiler_params=params(),
        cost_estimate=pl.CostEstimate(flops=2 * 336 * 512 * 512, bytes_accessed=1000000, transcendentals=0),
    )(own, ut)


def weight_kernel(count, u_ref, *refs):
    rows = jnp.concatenate([ref[...] for ref in refs[:count]], axis=0)
    refs[-1][...] = jnp.dot(u_ref[...], rows, preferred_element_type=F32).astype(BF)


def weight_grad(u, blocks, width, first, columns, block, base=None):
    hidden = u.shape[0]
    rows = blocks[0][0].shape[0]
    start = first // block
    specs = [pl.BlockSpec(u.shape, lambda i: (0, 0))]
    for _, at in blocks:
        specs.append(pl.BlockSpec((rows, block), lambda i, at=at: (0, at // block + i)))
    operands = [u, *[value for value, _ in blocks]]
    aliases = {}
    if base is not None:
        specs.append(pl.BlockSpec(memory_space=pl.ANY))
        operands.append(base)
        aliases = {len(operands) - 1: 0}
    return pl.pallas_call(
        functools.partial(weight_kernel, len(blocks)),
        grid=(columns // block,),
        in_specs=specs,
        out_specs=pl.BlockSpec((hidden, block), lambda i: (0, start + i)),
        out_shape=jax.ShapeDtypeStruct((hidden, width), BF),
        input_output_aliases=aliases,
        compiler_params=params(),
        cost_estimate=pl.CostEstimate(
            flops=2 * hidden * 512 * columns, bytes_accessed=2 * (512 + hidden) * columns, transcendentals=0
        ),
    )(*operands)


def swap(value, axis):
    return lax.ppermute(value, axis, [(0, 1), (1, 0)])


def cross(value, mask):
    return lax.ppermute(value, "zl", [(i, i ^ mask) for i in range(4)])


def body(tokens, routes, up_weight, gate_pre, grad_hidden):
    place = {name: lax.axis_index(name).astype(I32) for name in AXES}
    core, zh, zl, yi = place["c"], place["zh"], place["zl"], place["yi"]
    own_arg = (yi * 16 + zl * 4 + core * 2)[None]
    at_arg = jnp.stack([zh, zl, core])
    home_arg = (place["x"] * 2 + place["yp"])[None]
    weight_t = jnp.swapaxes(up_weight, 1, 2)[0]
    hidden, width = weight_t.shape
    half = width // 2

    rows = placed_rows(tokens, routes.T)
    rows, weight_t = lax.optimization_barrier((rows, weight_t))
    arrived = lax.all_to_all(
        rows.reshape(16, 16, FOLD + EXTRA), FAR, split_axis=0, concat_axis=0, tiled=True
    ).reshape(256, FOLD + EXTRA)

    give = other_half(core[None], weight_t)
    other_t = swap(give, "c")
    ut, u = gated(jnp.swapaxes(gate_pre, 1, 2)[0], jnp.swapaxes(grad_hidden, 1, 2)[0])
    other_u = swap(u, "c")
    terms = terms_of(core[None], u, other_u, weight_t, other_t)
    back = lax.all_to_all(
        terms.reshape(16, 32, half), PLANE, split_axis=0, concat_axis=0, tiled=True
    ).reshape(512, half)

    two = unfold(home_arg, arrived, width)
    run = jnp.concatenate([two] + [cross(two, k) for k in (1, 2, 3)], axis=0)
    pairs = [swap(run[:, :half], "yi"), swap(run[:, half:width], "yi")]
    u_rows = ordered(own_arg, ut)
    run_routes = run[:, width:]
    choice = chooser(at_arg, run_routes, swap(run_routes, "c"))
    other_run = swap(run, "c")

    sums = combined(choice, back)
    parts = lax.all_to_all(
        sums.reshape(8, 2 * PAD, half), RING, split_axis=0, concat_axis=0, tiled=True
    )
    total = jnp.sum(parts.astype(F32), axis=0).astype(BF)
    mine, other = total[:PAD], swap(total[PAD:], "c")
    left, right = jnp.where(core == 0, mine, other), jnp.where(core == 0, other, mine)
    grad_rows = jnp.concatenate([left, right], axis=1)[:TOK]

    def part(index, pair, base):
        at = index * half
        rows = [(run, at), (pair, 0), (other_run, at), (swap(pair, "c"), 0)]
        return weight_grad(u_rows, rows, width, at, half, 1024, base)

    grad = part(0, lax.optimization_barrier((pairs[0], sums))[0], None)
    pair, grad = lax.optimization_barrier((pairs[1], grad))
    grad = part(1, pair, grad)
    return (grad_rows, jnp.swapaxes(grad[None], 1, 2))


def solution(mesh):
    fine = Mesh(mesh.devices.reshape(SIZES), AXES)
    part, column = AXES[:4], AXES[4:]
    in_specs = (
        P(AXES, None),
        P(AXES, None),
        P(part, None, column),
        P(part, None, column),
        P(part, None, column),
    )
    out_specs = (P(AXES, None), P(part, None, column))
    return jax.shard_map(body, mesh=fine, in_specs=in_specs, out_specs=out_specs, check_vma=False)
```

time: 161 us -> 135 us (0.84)
  the two profiles are of different devices: /device:TPU:61 before, /device:TPU:1 now
where the time goes in v4:
time: 135 us; the launch traced here: 134 us
  waiting for transfers between devices  59.2 us (44%)
  starting transfers between devices  36.1 us (27%)
  Pallas kernels  27.9 us (21%)
  local copies, waits for them, and re-layouts  7.18 us (5%)
  other arithmetic  2.75 us (2%)
    ppermute x3, waiting for transfers between devices, cross(): return lax.ppermute(value, 'zl', [(i, i ^ mask) for i in range(4)])  33.4 us
    all_to_all x1, waiting for transfers between devices, body(): lax.all_to_all(sums.reshape(8, 2 * PAD, half), RING, split_axis=0, concat...  13.4 us
    all_to_all x1, starting transfers between devices, body(): lax.all_to_all(rows.reshape(16, 16, FOLD + EXTRA), FAR, split_axis=0, con...  11.6 us
    ppermute x9, waiting for transfers between devices, swap(): return lax.ppermute(value, axis, [(0, 1), (1, 0)])  11 us
    ppermute x9, starting transfers between devices, swap(): return lax.ppermute(value, axis, [(0, 1), (1, 0)])  8.53 us
    pallas_call x2, Pallas kernels, weight_grad(): pl.pallas_call(functools.partial(weight_kernel, len(blocks)), grid=(colum...  8.38 us
    ppermute x3, starting transfers between devices, cross(): return lax.ppermute(value, 'zl', [(i, i ^ mask) for i in range(4)])  5.6 us
    pallas_call x1, Pallas kernels, terms_of(): pl.pallas_call(terms_kernel, grid_spec=pltpu.PrefetchScalarGridSpec(num_s...  5.43 us
  transfers between devices with their start and end apart: 15, of which 8 were waited for; matrix products, arithmetic and copies ran while one was open for 4% of the time, Pallas kernels for 13%

profile of v4, /device:TPU:1, one launch (start us, length us, event | category | flops | bytes accessed | tf_op | source)
XLA Modules:
  0.0 133.9 jit_solution(17788613980619632187)
XLA Ops:
  0.6 3.0 %shard_map.68 = bf16[256,896]{1,0:T(8,128)(2,1)} custom-call(bf16[6,6144]{1,0:T(8,128)(2,1)} %tokens_ref.1, s32[4,6]{1,0:T(4,128)} %bitcast.30), custom_call_target="tpu_custom_call" | custom-call | flops 1000000 | bytes 500000 | tf_op jit(solution)/shard_map/pallas_call | solution.py:137
  3.7 3.7 %shard_map.72 = bf16[336,3072]{1,0:T(8,128)(2,1)} custom-call(s32[1]{0:T(128)} %bitcast.2.core_ref, bf16[336,6144]{1,0:T(8,128)(2,1)} %bitcast.23), custom_call_target="tpu_custom_call" | custom-call | bytes 4200000 | tf_op jit(solution)/shard_map/pallas_call | solution.py:61
  7.4 3.2 %collective-permute-start.5 = (bf16[336,3072]{1,0:T(8,128)(2,1)}, bf16[336,3072]{1,0:T(8,128)(2,1)S(1)}, u32[]{:S(2)}, u32[]{:S(2)}) collective-permute-start(bf16[336,3072]{1,0:T(8,128)(2,1)} %shard_map.72), channel_id=1, source_target_pairs={{0,1},{1,0},{2,3},{3,2},{4,5},{5,4},{6,7},{7,6},{8,9},{9,8},{10,11... | collective-permute-start | bytes 6193160 | tf_op jit(solution)/shard_map/ppermute | solution.py:267
  10.6 11.6 %all-to-all-start = ((bf16[16,16,896]{2,1,0:T(8,128)(2,1)}), bf16[16,16,896]{2,1,0:T(8,128)(2,1)S(1)}, u32[]{:S(2)}, u32[]{:S(2)}) async-start(bf16[16,16,896]{2,1,0:T(8,128)(2,1)} %bitcast.7), calls=%async_computation | async-start | bytes 917504 | tf_op jit(solution)/shard_map/all_to_all | solution.py:286
  22.3 2.2 %shard_map.71 = (bf16[336,512]{1,0:T(8,128)(2,1)}, bf16[512,336]{1,0:T(8,128)(2,1)}) custom-call(bf16[336,512]{1,0:T(8,128)(2,1)} %bitcast.28, bf16[336,512]{1,0:T(8,128)(2,1)} %bitcast.29), custom_call_target="tpu_custom_call" | custom-call | flops 1000000 | bytes 1400000 | tf_op jit(solution)/shard_map/pallas_call | solution.py:42
  24.5 0.3 collective-permute-start.4
  24.8 1.6 %collective-permute-done.4.v_ref = bf16[512,336]{1,0:T(8,128)(2,1)S(1)} collective-permute-done((bf16[512,336]{1,0:T(8,128)(2,1)}, bf16[512,336]{1,0:T(8,128)(2,1)S(1)}, u32[]{:S(2)}, u32[]{:S(2)}) %collective-permute-start.4) | collective-permute-done | bytes 344096 | tf_op jit(solution)/shard_map/ppermute | solution.py:267
  26.4 0.0 collective-permute-done.5.x_ref
  26.4 2.2 %copy-done = bf16[1,6144,336]{1,2,0:T(8,128)(2,1)S(1)} copy-done((bf16[1,6144,336]{1,2,0:T(8,128)(2,1)S(1)}, bf16[1,6144,336]{1,2,0:T(8,128)(2,1)}, u32[]{:S(2)}) %copy-start) | copy-done | bytes 4128792
  28.6 1.0 copy-done.2
  29.6 5.4 %shard_map.73 = bf16[16,2,16,3072]{3,2,1,0:T(8,128)(2,1)} custom-call(s32[1]{0:T(128)} %bitcast.2.core_ref, bf16[512,336]{1,0:T(8,128)(2,1)S(1)} %copy-done.2, bf16[512,336]{1,0:T(8,128)(2,1)S(1)} %collective-permute-done.4.v_ref, bf16[336,6144]{1,0:T(8,128)(2,1)S(1)} %bitcast.24, bf16[336,3072]{1,0:T(8,128)(2,1)S(1)} %collective-permute-done.5.x_ref), custom_call_target="tpu_custom_call" | custom-call | flops 2113929216 | bytes 8000000 | tf_op jit(solution)/shard_map/pallas_call | solution.py:88
  35.0 1.5 %all-to-all-done = bf16[16,16,896]{2,1,0:T(8,128)(2,1)S(1)} async-done(((bf16[16,16,896]{2,1,0:T(8,128)(2,1)}), bf16[16,16,896]{2,1,0:T(8,128)(2,1)S(1)}, u32[]{:S(2)}, u32[]{:S(2)}) %all-to-all-start) | async-done | bytes 458784 | tf_op jit(solution)/shard_map/all_to_all | solution.py:286
  36.5 5.4 %all-to-all-start.1 = ((bf16[16,32,3072]{2,1,0:T(8,128)(2,1)}), bf16[16,32,3072]{2,1,0:T(8,128)(2,1)}, u32[]{:S(2)}, u32[]{:S(2)}) async-start(bf16[16,32,3072]{2,1,0:T(8,128)(2,1)} %bitcast.13), calls=%async_computation.1 | async-start | bytes 6291456 | tf_op jit(solution)/shard_map/all_to_all | solution.py:295
  41.9 0.7 shard_map.69
  42.6 1.7 %collective-permute-start.2 = (bf16[32,6272]{1,0:T(8,128)(2,1)S(1)}, bf16[32,6272]{1,0:T(8,128)(2,1)S(1)}, u32[]{:S(2)}, u32[]{:S(2)}) collective-permute-start(bf16[32,6272]{1,0:T(8,128)(2,1)S(1)} %shard_map.69), channel_id=1, source_target_pairs={{0,6},{2,4},{4,2},{6,0},{1,7},{3,5},{5,3},{7,1},{8,14},{10,12},{12... | collective-permute-start | bytes 1204232 | tf_op jit(solution)/shard_map/ppermute | solution.py:271
  44.3 3.9 %collective-permute-start.1 = (bf16[32,6272]{1,0:T(8,128)(2,1)S(1)}, bf16[32,6272]{1,0:T(8,128)(2,1)S(1)}, u32[]{:S(2)}, u32[]{:S(2)}) collective-permute-start(bf16[32,6272]{1,0:T(8,128)(2,1)S(1)} %shard_map.69), channel_id=1, source_target_pairs={{0,4},{2,6},{4,0},{6,2},{1,5},{3,7},{5,1},{7,3},{8,12},{10,14},{12... | collective-permute-start | bytes 1204232 | tf_op jit(solution)/shard_map/ppermute | solution.py:271
  48.2 0.0 collective-permute-start
  48.2 4.3 %collective-permute-done.2 = bf16[32,6272]{1,0:T(8,128)(2,1)S(1)} collective-permute-done((bf16[32,6272]{1,0:T(8,128)(2,1)S(1)}, bf16[32,6272]{1,0:T(8,128)(2,1)S(1)}, u32[]{:S(2)}, u32[]{:S(2)}) %collective-permute-start.2) | collective-permute-done | bytes 401440 | tf_op jit(solution)/shard_map/ppermute | solution.py:271
  52.4 29.1 %collective-permute-done.1 = bf16[32,6272]{1,0:T(8,128)(2,1)S(1)} collective-permute-done((bf16[32,6272]{1,0:T(8,128)(2,1)S(1)}, bf16[32,6272]{1,0:T(8,128)(2,1)S(1)}, u32[]{:S(2)}, u32[]{:S(2)}) %collective-permute-start.1) | collective-permute-done | bytes 401440 | tf_op jit(solution)/shard_map/ppermute | solution.py:271
  81.6 0.0 collective-permute-done
  81.6 0.1 pad_maximum_fusion.refs_0_
  81.7 0.5 collective-permute-start.9
  82.2 1.4 %fusion = (bf16[128,3072]{1,0:T(8,128)(2,1)}, bf16[128,3072]{1,0:T(8,128)(2,1)}) fusion(bf16[128,6272]{1,0:T(8,128)(2,1)S(1)} %pad_maximum_fusion.refs_0_), kind=kLoop, calls=%fused_computation.5 | loop fusion | bytes 3145728 | tf_op jit(solution)/shard_map/slice | solution.py:301
  83.5 1.3 collective-permute-start.8
  84.8 0.4 collective-permute-start.3
  85.3 0.1 pad_add_fusion.at_ref
  85.3 0.8 collective-permute-done.3.other_ref
  86.1 1.0 shard_map.70.choice_ref
  87.2 3.1 %shard_map.74 = bf16[128,3072]{1,0:T(8,128)(2,1)S(1)} custom-call(bf16[128,512]{1,0:T(8,128)(2,1)S(1)} %shard_map.70.choice_ref, bf16[512,3072]{1,0:T(8,128)(2,1)} %bitcast.14.back_ref), custom_call_target="tpu_custom_call" | custom-call | flops 402653184 | bytes 4000000 | tf_op jit(solution)/shard_map/pallas_call | solution.py:202
  90.3 0.0 copy-start.1
  90.3 0.9 copy-done.1
  91.2 5.0 %all-to-all-start.2 = ((bf16[8,16,3072]{2,1,0:T(8,128)(2,1)}), bf16[8,16,3072]{2,1,0:T(8,128)(2,1)}, u32[]{:S(2)}, u32[]{:S(2)}) async-start(bf16[8,16,3072]{2,1,0:T(8,128)(2,1)} %bitcast.25), calls=%async_computation.2 | async-start | bytes 1572864 | tf_op jit(solution)/shard_map/all_to_all | solution.py:308
  96.1 6.7 %collective-permute-done.8.refs_1_ = bf16[128,3072]{1,0:T(8,128)(2,1)} collective-permute-done((bf16[128,3072]{1,0:T(8,128)(2,1)}, bf16[128,3072]{1,0:T(8,128)(2,1)}, u32[]{:S(2)}, u32[]{:S(2)}) %collective-permute-start.8) | collective-permute-done | bytes 786464 | tf_op jit(solution)/shard_map/ppermute | solution.py:267
  102.8 0.9 collective-permute-start.10
  103.8 1.3 collective-permute-start.7
  105.1 1.0 copy-done.3
  106.1 0.4 shard_map.75.u_ref
  106.5 13.4 %all-to-all-done.2 = bf16[8,16,3072]{2,1,0:T(8,128)(2,1)} async-done(((bf16[8,16,3072]{2,1,0:T(8,128)(2,1)}), bf16[8,16,3072]{2,1,0:T(8,128)(2,1)}, u32[]{:S(2)}, u32[]{:S(2)}) %all-to-all-start.2) | async-done | bytes 786464 | tf_op jit(solution)/shard_map/all_to_all | solution.py:308
  119.8 1.9 %reduce_sum.12 = bf16[16,3072]{1,0:T(8,128)(2,1)} reduce(bf16[8,16,3072]{2,1,0:T(8,128)(2,1)} %all-to-all-done.2, bf16[]{:T(256)} %constant.31.clone.1), dimensions={0}, to_apply=%region_0.0 | reduce | flops 344064 | bytes 884738 | tf_op jit(solution)/shard_map/reduce_sum | solution.py:311
  121.7 0.8 slice.26
  122.5 0.5 collective-permute-start.6
  123.0 0.0 collective-permute-done.9.refs_2_
  123.0 4.3 %shard_map.76.refs_4_ = bf16[336,6144]{1,0:T(8,128)(2,1)} custom-call(bf16[336,512]{1,0:T(8,128)(2,1)S(1)} %shard_map.75.u_ref, bf16[128,6272]{1,0:T(8,128)(2,1)S(1)} %pad_maximum_fusion.refs_0_, bf16[128,3072]{1,0:T(8,128)(2,1)} %collective-permute-done.8.refs_1_, bf16[128,6272]{1,0:T(8,128)(2,1)S(1)} %collective-permute-done.9.refs_2_, ...), custom_call_target="tpu_custom_call" | custom-call | flops 1056964608 | bytes 5210112 | tf_op jit(solution)/shard_map/pallas_call | solution.py:252
  127.3 0.0 collective-permute-start.11
  127.3 0.0 collective-permute-done.6
  127.4 0.6 pad_maximum_fusion.1
  128.0 1.8 %collective-permute-done.11.refs_3_ = bf16[128,3072]{1,0:T(8,128)(2,1)S(1)} collective-permute-done((bf16[128,3072]{1,0:T(8,128)(2,1)}, bf16[128,3072]{1,0:T(8,128)(2,1)S(1)}, u32[]{:S(2)}, u32[]{:S(2)}) %collective-permute-start.11) | collective-permute-done | bytes 786464 | tf_op jit(solution)/shard_map/ppermute | solution.py:267
  129.8 4.1 %shard_map.77 = bf16[336,6144]{1,0:T(8,128)(2,1)} custom-call(bf16[336,512]{1,0:T(8,128)(2,1)S(1)} %shard_map.75.u_ref, bf16[128,6272]{1,0:T(8,128)(2,1)S(1)} %pad_maximum_fusion.refs_0_, bf16[128,3072]{1,0:T(8,128)(2,1)} %collective-permute-done.7.refs_1_, bf16[128,6272]{1,0:T(8,128)(2,1)S(1)} %collective-permute-done.9.refs_2_, ...), custom_call_target="tpu_custom_call", output_to_operand_aliasing={{}: (5, {})} | custom-call | flops 1056964608 | bytes 5210112 | tf_op jit(solution)/shard_map/pallas_call | solution.py:252
  (10 shorter events, 0.0 us)
Async XLA Ops:
  7.4 19.0 %collective-permute-start.5 = (bf16[336,3072]{1,0:T(8,128)(2,1)}, bf16[336,3072]{1,0:T(8,128)(2,1)S(1)}, u32[]{:S(2)}, u32[]{:S(2)}) collective-permute-start(bf16[336,3072]{1,0:T(8,128)(2,1)} %shard_map.72), channel_id=1, source_target_pairs={{0,1},{1,0},{2,3},{3,2},{4,5},{5,4},{6,7},{7,6},{8,9},{9,8},{10,11... | collective-permute-start | bytes 6193160 | tf_op jit(solution)/shard_map/ppermute | solution.py:267
  10.6 25.9 %all-to-all-start = ((bf16[16,16,896]{2,1,0:T(8,128)(2,1)}), bf16[16,16,896]{2,1,0:T(8,128)(2,1)S(1)}, u32[]{:S(2)}, u32[]{:S(2)}) async-start(bf16[16,16,896]{2,1,0:T(8,128)(2,1)} %bitcast.7), calls=%async_computation | async-start | bytes 917504 | tf_op jit(solution)/shard_map/all_to_all | solution.py:286
  24.5 1.9 %collective-permute-start.4 = (bf16[512,336]{1,0:T(8,128)(2,1)}, bf16[512,336]{1,0:T(8,128)(2,1)S(1)}, u32[]{:S(2)}, u32[]{:S(2)}) collective-permute-start(bf16[512,336]{1,0:T(8,128)(2,1)} %get-tuple-element.10.u_ref), channel_id=1, source_target_pairs={{0,1},{1,0},{2,3},{3,2},{4,5},{5,4},{6,7},{7,6},{8,9},{9,8},{10,11... | collective-permute-start | bytes 1032200 | tf_op jit(solution)/shard_map/ppermute | solution.py:267
  26.4 2.2 %copy-start = (bf16[1,6144,336]{1,2,0:T(8,128)(2,1)S(1)}, bf16[1,6144,336]{1,2,0:T(8,128)(2,1)}, u32[]{:S(2)}) copy-start(bf16[1,6144,336]{1,2,0:T(8,128)(2,1)} %param.7) | copy-start | bytes 12386308
  28.6 1.0 copy-start.2
  36.5 50.6 %all-to-all-start.1 = ((bf16[16,32,3072]{2,1,0:T(8,128)(2,1)}), bf16[16,32,3072]{2,1,0:T(8,128)(2,1)}, u32[]{:S(2)}, u32[]{:S(2)}) async-start(bf16[16,32,3072]{2,1,0:T(8,128)(2,1)} %bitcast.13), calls=%async_computation.1 | async-start | bytes 6291456 | tf_op jit(solution)/shard_map/all_to_all | solution.py:295
  42.6 9.9 %collective-permute-start.2 = (bf16[32,6272]{1,0:T(8,128)(2,1)S(1)}, bf16[32,6272]{1,0:T(8,128)(2,1)S(1)}, u32[]{:S(2)}, u32[]{:S(2)}) collective-permute-start(bf16[32,6272]{1,0:T(8,128)(2,1)S(1)} %shard_map.69), channel_id=1, source_target_pairs={{0,6},{2,4},{4,2},{6,0},{1,7},{3,5},{5,3},{7,1},{8,14},{10,12},{12... | collective-permute-start | bytes 1204232 | tf_op jit(solution)/shard_map/ppermute | solution.py:271
  44.3 37.3 %collective-permute-start.1 = (bf16[32,6272]{1,0:T(8,128)(2,1)S(1)}, bf16[32,6272]{1,0:T(8,128)(2,1)S(1)}, u32[]{:S(2)}, u32[]{:S(2)}) collective-permute-start(bf16[32,6272]{1,0:T(8,128)(2,1)S(1)} %shard_map.69), channel_id=1, source_target_pairs={{0,4},{2,6},{4,0},{6,2},{1,5},{3,7},{5,1},{7,3},{8,12},{10,14},{12... | collective-permute-start | bytes 1204232 | tf_op jit(solution)/shard_map/ppermute | solution.py:271
  48.2 33.4 %collective-permute-start = (bf16[32,6272]{1,0:T(8,128)(2,1)S(1)}, bf16[32,6272]{1,0:T(8,128)(2,1)S(1)}, u32[]{:S(2)}, u32[]{:S(2)}) collective-permute-start(bf16[32,6272]{1,0:T(8,128)(2,1)S(1)} %shard_map.69), channel_id=1, source_target_pairs={{0,2},{2,0},{4,6},{6,4},{1,3},{3,1},{5,7},{7,5},{8,10},{10,8},{12,... | collective-permute-start | bytes 1204232 | tf_op jit(solution)/shard_map/ppermute | solution.py:271
  81.7 41.3 %collective-permute-start.9 = (bf16[128,6272]{1,0:T(8,128)(2,1)S(1)}, bf16[128,6272]{1,0:T(8,128)(2,1)S(1)}, u32[]{:S(2)}, u32[]{:S(2)}) collective-permute-start(bf16[128,6272]{1,0:T(8,128)(2,1)S(1)} %pad_maximum_fusion.refs_0_), channel_id=1, source_target_pairs={{0,1},{1,0},{2,3},{3,2},{4,5},{5,4},{6,7},{7,6},{8,9},{9,8},{10,11... | collective-permute-start | bytes 4816904 | tf_op jit(solution)/shard_map/ppermute | solution.py:267
  83.5 19.3 %collective-permute-start.8 = (bf16[128,3072]{1,0:T(8,128)(2,1)}, bf16[128,3072]{1,0:T(8,128)(2,1)}, u32[]{:S(2)}, u32[]{:S(2)}) collective-permute-start(bf16[128,3072]{1,0:T(8,128)(2,1)} %get-tuple-element.16), channel_id=1, source_target_pairs={{0,8},{8,0},{1,9},{9,1},{2,10},{10,2},{3,11},{11,3},{4,12},{12,4},... | collective-permute-start | bytes 2359304 | tf_op jit(solution)/shard_map/ppermute | solution.py:267
  84.8 1.3 collective-permute-start.3
  90.3 0.9 copy-start.1
  91.2 28.6 %all-to-all-start.2 = ((bf16[8,16,3072]{2,1,0:T(8,128)(2,1)}), bf16[8,16,3072]{2,1,0:T(8,128)(2,1)}, u32[]{:S(2)}, u32[]{:S(2)}) async-start(bf16[8,16,3072]{2,1,0:T(8,128)(2,1)} %bitcast.25), calls=%async_computation.2 | async-start | bytes 1572864 | tf_op jit(solution)/shard_map/all_to_all | solution.py:308
  102.8 20.2 %collective-permute-start.10 = (bf16[128,3072]{1,0:T(8,128)(2,1)}, bf16[128,3072]{1,0:T(8,128)(2,1)}, u32[]{:S(2)}, u32[]{:S(2)}) collective-permute-start(bf16[128,3072]{1,0:T(8,128)(2,1)} %collective-permute-done.8.refs_1_), channel_id=1, source_target_pairs={{0,1},{1,0},{2,3},{3,2},{4,5},{5,4},{6,7},{7,6},{8,9},{9,8},{10,11... | collective-permute-start | bytes 2359304 | tf_op jit(solution)/shard_map/ppermute | solution.py:267
  103.8 23.5 %collective-permute-start.7 = (bf16[128,3072]{1,0:T(8,128)(2,1)}, bf16[128,3072]{1,0:T(8,128)(2,1)}, u32[]{:S(2)}, u32[]{:S(2)}) collective-permute-start(bf16[128,3072]{1,0:T(8,128)(2,1)} %get-tuple-element.17), channel_id=1, source_target_pairs={{0,8},{8,0},{1,9},{9,1},{2,10},{10,2},{3,11},{11,3},{4,12},{12,4},... | collective-permute-start | bytes 2359304 | tf_op jit(solution)/shard_map/ppermute | solution.py:267
  105.1 1.0 copy-start.3
  122.5 4.8 %copy-start.4 = (bf16[16,3072]{1,0:T(8,128)(2,1)S(1)}, bf16[16,3072]{1,0:T(8,128)(2,1)}, u32[]{:S(2)}) copy-start(bf16[16,3072]{1,0:T(8,128)(2,1)} %reduce_sum.12) | copy-start | bytes 294916
  122.5 4.8 %collective-permute-start.6 = (bf16[8,3072]{1,0:T(8,128)(2,1)S(1)}, bf16[8,3072]{1,0:T(8,128)(2,1)S(1)}, u32[]{:S(2)}, u32[]{:S(2)}) collective-permute-start(bf16[8,3072]{1,0:T(8,128)(2,1)S(1)} %slice.26), channel_id=1, source_target_pairs={{0,1},{1,0},{2,3},{3,2},{4,5},{5,4},{6,7},{7,6},{8,9},{9,8},{10,11... | collective-permute-start | bytes 147464 | tf_op jit(solution)/shard_map/ppermute | solution.py:267
  127.3 2.5 %collective-permute-start.11 = (bf16[128,3072]{1,0:T(8,128)(2,1)}, bf16[128,3072]{1,0:T(8,128)(2,1)S(1)}, u32[]{:S(2)}, u32[]{:S(2)}) collective-permute-start(bf16[128,3072]{1,0:T(8,128)(2,1)} %collective-permute-done.7.refs_1_), channel_id=1, source_target_pairs={{0,1},{1,0},{2,3},{3,2},{4,5},{5,4},{6,7},{7,6},{8,9},{9,8},{10,11... | collective-permute-start | bytes 2359304 | tf_op jit(solution)/shard_map/ppermute | solution.py:267

commit v5 on v4

--- a/solution.py
+++ b/solution.py
@@ -19,6 +19,7 @@
 FOLD = 768
 EXTRA = 128
 MIB = 1 << 20
+SMALL = pl.CostEstimate(flops=1000, bytes_accessed=1000, transcendentals=0)
 BF, F32, I32 = jnp.bfloat16, jnp.float32, jnp.int32
 
 
@@ -83,7 +84,7 @@
 def terms_of(core, u, v, weight_t, other_t):
     rows, hidden = u.shape
     half = other_t.shape[1]
-    block = 512
+    block = 1024
     steps = half // block
     return pl.pallas_call(
         terms_kernel,
@@ -123,11 +124,11 @@
     lower = jnp.where(iota((PAD, PAD), 0) > iota((PAD, PAD), 1), 1.0, 0.0)
     before = jnp.dot(lower, named, preferred_element_type=F32)
     chosen = jnp.where(before == (column // 8 % 2).astype(F32), named, 0.0)
-    total = jnp.zeros((256, FOLD), F32)
-    for fold in range(width // FOLD):
-        pick = jnp.where(column % 8 == fold, chosen, 0.0).T.astype(BF)
-        piece = held_ref[:, fold * FOLD : fold * FOLD + FOLD].astype(BF)
-        total += jnp.dot(pick, piece, preferred_element_type=F32)
+    folds = range(width // FOLD)
+    pick = jnp.concatenate([jnp.where(column % 8 == fold, chosen, 0.0) for fold in folds], axis=0)
+    pieces = [held_ref[:, fold * FOLD : fold * FOLD + FOLD] for fold in folds]
+    pieces = jnp.concatenate(pieces, axis=0).astype(BF)
+    total = jnp.dot(pick.T.astype(BF), pieces, preferred_element_type=F32)
     out_ref[:, :FOLD] = total.astype(BF)
     spread = jnp.where(iota((256, PAD), 0) % PAD == iota((256, PAD), 1), 1.0, 0.0).astype(BF)
     out_ref[:, FOLD:] = jnp.dot(spread, routes.astype(BF), preferred_element_type=F32).astype(BF)
@@ -165,11 +166,12 @@
     )(at, rows)
 
 
-def choose_kernel(at_ref, mine_ref, other_ref, out_ref):
+def choose_kernel(at_ref, *refs):
+    out_ref = refs[-1]
     shape = (8 * 2 * PAD, 512)
     row, column = iota(shape, 0), iota(shape, 1)
     expert = at_ref[0] * 8 + column // 64
-    routes = jnp.concatenate([mine_ref[...], other_ref[...]], axis=0)
+    routes = jnp.concatenate([ref[...] for ref in refs[:-1]], axis=0)
     r, s = iota((128, 256), 0), iota((128, 256), 1)
     came = (r // 8) % 2 * 128 + jnp.bitwise_xor((r // 16) % 4, at_ref[1]) * 32 + r // 64 * 8 + r % 8
     move = jnp.where(came == s, 1.0, 0.0).astype(BF)
@@ -179,38 +181,81 @@
     before = jnp.dot(lower.astype(BF), named.astype(BF), preferred_element_type=F32)
     device = row // 16 * 2 + jnp.bitwise_xor((row // 8) % 2, at_ref[2])
     fits = (before == (column % 2).astype(F32)) & (device == (column // 2) % 16)
-    out_ref[...] = jnp.where(fits, named, 0.0).astype(BF)
-
-
-def chooser(at, mine, other):
+    chosen = jnp.where(fits, named, 0.0).astype(BF)
+    r, s = iota((192, 128), 0), iota((192, 128), 1)
+    late = r // 64
+    token = r % 8 + jnp.where(late == 0, 0, 12 - 4 * late)
+    real = (late == 0) | ((token >= 8) & (token < 12))
+    place = r % 64 // 8 * 16 + token // TOK * PAD + token % TOK
+    move = jnp.where((place == s) & real, 1.0, 0.0).astype(BF)
+    out_ref[...] = jnp.dot(move, chosen, preferred_element_type=F32).astype(BF)
+
+
+def chooser(at, *runs):
+    last = runs[0].shape[1] // EXTRA - 1
     return pl.pallas_call(
         choose_kernel,
-        in_specs=[pl.BlockSpec(memory_space=pltpu.SMEM)] + [pl.BlockSpec(memory_space=pltpu.VMEM)] * 2,
-        out_shape=jax.ShapeDtypeStruct((8 * 2 * PAD, 512), BF),
+        grid=(1,),
+        in_specs=[pl.BlockSpec(memory_space=pltpu.SMEM)]
+        + [pl.BlockSpec((value.shape[0], EXTRA), lambda i: (0, last)) for value in runs],
+        out_specs=pl.BlockSpec((192, 512), lambda i: (0, 0)),
+        out_shape=jax.ShapeDtypeStruct((192, 512), BF),
         compiler_params=params(),
         cost_estimate=pl.CostEstimate(flops=10**6, bytes_accessed=200000, transcendentals=0),
-    )(at, mine, other)
+    )(at, *runs)
 
 
 def combine_kernel(choice_ref, back_ref, out_ref):
-    out_ref[...] = jnp.dot(choice_ref[...], back_ref[...], preferred_element_type=F32).astype(BF)
+    half = back_ref.shape[1]
+    step = half // 4
+    for at in range(0, half // 2, step):
+        low = jnp.dot(choice_ref[...], back_ref[:, at : at + step], preferred_element_type=F32)
+        high = back_ref[:, half // 2 + at : half // 2 + at + step]
+        high = jnp.dot(choice_ref[...], high, preferred_element_type=F32)
+        out_ref[:, at : at + step] = low[:64].astype(BF)
+        out_ref[:, half // 2 + at : half // 2 + at + step] = high[:64].astype(BF)
+        out_ref[:, half + at : half + at + step] = (low[64:128] + high[128:]).astype(BF)
 
 
 def combined(choice, back):
-    rows, width = back.shape
-    block = 1024
+    rows, half = back.shape
     return pl.pallas_call(
         combine_kernel,
-        grid=(width // block,),
-        in_specs=[
-            pl.BlockSpec(choice.shape, lambda i: (0, 0)),
-            pl.BlockSpec((rows, block), lambda i: (0, i)),
-        ],
-        out_specs=pl.BlockSpec((choice.shape[0], block), lambda i: (0, i)),
-        out_shape=jax.ShapeDtypeStruct((choice.shape[0], width), BF),
-        compiler_params=params(),
-        cost_estimate=pl.CostEstimate(flops=2 * 128 * rows * width, bytes_accessed=4000000, transcendentals=0),
+        out_shape=jax.ShapeDtypeStruct((64, half + half // 2), BF),
+        compiler_params=params(),
+        cost_estimate=pl.CostEstimate(flops=2 * 192 * rows * half, bytes_accessed=4000000, transcendentals=0),
     )(choice, back)
+
+
+def total_kernel(parts_ref, mine_ref, other_ref):
+    half = mine_ref.shape[1]
+    total = parts_ref[0].astype(F32)
+    for source in range(1, parts_ref.shape[0]):
+        total += parts_ref[source].astype(F32)
+    total = total.astype(BF)
+    mine_ref[...] = total[:, :half]
+    r, s = iota((PAD, PAD), 0), iota((PAD, PAD), 1)
+
+    def moved(shift, keep, value):
+        move = jnp.where((s == r + shift) & keep, 1.0, 0.0).astype(BF)
+        return jnp.dot(move, value, preferred_element_type=F32)
+
+    first = moved(TOK, r < 2, total[:, :half])
+    second = (r >= 2) & (r < TOK)
+    rest = total[:, half:]
+    rest = jnp.concatenate([moved(-2, second, rest), moved(2, second, rest)], axis=1)
+    other_ref[...] = (first + rest).astype(BF)
+
+
+def totalled(parts):
+    half = parts.shape[2] * 2 // 3
+    like = jax.ShapeDtypeStruct((PAD, half), BF)
+    return pl.pallas_call(
+        total_kernel,
+        out_shape=(like, like),
+        compiler_params=params(),
+        cost_estimate=SMALL,
+    )(parts)
 
 
 def order_kernel(own_ref, ut_ref, out_ref):
@@ -227,7 +272,7 @@
         in_specs=[pl.BlockSpec(memory_space=pltpu.SMEM), pl.BlockSpec(memory_space=pltpu.VMEM)],
         out_shape=jax.ShapeDtypeStruct(ut.shape, BF),
         compiler_params=params(),
-        cost_estimate=pl.CostEstimate(flops=2 * 336 * 512 * 512, bytes_accessed=1000000, transcendentals=0),
+        cost_estimate=SMALL,
     )(own, ut)
 
 
@@ -236,31 +281,21 @@
     refs[-1][...] = jnp.dot(u_ref[...], rows, preferred_element_type=F32).astype(BF)
 
 
-def weight_grad(u, blocks, width, first, columns, block, base=None):
+def weight_grad(u, blocks, width, block):
     hidden = u.shape[0]
-    rows = blocks[0][0].shape[0]
-    start = first // block
     specs = [pl.BlockSpec(u.shape, lambda i: (0, 0))]
-    for _, at in blocks:
-        specs.append(pl.BlockSpec((rows, block), lambda i, at=at: (0, at // block + i)))
-    operands = [u, *[value for value, _ in blocks]]
-    aliases = {}
-    if base is not None:
-        specs.append(pl.BlockSpec(memory_space=pl.ANY))
-        operands.append(base)
-        aliases = {len(operands) - 1: 0}
+    specs += [pl.BlockSpec((value.shape[0], block), lambda i: (0, i)) for value in blocks]
     return pl.pallas_call(
         functools.partial(weight_kernel, len(blocks)),
-        grid=(columns // block,),
+        grid=(width // block,),
         in_specs=specs,
-        out_specs=pl.BlockSpec((hidden, block), lambda i: (0, start + i)),
+        out_specs=pl.BlockSpec((hidden, block), lambda i: (0, i)),
         out_shape=jax.ShapeDtypeStruct((hidden, width), BF),
-        input_output_aliases=aliases,
         compiler_params=params(),
         cost_estimate=pl.CostEstimate(
-            flops=2 * hidden * 512 * columns, bytes_accessed=2 * (512 + hidden) * columns, transcendentals=0
+            flops=2 * hidden * 512 * width, bytes_accessed=2 * (512 + hidden) * width, transcendentals=0
         ),
-    )(*operands)
+    )(u, *blocks)
 
 
 def swap(value, axis):
@@ -298,29 +333,24 @@
 
     two = unfold(home_arg, arrived, width)
     run = jnp.concatenate([two] + [cross(two, k) for k in (1, 2, 3)], axis=0)
-    pairs = [swap(run[:, :half], "yi"), swap(run[:, half:width], "yi")]
+    other_run = swap(run, "c")
+    pair = swap(run, "yi")
     u_rows = ordered(own_arg, ut)
-    run_routes = run[:, width:]
-    choice = chooser(at_arg, run_routes, swap(run_routes, "c"))
-    other_run = swap(run, "c")
+    choice = chooser(at_arg, run, other_run)
 
     sums = combined(choice, back)
     parts = lax.all_to_all(
-        sums.reshape(8, 2 * PAD, half), RING, split_axis=0, concat_axis=0, tiled=True
+        sums.reshape(8, PAD, half + half // 2), RING, split_axis=0, concat_axis=0, tiled=True
     )
-    total = jnp.sum(parts.astype(F32), axis=0).astype(BF)
-    mine, other = total[:PAD], swap(total[PAD:], "c")
+
+    pair = lax.optimization_barrier((pair, sums))[0]
+    rows = [run, pair, other_run, swap(pair, "c")]
+    grad = weight_grad(u_rows, rows, width, 2048)
+
+    mine, other = totalled(parts)
+    other = swap(other, "c")
     left, right = jnp.where(core == 0, mine, other), jnp.where(core == 0, other, mine)
     grad_rows = jnp.concatenate([left, right], axis=1)[:TOK]
-
-    def part(index, pair, base):
-        at = index * half
-        rows = [(run, at), (pair, 0), (other_run, at), (swap(pair, "c"), 0)]
-        return weight_grad(u_rows, rows, width, at, half, 1024, base)
-
-    grad = part(0, lax.optimization_barrier((pairs[0], sums))[0], None)
-    pair, grad = lax.optimization_barrier((pairs[1], grad))
-    grad = part(1, pair, grad)
     return (grad_rows, jnp.swapaxes(grad[None], 1, 2))
 
 

time: 135 us -> 131 us (0.970)
  waiting for transfers between devices: 59.2 us -> 62.7 us
  starting transfers between devices: 36.1 us -> 33.7 us
  Pallas kernels: 27.9 us -> 25.8 us
  local copies, waits for them, and re-layouts: 7.18 us -> 5.57 us
    ppermute x9 -> x6, waiting for transfers between devices: 11 us -> 27.6 us  [swap(): return lax.ppermute(value, axis, [(0, 1), (1, 0)])]
    all_to_all x1, waiting for transfers between devices: 13.4 us -> 0.01 us  [body(): lax.all_to_all(sums.reshape(8, PAD, half + half // 2), RING, split_axis=0...]
    ppermute x9 -> x6, starting transfers between devices: 8.53 us -> 6.26 us  [swap(): return lax.ppermute(value, axis, [(0, 1), (1, 0)])]
    slice x3 -> x0, local copies, waits for them, and re-layouts: 2.16 us -> none  [the longest x1 1.36 us: body(): pairs = [swap(run[:, :half], 'yi'), swap(run[:, half:width], 'yi')]]
    reduce_sum x1 -> x0, other arithmetic: 1.91 us -> none  [body(): total = jnp.sum(parts.astype(F32), axis=0).astype(BF)]
  transfers between devices with their start and end apart: 15 -> 12, of which waited for: 8 -> 7; matrix products, arithmetic and copies ran while one was open for 4% -> 1% of each run, Pallas kernels for 13% -> 11%
where the time goes in v5:
time: 131 us; the launch traced here: 130 us
  waiting for transfers between devices  62.7 us (48%)
  starting transfers between devices  33.7 us (26%)
  Pallas kernels  25.8 us (20%)
  local copies, waits for them, and re-layouts  5.57 us (4%)
  other arithmetic  1.67 us (1%)
    ppermute x3, waiting for transfers between devices, cross(): return lax.ppermute(value, 'zl', [(i, i ^ mask) for i in range(4)])  33.2 us
    ppermute x6, waiting for transfers between devices, swap(): return lax.ppermute(value, axis, [(0, 1), (1, 0)])  27.6 us
    all_to_all x1, starting transfers between devices, body(): lax.all_to_all(rows.reshape(16, 16, FOLD + EXTRA), FAR, split_axis=0, con...  11.6 us
    ppermute x6, starting transfers between devices, swap(): return lax.ppermute(value, axis, [(0, 1), (1, 0)])  6.26 us
    pallas_call x1, Pallas kernels, weight_grad(): pl.pallas_call(functools.partial(weight_kernel, len(blocks)), grid=(width...  5.82 us
    ppermute x3, starting transfers between devices, cross(): return lax.ppermute(value, 'zl', [(i, i ^ mask) for i in range(4)])  5.82 us
    unnamed x10, local copies, waits for them, and re-layouts  5.57 us
    all_to_all x1, starting transfers between devices, body(): lax.all_to_all(terms.reshape(16, 32, half), PLANE, split_axis=0, concat_a...  5.13 us
  transfers between devices with their start and end apart: 12, of which 7 were waited for; matrix products, arithmetic and copies ran while one was open for 1% of the time, Pallas kernels for 11%

profile of v5, /device:TPU:1, one launch (start us, length us, event | category | flops | bytes accessed | tf_op | source)
XLA Modules:
  0.0 130.2 jit_solution(16218535027047312993)
XLA Ops:
  0.6 2.3 %shard_map.68 = bf16[256,896]{1,0:T(8,128)(2,1)} custom-call(bf16[6,6144]{1,0:T(8,128)(2,1)} %tokens_ref.1, s32[4,6]{1,0:T(4,128)} %bitcast.30), custom_call_target="tpu_custom_call" | custom-call | flops 1000000 | bytes 500000 | tf_op jit(solution)/shard_map/pallas_call | solution.py:138
  2.9 3.7 %shard_map.72 = bf16[336,3072]{1,0:T(8,128)(2,1)} custom-call(s32[1]{0:T(128)} %bitcast.2.core_ref, bf16[336,6144]{1,0:T(8,128)(2,1)} %bitcast.23), custom_call_target="tpu_custom_call" | custom-call | bytes 4200000 | tf_op jit(solution)/shard_map/pallas_call | solution.py:62
  6.6 3.2 %collective-permute-start.5 = (bf16[336,3072]{1,0:T(8,128)(2,1)}, bf16[336,3072]{1,0:T(8,128)(2,1)S(1)}, u32[]{:S(2)}, u32[]{:S(2)}) collective-permute-start(bf16[336,3072]{1,0:T(8,128)(2,1)} %shard_map.72), channel_id=1, source_target_pairs={{0,1},{1,0},{2,3},{3,2},{4,5},{5,4},{6,7},{7,6},{8,9},{9,8},{10,11... | collective-permute-start | bytes 6193160 | tf_op jit(solution)/shard_map/ppermute | solution.py:302
  9.8 11.6 %all-to-all-start = ((bf16[16,16,896]{2,1,0:T(8,128)(2,1)}), bf16[16,16,896]{2,1,0:T(8,128)(2,1)S(1)}, u32[]{:S(2)}, u32[]{:S(2)}) async-start(bf16[16,16,896]{2,1,0:T(8,128)(2,1)} %bitcast.7), calls=%async_computation | async-start | bytes 917504 | tf_op jit(solution)/shard_map/all_to_all | solution.py:321
  21.5 2.2 %shard_map.71 = (bf16[336,512]{1,0:T(8,128)(2,1)}, bf16[512,336]{1,0:T(8,128)(2,1)}) custom-call(bf16[336,512]{1,0:T(8,128)(2,1)} %bitcast.28, bf16[336,512]{1,0:T(8,128)(2,1)} %bitcast.29), custom_call_target="tpu_custom_call" | custom-call | flops 1000000 | bytes 1400000 | tf_op jit(solution)/shard_map/pallas_call | solution.py:43
  23.7 0.3 collective-permute-start.4
  23.9 1.6 %collective-permute-done.4.v_ref = bf16[512,336]{1,0:T(8,128)(2,1)S(1)} collective-permute-done((bf16[512,336]{1,0:T(8,128)(2,1)}, bf16[512,336]{1,0:T(8,128)(2,1)S(1)}, u32[]{:S(2)}, u32[]{:S(2)}) %collective-permute-start.4) | collective-permute-done | bytes 344096 | tf_op jit(solution)/shard_map/ppermute | solution.py:302
  25.6 0.0 collective-permute-done.5.x_ref
  25.6 0.0 copy-start
  25.6 2.2 %copy-done = bf16[1,6144,336]{1,2,0:T(8,128)(2,1)S(1)} copy-done((bf16[1,6144,336]{1,2,0:T(8,128)(2,1)S(1)}, bf16[1,6144,336]{1,2,0:T(8,128)(2,1)}, u32[]{:S(2)}) %copy-start) | copy-done | bytes 4128792
  27.8 0.0 copy-start.2
  27.8 1.0 copy-done.2
  28.8 5.0 %shard_map.73 = bf16[16,2,16,3072]{3,2,1,0:T(8,128)(2,1)} custom-call(s32[1]{0:T(128)} %bitcast.2.core_ref, bf16[512,336]{1,0:T(8,128)(2,1)S(1)} %copy-done.2, bf16[512,336]{1,0:T(8,128)(2,1)S(1)} %collective-permute-done.4.v_ref, bf16[336,6144]{1,0:T(8,128)(2,1)S(1)} %bitcast.24, bf16[336,3072]{1,0:T(8,128)(2,1)S(1)} %collective-permute-done.5.x_ref), custom_call_target="tpu_custom_call" | custom-call | flops 2113929216 | bytes 8000000 | tf_op jit(solution)/shard_map/pallas_call | solution.py:89
  33.8 2.0 %all-to-all-done = bf16[16,16,896]{2,1,0:T(8,128)(2,1)S(1)} async-done(((bf16[16,16,896]{2,1,0:T(8,128)(2,1)}), bf16[16,16,896]{2,1,0:T(8,128)(2,1)S(1)}, u32[]{:S(2)}, u32[]{:S(2)}) %all-to-all-start) | async-done | bytes 458784 | tf_op jit(solution)/shard_map/all_to_all | solution.py:321
  35.8 5.1 %all-to-all-start.1 = ((bf16[16,32,3072]{2,1,0:T(8,128)(2,1)}), bf16[16,32,3072]{2,1,0:T(8,128)(2,1)}, u32[]{:S(2)}, u32[]{:S(2)}) async-start(bf16[16,32,3072]{2,1,0:T(8,128)(2,1)} %bitcast.13), calls=%async_computation.1 | async-start | bytes 6291456 | tf_op jit(solution)/shard_map/all_to_all | solution.py:330
  40.9 0.7 shard_map.69
  41.6 1.8 %collective-permute-start.2 = (bf16[32,6272]{1,0:T(8,128)(2,1)S(1)}, bf16[32,6272]{1,0:T(8,128)(2,1)S(1)}, u32[]{:S(2)}, u32[]{:S(2)}) collective-permute-start(bf16[32,6272]{1,0:T(8,128)(2,1)S(1)} %shard_map.69), channel_id=1, source_target_pairs={{0,6},{2,4},{4,2},{6,0},{1,7},{3,5},{5,3},{7,1},{8,14},{10,12},{12... | collective-permute-start | bytes 1204232 | tf_op jit(solution)/shard_map/ppermute | solution.py:306
  43.3 4.1 %collective-permute-start.1 = (bf16[32,6272]{1,0:T(8,128)(2,1)S(1)}, bf16[32,6272]{1,0:T(8,128)(2,1)S(1)}, u32[]{:S(2)}, u32[]{:S(2)}) collective-permute-start(bf16[32,6272]{1,0:T(8,128)(2,1)S(1)} %shard_map.69), channel_id=1, source_target_pairs={{0,4},{2,6},{4,0},{6,2},{1,5},{3,7},{5,1},{7,3},{8,12},{10,14},{12... | collective-permute-start | bytes 1204232 | tf_op jit(solution)/shard_map/ppermute | solution.py:306
  47.4 0.0 collective-permute-start
  47.4 3.8 %collective-permute-done.2 = bf16[32,6272]{1,0:T(8,128)(2,1)S(1)} collective-permute-done((bf16[32,6272]{1,0:T(8,128)(2,1)S(1)}, bf16[32,6272]{1,0:T(8,128)(2,1)S(1)}, u32[]{:S(2)}, u32[]{:S(2)}) %collective-permute-start.2) | collective-permute-done | bytes 401440 | tf_op jit(solution)/shard_map/ppermute | solution.py:306
  51.2 29.3 %collective-permute-done.1 = bf16[32,6272]{1,0:T(8,128)(2,1)S(1)} collective-permute-done((bf16[32,6272]{1,0:T(8,128)(2,1)S(1)}, bf16[32,6272]{1,0:T(8,128)(2,1)S(1)}, u32[]{:S(2)}, u32[]{:S(2)}) %collective-permute-start.1) | collective-permute-done | bytes 401440 | tf_op jit(solution)/shard_map/ppermute | solution.py:306
  80.6 0.0 collective-permute-done
  80.6 0.1 pad_maximum_fusion.refs_0_
  80.7 0.5 collective-permute-start.3
  81.2 1.3 %collective-permute-start.7 = (bf16[128,6272]{1,0:T(8,128)(2,1)S(1)}, bf16[128,6272]{1,0:T(8,128)(2,1)}, u32[]{:S(2)}, u32[]{:S(2)}) collective-permute-start(bf16[128,6272]{1,0:T(8,128)(2,1)S(1)} %pad_maximum_fusion.refs_0_), channel_id=1, source_target_pairs={{0,8},{8,0},{1,9},{9,1},{2,10},{10,2},{3,11},{11,3},{4,12},{12,4},... | collective-permute-start | bytes 4816904 | tf_op jit(solution)/shard_map/ppermute | solution.py:302
  82.5 0.1 pad_add_fusion.at_ref
  82.6 1.7 %collective-permute-done.3.refs_1_.refs_2_ = bf16[128,6272]{1,0:T(8,128)(2,1)S(1)} collective-permute-done((bf16[128,6272]{1,0:T(8,128)(2,1)S(1)}, bf16[128,6272]{1,0:T(8,128)(2,1)S(1)}, u32[]{:S(2)}, u32[]{:S(2)}) %collective-permute-start.3) | collective-permute-done | bytes 1605664 | tf_op jit(solution)/shard_map/ppermute | solution.py:302
  84.3 1.2 shard_map.70.choice_ref
  85.5 0.0 all-to-all-done.1
  85.5 2.7 %shard_map.74 = bf16[64,4608]{1,0:T(8,128)(2,1)S(1)} custom-call(bf16[192,512]{1,0:T(8,128)(2,1)S(1)} %shard_map.70.choice_ref, bf16[512,3072]{1,0:T(8,128)(2,1)} %bitcast.14.back_ref), custom_call_target="tpu_custom_call" | custom-call | flops 603979776 | bytes 4000000 | tf_op jit(solution)/shard_map/pallas_call | solution.py:222
  88.2 0.0 copy-start.1
  88.2 0.8 copy-done.1
  89.0 4.8 %all-to-all-start.2 = ((bf16[8,8,4608]{2,1,0:T(8,128)(2,1)}), bf16[8,8,4608]{2,1,0:T(8,128)(2,1)}, u32[]{:S(2)}, u32[]{:S(2)}) async-start(bf16[8,8,4608]{2,1,0:T(8,128)(2,1)} %bitcast.25), calls=%async_computation.2 | async-start | bytes 1179648 | tf_op jit(solution)/shard_map/all_to_all | solution.py:342
  93.8 24.0 %collective-permute-done.7.refs_1_ = bf16[128,6272]{1,0:T(8,128)(2,1)} collective-permute-done((bf16[128,6272]{1,0:T(8,128)(2,1)S(1)}, bf16[128,6272]{1,0:T(8,128)(2,1)}, u32[]{:S(2)}, u32[]{:S(2)}) %collective-permute-start.7) | collective-permute-done | bytes 1605664 | tf_op jit(solution)/shard_map/ppermute | solution.py:302
  117.8 0.9 collective-permute-start.8
  118.8 0.0 all-to-all-done.2.parts_ref
  118.8 1.9 %shard_map.75 = (bf16[8,3072]{1,0:T(8,128)(2,1)S(1)}, bf16[8,3072]{1,0:T(8,128)(2,1)}) custom-call(bf16[8,8,4608]{2,1,0:T(8,128)(2,1)} %all-to-all-done.2.parts_ref), custom_call_target="tpu_custom_call" | custom-call | flops 1000 | bytes 1000 | tf_op jit(solution)/shard_map/pallas_call | solution.py:253
  120.7 0.0 copy-start.4
  120.7 0.6 copy-done.4
  121.3 0.0 collective-permute-start.6
  121.3 0.0 copy-start.3
  121.3 1.0 copy-done.3
  122.3 0.4 shard_map.76.u_ref
  122.7 0.2 collective-permute-done.6
  122.9 0.8 broadcast_select_fusion.1
  123.7 0.6 pad_maximum_fusion.1
  124.4 0.0 collective-permute-done.8.refs_3_
  124.4 5.8 %shard_map.77 = bf16[336,6144]{1,0:T(8,128)(2,1)} custom-call(bf16[336,512]{1,0:T(8,128)(2,1)S(1)} %shard_map.76.u_ref, bf16[128,6272]{1,0:T(8,128)(2,1)S(1)} %pad_maximum_fusion.refs_0_, bf16[128,6272]{1,0:T(8,128)(2,1)} %collective-permute-done.7.refs_1_, bf16[128,6272]{1,0:T(8,128)(2,1)S(1)} %collective-permute-done.3.refs_1_.refs_2_, ...), custom_call_target="tpu_custom_call" | custom-call | flops 2113929216 | bytes 10420224 | tf_op jit(solution)/shard_map/pallas_call | solution.py:288
Async XLA Ops:
  6.6 19.0 %collective-permute-start.5 = (bf16[336,3072]{1,0:T(8,128)(2,1)}, bf16[336,3072]{1,0:T(8,128)(2,1)S(1)}, u32[]{:S(2)}, u32[]{:S(2)}) collective-permute-start(bf16[336,3072]{1,0:T(8,128)(2,1)} %shard_map.72), channel_id=1, source_target_pairs={{0,1},{1,0},{2,3},{3,2},{4,5},{5,4},{6,7},{7,6},{8,9},{9,8},{10,11... | collective-permute-start | bytes 6193160 | tf_op jit(solution)/shard_map/ppermute | solution.py:302
  9.8 25.9 %all-to-all-start = ((bf16[16,16,896]{2,1,0:T(8,128)(2,1)}), bf16[16,16,896]{2,1,0:T(8,128)(2,1)S(1)}, u32[]{:S(2)}, u32[]{:S(2)}) async-start(bf16[16,16,896]{2,1,0:T(8,128)(2,1)} %bitcast.7), calls=%async_computation | async-start | bytes 917504 | tf_op jit(solution)/shard_map/all_to_all | solution.py:321
  23.7 1.9 %collective-permute-start.4 = (bf16[512,336]{1,0:T(8,128)(2,1)}, bf16[512,336]{1,0:T(8,128)(2,1)S(1)}, u32[]{:S(2)}, u32[]{:S(2)}) collective-permute-start(bf16[512,336]{1,0:T(8,128)(2,1)} %get-tuple-element.10.u_ref), channel_id=1, source_target_pairs={{0,1},{1,0},{2,3},{3,2},{4,5},{5,4},{6,7},{7,6},{8,9},{9,8},{10,11... | collective-permute-start | bytes 1032200 | tf_op jit(solution)/shard_map/ppermute | solution.py:302
  25.6 2.2 %copy-start = (bf16[1,6144,336]{1,2,0:T(8,128)(2,1)S(1)}, bf16[1,6144,336]{1,2,0:T(8,128)(2,1)}, u32[]{:S(2)}) copy-start(bf16[1,6144,336]{1,2,0:T(8,128)(2,1)} %param.7) | copy-start | bytes 12386308
  27.8 1.0 copy-start.2
  35.8 49.7 %all-to-all-start.1 = ((bf16[16,32,3072]{2,1,0:T(8,128)(2,1)}), bf16[16,32,3072]{2,1,0:T(8,128)(2,1)}, u32[]{:S(2)}, u32[]{:S(2)}) async-start(bf16[16,32,3072]{2,1,0:T(8,128)(2,1)} %bitcast.13), calls=%async_computation.1 | async-start | bytes 6291456 | tf_op jit(solution)/shard_map/all_to_all | solution.py:330
  41.6 9.7 %collective-permute-start.2 = (bf16[32,6272]{1,0:T(8,128)(2,1)S(1)}, bf16[32,6272]{1,0:T(8,128)(2,1)S(1)}, u32[]{:S(2)}, u32[]{:S(2)}) collective-permute-start(bf16[32,6272]{1,0:T(8,128)(2,1)S(1)} %shard_map.69), channel_id=1, source_target_pairs={{0,6},{2,4},{4,2},{6,0},{1,7},{3,5},{5,3},{7,1},{8,14},{10,12},{12... | collective-permute-start | bytes 1204232 | tf_op jit(solution)/shard_map/ppermute | solution.py:306
  43.3 37.2 %collective-permute-start.1 = (bf16[32,6272]{1,0:T(8,128)(2,1)S(1)}, bf16[32,6272]{1,0:T(8,128)(2,1)S(1)}, u32[]{:S(2)}, u32[]{:S(2)}) collective-permute-start(bf16[32,6272]{1,0:T(8,128)(2,1)S(1)} %shard_map.69), channel_id=1, source_target_pairs={{0,4},{2,6},{4,0},{6,2},{1,5},{3,7},{5,1},{7,3},{8,12},{10,14},{12... | collective-permute-start | bytes 1204232 | tf_op jit(solution)/shard_map/ppermute | solution.py:306
  47.4 33.2 %collective-permute-start = (bf16[32,6272]{1,0:T(8,128)(2,1)S(1)}, bf16[32,6272]{1,0:T(8,128)(2,1)S(1)}, u32[]{:S(2)}, u32[]{:S(2)}) collective-permute-start(bf16[32,6272]{1,0:T(8,128)(2,1)S(1)} %shard_map.69), channel_id=1, source_target_pairs={{0,2},{2,0},{4,6},{6,4},{1,3},{3,1},{5,7},{7,5},{8,10},{10,8},{12,... | collective-permute-start | bytes 1204232 | tf_op jit(solution)/shard_map/ppermute | solution.py:306
  80.7 3.6 %collective-permute-start.3 = (bf16[128,6272]{1,0:T(8,128)(2,1)S(1)}, bf16[128,6272]{1,0:T(8,128)(2,1)S(1)}, u32[]{:S(2)}, u32[]{:S(2)}) collective-permute-start(bf16[128,6272]{1,0:T(8,128)(2,1)S(1)} %pad_maximum_fusion.refs_0_), channel_id=1, source_target_pairs={{0,1},{1,0},{2,3},{3,2},{4,5},{5,4},{6,7},{7,6},{8,9},{9,8},{10,11... | collective-permute-start | bytes 4816904 | tf_op jit(solution)/shard_map/ppermute | solution.py:302
  81.2 36.7 %collective-permute-start.7 = (bf16[128,6272]{1,0:T(8,128)(2,1)S(1)}, bf16[128,6272]{1,0:T(8,128)(2,1)}, u32[]{:S(2)}, u32[]{:S(2)}) collective-permute-start(bf16[128,6272]{1,0:T(8,128)(2,1)S(1)} %pad_maximum_fusion.refs_0_), channel_id=1, source_target_pairs={{0,8},{8,0},{1,9},{9,1},{2,10},{10,2},{3,11},{11,3},{4,12},{12,4},... | collective-permute-start | bytes 4816904 | tf_op jit(solution)/shard_map/ppermute | solution.py:302
  88.2 0.8 copy-start.1
  89.0 29.8 %all-to-all-start.2 = ((bf16[8,8,4608]{2,1,0:T(8,128)(2,1)}), bf16[8,8,4608]{2,1,0:T(8,128)(2,1)}, u32[]{:S(2)}, u32[]{:S(2)}) async-start(bf16[8,8,4608]{2,1,0:T(8,128)(2,1)} %bitcast.25), calls=%async_computation.2 | async-start | bytes 1179648 | tf_op jit(solution)/shard_map/all_to_all | solution.py:342
  117.8 6.5 %collective-permute-start.8 = (bf16[128,6272]{1,0:T(8,128)(2,1)}, bf16[128,6272]{1,0:T(8,128)(2,1)}, u32[]{:S(2)}, u32[]{:S(2)}) collective-permute-start(bf16[128,6272]{1,0:T(8,128)(2,1)} %collective-permute-done.7.refs_1_), channel_id=1, source_target_pairs={{0,1},{1,0},{2,3},{3,2},{4,5},{5,4},{6,7},{7,6},{8,9},{9,8},{10,11... | collective-permute-start | bytes 4816904 | tf_op jit(solution)/shard_map/ppermute | solution.py:302
  120.7 0.6 copy-start.4
  121.3 1.6 %collective-permute-start.6 = (bf16[8,3072]{1,0:T(8,128)(2,1)}, bf16[8,3072]{1,0:T(8,128)(2,1)}, u32[]{:S(2)}, u32[]{:S(2)}) collective-permute-start(bf16[8,3072]{1,0:T(8,128)(2,1)} %get-tuple-element.13), channel_id=1, source_target_pairs={{0,1},{1,0},{2,3},{3,2},{4,5},{5,4},{6,7},{7,6},{8,9},{9,8},{10,11... | collective-permute-start | bytes 147464 | tf_op jit(solution)/shard_map/ppermute | solution.py:302
  121.3 1.0 copy-start.3

commit v6 on v5

--- a/solution.py
+++ b/solution.py
@@ -144,7 +144,28 @@
     )(tokens, routes)
 
 
-def unfold_kernel(at_ref, rows_ref, out_ref):
+def routes_kernel(at_ref, rows_ref, out_ref):
+    r, s = iota((16, 256), 0), iota((16, 256), 1)
+    move = jnp.where(s == r // 8 * 128 + at_ref[0] * 16 + r % 8, 1.0, 0.0).astype(BF)
+    out_ref[...] = jnp.dot(move, rows_ref[...], preferred_element_type=F32).astype(BF)
+
+
+def own_routes(at, rows):
+    return pl.pallas_call(
+        routes_kernel,
+        grid=(1,),
+        in_specs=[
+            pl.BlockSpec(memory_space=pltpu.SMEM),
+            pl.BlockSpec((rows.shape[0], EXTRA), lambda i: (0, FOLD // EXTRA)),
+        ],
+        out_specs=pl.BlockSpec((16, EXTRA), lambda i: (0, 0)),
+        out_shape=jax.ShapeDtypeStruct((16, EXTRA), BF),
+        compiler_params=params(),
+        cost_estimate=SMALL,
+    )(at, rows)
+
+
+def unfold_kernel(rows_ref, mine_ref, other_ref, out_ref):
     width = out_ref.shape[1] - EXTRA
     rows = rows_ref[...]
     r, s = iota((32, 256), 0), iota((32, 256), 1)
@@ -152,18 +173,16 @@
         move = jnp.where(s == r * 8 + fold, 1.0, 0.0).astype(BF)
         piece = jnp.dot(move, rows[:, :FOLD], preferred_element_type=F32)
         out_ref[:, fold * FOLD : fold * FOLD + FOLD] = piece.astype(BF)
-    move = jnp.where((s == r // 8 * 128 + at_ref[0] * 16 + r % 8) & (r < 16), 1.0, 0.0).astype(BF)
-    out_ref[:, width:] = jnp.dot(move, rows[:, FOLD:], preferred_element_type=F32).astype(BF)
-
-
-def unfold(at, rows, width):
+    out_ref[:, width:] = jnp.concatenate([mine_ref[...], other_ref[...]], axis=0)
+
+
+def unfold(rows, mine, other, width):
     return pl.pallas_call(
         unfold_kernel,
-        in_specs=[pl.BlockSpec(memory_space=pltpu.SMEM), pl.BlockSpec(memory_space=pltpu.VMEM)],
         out_shape=jax.ShapeDtypeStruct((32, width + EXTRA), BF),
         compiler_params=params(),
         cost_estimate=pl.CostEstimate(flops=10**6, bytes_accessed=1000000, transcendentals=0),
-    )(at, rows)
+    )(rows, mine, other)
 
 
 def choose_kernel(at_ref, *refs):
@@ -172,8 +191,8 @@
     row, column = iota(shape, 0), iota(shape, 1)
     expert = at_ref[0] * 8 + column // 64
     routes = jnp.concatenate([ref[...] for ref in refs[:-1]], axis=0)
-    r, s = iota((128, 256), 0), iota((128, 256), 1)
-    came = (r // 8) % 2 * 128 + jnp.bitwise_xor((r // 16) % 4, at_ref[1]) * 32 + r // 64 * 8 + r % 8
+    r, s = iota((128, 128), 0), iota((128, 128), 1)
+    came = (4 - jnp.bitwise_xor((r // 16) % 4, at_ref[1])) % 4 * 32 + (r // 8) % 2 * 16 + r // 64 * 8 + r % 8
     move = jnp.where(came == s, 1.0, 0.0).astype(BF)
     named = named_mask(jnp.dot(move, routes, preferred_element_type=F32), expert.astype(F32))
     r, s = iota((128, 128), 0), iota((128, 128), 1)
@@ -260,7 +279,7 @@
 
 def order_kernel(own_ref, ut_ref, out_ref):
     row, column = iota((512, 512), 0), iota((512, 512), 1)
-    near = (column // 128) % 2 * 16 + (column // 32) % 4 * 4 + column // 256 * 2
+    near = (column // 128) % 2 * 16 + (4 - (column // 32) % 4) % 4 * 4 + column // 256 * 2
     origin = column % 32 // 2 * 32 + jnp.bitwise_xor(own_ref[0], near) + column % 2
     move = jnp.where(row == origin, 1.0, 0.0).astype(BF)
     out_ref[...] = jnp.dot(ut_ref[...], move, preferred_element_type=F32).astype(BF)
@@ -327,24 +346,33 @@
     ut, u = gated(jnp.swapaxes(gate_pre, 1, 2)[0], jnp.swapaxes(grad_hidden, 1, 2)[0])
     other_u = swap(u, "c")
     terms = terms_of(core[None], u, other_u, weight_t, other_t)
+    arrived, terms = lax.optimization_barrier((arrived, terms))
     back = lax.all_to_all(
         terms.reshape(16, 32, half), PLANE, split_axis=0, concat_axis=0, tiled=True
     ).reshape(512, half)
 
-    two = unfold(home_arg, arrived, width)
-    run = jnp.concatenate([two] + [cross(two, k) for k in (1, 2, 3)], axis=0)
-    other_run = swap(run, "c")
-    pair = swap(run, "yi")
+    near_routes = own_routes(home_arg, arrived)
+    two = unfold(arrived, near_routes, swap(near_routes, "c"), width)
+    near, far, far_too = (cross(two, k) for k in (3, 2, 1))
+    early, late = jnp.concatenate([two, near], axis=0), jnp.concatenate([far, far_too], axis=0)
+    early_pair = swap(early, "yi")
+    other_early, other_late = swap(early, "c"), swap(late, "c")
     u_rows = ordered(own_arg, ut)
-    choice = chooser(at_arg, run, other_run)
+    choice = chooser(at_arg, early, late)
 
     sums = combined(choice, back)
     parts = lax.all_to_all(
         sums.reshape(8, PAD, half + half // 2), RING, split_axis=0, concat_axis=0, tiled=True
     )
 
-    pair = lax.optimization_barrier((pair, sums))[0]
-    rows = [run, pair, other_run, swap(pair, "c")]
+    ready, _ = lax.optimization_barrier((late, sums))
+    late_pair = swap(ready, "yi")
+    other_early_pair = swap(early_pair, "c")
+    parts, other_early, other_late, other_early_pair = lax.optimization_barrier(
+        (parts, other_early, other_late, other_early_pair)
+    )
+    rows = [early, late, early_pair, late_pair, other_early, other_late]
+    rows += [other_early_pair, swap(late_pair, "c")]
     grad = weight_grad(u_rows, rows, width, 2048)
 
     mine, other = totalled(parts)

time: 131 us -> 134 us (1.023)
  the two profiles are of different devices: /device:TPU:1 before, /device:TPU:49 now
where the time goes in v6:
time: 134 us; the launch traced here: 133 us
  waiting for transfers between devices  62.3 us (46%)
  starting transfers between devices  35 us (26%)
  Pallas kernels  22.3 us (17%)
  local copies, waits for them, and re-layouts  9.7 us (7%)
  other arithmetic  2.69 us (2%)
    ppermute x3, waiting for transfers between devices, cross(): return lax.ppermute(value, 'zl', [(i, i ^ mask) for i in range(4)])  29.3 us
    ppermute x10, waiting for transfers between devices, swap(): return lax.ppermute(value, axis, [(0, 1), (1, 0)])  24 us
    all_to_all x1, starting transfers between devices, body(): lax.all_to_all(rows.reshape(16, 16, FOLD + EXTRA), FAR, split_axis=0, con...  12.4 us
    unnamed x21, local copies, waits for them, and re-layouts  9.67 us
    ppermute x10, starting transfers between devices, swap(): return lax.ppermute(value, axis, [(0, 1), (1, 0)])  8.06 us
    all_to_all x1, starting transfers between devices, body(): lax.all_to_all(sums.reshape(8, PAD, half + half // 2), RING, split_axis=0...  6.23 us
    pallas_call x1, Pallas kernels, weight_grad(): pl.pallas_call(functools.partial(weight_kernel, len(blocks)), grid=(width...  5.59 us
    all_to_all x1, starting transfers between devices, body(): lax.all_to_all(terms.reshape(16, 32, half), PLANE, split_axis=0, concat_a...  5.56 us
  transfers between devices with their start and end apart: 16, of which 10 were waited for; matrix products, arithmetic and copies ran while one was open for 2% of the time, Pallas kernels for 8%

profile of v6, /device:TPU:49, one launch (start us, length us, event | category | flops | bytes accessed | tf_op | source)
XLA Modules:
  0.0 132.8 jit_solution(3680946582265411809)
XLA Ops:
  0.6 2.3 %shard_map.68 = bf16[256,896]{1,0:T(8,128)(2,1)} custom-call(bf16[6,6144]{1,0:T(8,128)(2,1)} %tokens_ref.1, s32[4,6]{1,0:T(4,128)} %bitcast.32), custom_call_target="tpu_custom_call" | custom-call | flops 1000000 | bytes 500000 | tf_op jit(solution)/shard_map/pallas_call | solution.py:138
  2.9 3.7 %shard_map.70 = bf16[336,3072]{1,0:T(8,128)(2,1)} custom-call(s32[1]{0:T(128)} %bitcast.2.core_ref, bf16[336,6144]{1,0:T(8,128)(2,1)} %bitcast.23), custom_call_target="tpu_custom_call" | custom-call | bytes 4200000 | tf_op jit(solution)/shard_map/pallas_call | solution.py:62
  6.6 0.7 collective-permute-start.1
  7.3 12.4 %all-to-all-start = ((bf16[16,16,896]{2,1,0:T(8,128)(2,1)}), bf16[16,16,896]{2,1,0:T(8,128)(2,1)S(1)}, u32[]{:S(2)}, u32[]{:S(2)}) async-start(bf16[16,16,896]{2,1,0:T(8,128)(2,1)} %bitcast.6), calls=%async_computation | async-start | bytes 917504 | tf_op jit(solution)/shard_map/all_to_all | solution.py:340
  19.7 2.2 %shard_map.69 = (bf16[336,512]{1,0:T(8,128)(2,1)}, bf16[512,336]{1,0:T(8,128)(2,1)}) custom-call(bf16[336,512]{1,0:T(8,128)(2,1)} %bitcast.30, bf16[336,512]{1,0:T(8,128)(2,1)} %bitcast.31), custom_call_target="tpu_custom_call" | custom-call | flops 1000000 | bytes 1400000 | tf_op jit(solution)/shard_map/pallas_call | solution.py:43
  21.9 0.6 collective-permute-start
  22.5 1.6 %collective-permute-done.v_ref = bf16[512,336]{1,0:T(8,128)(2,1)S(1)} collective-permute-done((bf16[512,336]{1,0:T(8,128)(2,1)}, bf16[512,336]{1,0:T(8,128)(2,1)S(1)}, u32[]{:S(2)}, u32[]{:S(2)}) %collective-permute-start) | collective-permute-done | bytes 344096 | tf_op jit(solution)/shard_map/ppermute | solution.py:321
  24.0 2.2 %copy-done = bf16[1,6144,336]{1,2,0:T(8,128)(2,1)S(1)} copy-done((bf16[1,6144,336]{1,2,0:T(8,128)(2,1)S(1)}, bf16[1,6144,336]{1,2,0:T(8,128)(2,1)}, u32[]{:S(2)}) %copy-start) | copy-done | bytes 4128792
  26.2 1.0 copy-done.8
  27.2 5.0 %shard_map.71 = bf16[16,2,16,3072]{3,2,1,0:T(8,128)(2,1)} custom-call(s32[1]{0:T(128)} %bitcast.2.core_ref, bf16[512,336]{1,0:T(8,128)(2,1)S(1)} %copy-done.8, bf16[512,336]{1,0:T(8,128)(2,1)S(1)} %collective-permute-done.v_ref, bf16[336,6144]{1,0:T(8,128)(2,1)S(1)} %bitcast.24, bf16[336,3072]{1,0:T(8,128)(2,1)S(1)} %collective-permute-done.1.x_ref), custom_call_target="tpu_custom_call" | custom-call | flops 2113929216 | bytes 8000000 | tf_op jit(solution)/shard_map/pallas_call | solution.py:89
  32.2 5.1 %all-to-all-done = bf16[16,16,896]{2,1,0:T(8,128)(2,1)S(1)} async-done(((bf16[16,16,896]{2,1,0:T(8,128)(2,1)}), bf16[16,16,896]{2,1,0:T(8,128)(2,1)S(1)}, u32[]{:S(2)}, u32[]{:S(2)}) %all-to-all-start) | async-done | bytes 458784 | tf_op jit(solution)/shard_map/all_to_all | solution.py:340
  37.3 0.8 copy-done.3
  38.1 5.6 %all-to-all-start.1 = ((bf16[16,32,3072]{2,1,0:T(8,128)(2,1)}), bf16[16,32,3072]{2,1,0:T(8,128)(2,1)S(1)}, u32[]{:S(2)}, u32[]{:S(2)}) async-start(bf16[16,32,3072]{2,1,0:T(8,128)(2,1)} %bitcast.13), calls=%async_computation.1 | async-start | bytes 6291456 | tf_op jit(solution)/shard_map/all_to_all | solution.py:350
  43.7 1.0 copy-done.4
  44.7 0.1 shard_map.72.mine_ref
  44.8 1.6 %collective-permute-start.2 = (bf16[16,128]{1,0:T(8,128)(2,1)S(1)}, bf16[16,128]{1,0:T(8,128)(2,1)S(1)}, u32[]{:S(2)}, u32[]{:S(2)}) collective-permute-start(bf16[16,128]{1,0:T(8,128)(2,1)S(1)} %shard_map.72.mine_ref), channel_id=1, source_target_pairs={{0,1},{1,0},{2,3},{3,2},{4,5},{5,4},{6,7},{7,6},{8,9},{9,8},{10,11... | collective-permute-start | bytes 12296 | tf_op jit(solution)/shard_map/ppermute | solution.py:321
  46.5 0.8 collective-permute-done.2.other_ref
  47.3 0.6 shard_map.73
  47.9 0.8 collective-permute-start.3
  48.7 0.1 pad_add_fusion.at_ref
  48.8 0.1 collective-permute-start.4
  48.9 1.9 %collective-permute-start.5 = (bf16[32,6272]{1,0:T(8,128)(2,1)S(1)}, bf16[32,6272]{1,0:T(8,128)(2,1)S(1)}, u32[]{:S(2)}, u32[]{:S(2)}) collective-permute-start(bf16[32,6272]{1,0:T(8,128)(2,1)S(1)} %shard_map.73), channel_id=1, source_target_pairs={{0,2},{2,0},{4,6},{6,4},{1,3},{3,1},{5,7},{7,5},{8,10},{10,8},{12,... | collective-permute-start | bytes 1204232 | tf_op jit(solution)/shard_map/ppermute | solution.py:325
  50.8 25.1 %collective-permute-done.3 = bf16[32,6272]{1,0:T(8,128)(2,1)} collective-permute-done((bf16[32,6272]{1,0:T(8,128)(2,1)S(1)}, bf16[32,6272]{1,0:T(8,128)(2,1)}, u32[]{:S(2)}, u32[]{:S(2)}) %collective-permute-start.3) | collective-permute-done | bytes 401440 | tf_op jit(solution)/shard_map/ppermute | solution.py:325
  75.9 2.0 %pad_maximum_fusion.refs_0_ = bf16[64,6272]{1,0:T(8,128)(2,1)} fusion(bf16[32,6272]{1,0:T(8,128)(2,1)} %collective-permute-done.3, bf16[32,6272]{1,0:T(8,128)(2,1)S(1)} %shard_map.73), kind=kLoop, calls=%fused_computation | loop fusion | flops 1605632 | bytes 1605632 | tf_op jit(solution)/shard_map/concatenate | solution.py:357
  77.8 0.9 collective-permute-start.8
  78.7 4.2 %collective-permute-done.4 = bf16[32,6272]{1,0:T(8,128)(2,1)S(1)} collective-permute-done((bf16[32,6272]{1,0:T(8,128)(2,1)S(1)}, bf16[32,6272]{1,0:T(8,128)(2,1)S(1)}, u32[]{:S(2)}, u32[]{:S(2)}) %collective-permute-start.4) | collective-permute-done | bytes 401440 | tf_op jit(solution)/shard_map/ppermute | solution.py:325
  83.0 1.4 %shard_map.74.choice_ref = bf16[192,512]{1,0:T(8,128)(2,1)S(1)} custom-call(s32[3]{0:T(128)S(1)} %pad_add_fusion.at_ref, bf16[64,6272]{1,0:T(8,128)(2,1)} %pad_maximum_fusion.refs_0_, bf16[64,6272]{1,0:T(8,128)(2,1)S(1)} %constant_dynamic-update-slice_fusion.refs_1_), custom_call_target="tpu_custom_call" | custom-call | flops 1000000 | bytes 200000 | tf_op jit(solution)/shard_map/pallas_call | solution.py:215
  84.4 0.9 copy-done.1
  85.3 0.8 shard_map.75
  86.1 0.8 copy-done.5
  86.9 6.2 %all-to-all-start.2 = ((bf16[8,8,4608]{2,1,0:T(8,128)(2,1)}), bf16[8,8,4608]{2,1,0:T(8,128)(2,1)S(1)}, u32[]{:S(2)}, u32[]{:S(2)}) async-start(bf16[8,8,4608]{2,1,0:T(8,128)(2,1)} %bitcast.28), calls=%async_computation.2 | async-start | bytes 1179648 | tf_op jit(solution)/shard_map/all_to_all | solution.py:364
  93.1 0.8 collective-permute-start.6
  93.9 8.9 %collective-permute-done.8.refs_2_ = bf16[64,6272]{1,0:T(8,128)(2,1)} collective-permute-done((bf16[64,6272]{1,0:T(8,128)(2,1)}, bf16[64,6272]{1,0:T(8,128)(2,1)}, u32[]{:S(2)}, u32[]{:S(2)}) %collective-permute-start.8) | collective-permute-done | bytes 802848 | tf_op jit(solution)/shard_map/ppermute | solution.py:321
  102.8 0.5 collective-permute-start.9
  103.3 0.6 collective-permute-start.11
  103.9 1.6 %collective-permute-done.9.refs_6_ = bf16[64,6272]{1,0:T(8,128)(2,1)S(1)} collective-permute-done((bf16[64,6272]{1,0:T(8,128)(2,1)}, bf16[64,6272]{1,0:T(8,128)(2,1)S(1)}, u32[]{:S(2)}, u32[]{:S(2)}) %collective-permute-start.9) | collective-permute-done | bytes 802848 | tf_op jit(solution)/shard_map/ppermute | solution.py:321
  105.5 0.9 copy-done.6
  106.3 3.9 %all-to-all-done.2.parts_ref = bf16[8,8,4608]{2,1,0:T(8,128)(2,1)S(1)} async-done(((bf16[8,8,4608]{2,1,0:T(8,128)(2,1)}), bf16[8,8,4608]{2,1,0:T(8,128)(2,1)S(1)}, u32[]{:S(2)}, u32[]{:S(2)}) %all-to-all-start.2) | async-done | bytes 589856 | tf_op jit(solution)/shard_map/all_to_all | solution.py:364
  110.3 0.2 shard_map.76
  110.5 1.7 %collective-permute-start.10 = (bf16[8,3072]{1,0:T(8,128)(2,1)S(1)}, bf16[8,3072]{1,0:T(8,128)(2,1)S(1)}, u32[]{:S(2)}, u32[]{:S(2)}) collective-permute-start(bf16[8,3072]{1,0:T(8,128)(2,1)S(1)} %get-tuple-element.22), channel_id=1, source_target_pairs={{0,1},{1,0},{2,3},{3,2},{4,5},{5,4},{6,7},{7,6},{8,9},{9,8},{10,11... | collective-permute-start | bytes 147464 | tf_op jit(solution)/shard_map/ppermute | solution.py:321
  112.1 1.0 copy-done.9
  113.1 0.4 shard_map.77.u_ref
  113.5 9.7 %collective-permute-done.11.refs_3_ = bf16[64,6272]{1,0:T(8,128)(2,1)} collective-permute-done((bf16[64,6272]{1,0:T(8,128)(2,1)}, bf16[64,6272]{1,0:T(8,128)(2,1)}, u32[]{:S(2)}, u32[]{:S(2)}) %collective-permute-start.11) | collective-permute-done | bytes 802848 | tf_op jit(solution)/shard_map/ppermute | solution.py:321
  123.1 0.8 collective-permute-start.12
  124.0 0.6 pad_maximum_fusion.1
  124.6 1.5 %collective-permute-done.12.refs_7_ = bf16[64,6272]{1,0:T(8,128)(2,1)S(1)} collective-permute-done((bf16[64,6272]{1,0:T(8,128)(2,1)}, bf16[64,6272]{1,0:T(8,128)(2,1)S(1)}, u32[]{:S(2)}, u32[]{:S(2)}) %collective-permute-start.12) | collective-permute-done | bytes 802848 | tf_op jit(solution)/shard_map/ppermute | solution.py:321
  126.1 1.1 copy-done.7
  127.2 5.6 %shard_map.78 = bf16[336,6144]{1,0:T(8,128)(2,1)} custom-call(bf16[336,512]{1,0:T(8,128)(2,1)S(1)} %shard_map.77.u_ref, bf16[64,6272]{1,0:T(8,128)(2,1)} %pad_maximum_fusion.refs_0_, bf16[64,6272]{1,0:T(8,128)(2,1)S(1)} %copy-done.2, bf16[64,6272]{1,0:T(8,128)(2,1)} %collective-permute-done.8.refs_2_, bf16[64,6272]{1,0:T(8,128)(2,1)} %collective-permute-done.11.refs_3_, ...), custom_call_target="tpu_custom_call" | custom-call | flops 2113929216 | bytes 10420224 | tf_op jit(solution)/shard_map/pallas_call | solution.py:307
  (21 shorter events, 0.1 us)
Async XLA Ops:
  6.6 17.5 %collective-permute-start.1 = (bf16[336,3072]{1,0:T(8,128)(2,1)}, bf16[336,3072]{1,0:T(8,128)(2,1)S(1)}, u32[]{:S(2)}, u32[]{:S(2)}) collective-permute-start(bf16[336,3072]{1,0:T(8,128)(2,1)} %shard_map.70), channel_id=1, source_target_pairs={{0,1},{1,0},{2,3},{3,2},{4,5},{5,4},{6,7},{7,6},{8,9},{9,8},{10,11... | collective-permute-start | bytes 6193160 | tf_op jit(solution)/shard_map/ppermute | solution.py:321
  7.3 30.1 %all-to-all-start = ((bf16[16,16,896]{2,1,0:T(8,128)(2,1)}), bf16[16,16,896]{2,1,0:T(8,128)(2,1)S(1)}, u32[]{:S(2)}, u32[]{:S(2)}) async-start(bf16[16,16,896]{2,1,0:T(8,128)(2,1)} %bitcast.6), calls=%async_computation | async-start | bytes 917504 | tf_op jit(solution)/shard_map/all_to_all | solution.py:340
  21.9 2.1 %collective-permute-start = (bf16[512,336]{1,0:T(8,128)(2,1)}, bf16[512,336]{1,0:T(8,128)(2,1)S(1)}, u32[]{:S(2)}, u32[]{:S(2)}) collective-permute-start(bf16[512,336]{1,0:T(8,128)(2,1)} %get-tuple-element.16.u_ref), channel_id=1, source_target_pairs={{0,1},{1,0},{2,3},{3,2},{4,5},{5,4},{6,7},{7,6},{8,9},{9,8},{10,11... | collective-permute-start | bytes 1032200 | tf_op jit(solution)/shard_map/ppermute | solution.py:321
  24.0 2.2 %copy-start = (bf16[1,6144,336]{1,2,0:T(8,128)(2,1)S(1)}, bf16[1,6144,336]{1,2,0:T(8,128)(2,1)}, u32[]{:S(2)}) copy-start(bf16[1,6144,336]{1,2,0:T(8,128)(2,1)} %param.7) | copy-start | bytes 12386308
  26.2 1.0 copy-start.8
  37.3 0.8 copy-start.3
  38.1 47.2 %all-to-all-start.1 = ((bf16[16,32,3072]{2,1,0:T(8,128)(2,1)}), bf16[16,32,3072]{2,1,0:T(8,128)(2,1)S(1)}, u32[]{:S(2)}, u32[]{:S(2)}) async-start(bf16[16,32,3072]{2,1,0:T(8,128)(2,1)} %bitcast.13), calls=%async_computation.1 | async-start | bytes 6291456 | tf_op jit(solution)/shard_map/all_to_all | solution.py:350
  43.7 1.0 copy-start.4
  44.8 2.5 %collective-permute-start.2 = (bf16[16,128]{1,0:T(8,128)(2,1)S(1)}, bf16[16,128]{1,0:T(8,128)(2,1)S(1)}, u32[]{:S(2)}, u32[]{:S(2)}) collective-permute-start(bf16[16,128]{1,0:T(8,128)(2,1)S(1)} %shard_map.72.mine_ref), channel_id=1, source_target_pairs={{0,1},{1,0},{2,3},{3,2},{4,5},{5,4},{6,7},{7,6},{8,9},{9,8},{10,11... | collective-permute-start | bytes 12296 | tf_op jit(solution)/shard_map/ppermute | solution.py:321
  47.9 27.9 %collective-permute-start.3 = (bf16[32,6272]{1,0:T(8,128)(2,1)S(1)}, bf16[32,6272]{1,0:T(8,128)(2,1)}, u32[]{:S(2)}, u32[]{:S(2)}) collective-permute-start(bf16[32,6272]{1,0:T(8,128)(2,1)S(1)} %shard_map.73), channel_id=1, source_target_pairs={{0,6},{2,4},{4,2},{6,0},{1,7},{3,5},{5,3},{7,1},{8,14},{10,12},{12... | collective-permute-start | bytes 1204232 | tf_op jit(solution)/shard_map/ppermute | solution.py:325
  48.8 34.1 %collective-permute-start.4 = (bf16[32,6272]{1,0:T(8,128)(2,1)S(1)}, bf16[32,6272]{1,0:T(8,128)(2,1)S(1)}, u32[]{:S(2)}, u32[]{:S(2)}) collective-permute-start(bf16[32,6272]{1,0:T(8,128)(2,1)S(1)} %shard_map.73), channel_id=1, source_target_pairs={{0,4},{2,6},{4,0},{6,2},{1,5},{3,7},{5,1},{7,3},{8,12},{10,14},{12... | collective-permute-start | bytes 1204232 | tf_op jit(solution)/shard_map/ppermute | solution.py:325
  48.9 34.0 %collective-permute-start.5 = (bf16[32,6272]{1,0:T(8,128)(2,1)S(1)}, bf16[32,6272]{1,0:T(8,128)(2,1)S(1)}, u32[]{:S(2)}, u32[]{:S(2)}) collective-permute-start(bf16[32,6272]{1,0:T(8,128)(2,1)S(1)} %shard_map.73), channel_id=1, source_target_pairs={{0,2},{2,0},{4,6},{6,4},{1,3},{3,1},{5,7},{7,5},{8,10},{10,8},{12,... | collective-permute-start | bytes 1204232 | tf_op jit(solution)/shard_map/ppermute | solution.py:325
  77.8 25.0 %collective-permute-start.8 = (bf16[64,6272]{1,0:T(8,128)(2,1)}, bf16[64,6272]{1,0:T(8,128)(2,1)}, u32[]{:S(2)}, u32[]{:S(2)}) collective-permute-start(bf16[64,6272]{1,0:T(8,128)(2,1)} %pad_maximum_fusion.refs_0_), channel_id=1, source_target_pairs={{0,8},{8,0},{1,9},{9,1},{2,10},{10,2},{3,11},{11,3},{4,12},{12,4},... | collective-permute-start | bytes 2408456 | tf_op jit(solution)/shard_map/ppermute | solution.py:321
  84.4 0.9 copy-start.1
  86.1 0.8 copy-start.5
  86.9 39.2 %copy-start.2 = (bf16[64,6272]{1,0:T(8,128)(2,1)S(1)}, bf16[64,6272]{1,0:T(8,128)(2,1)}, u32[]{:S(2)}) copy-start(bf16[64,6272]{1,0:T(8,128)(2,1)} %copy-done.1) | copy-start | bytes 2408452
  86.9 23.4 %all-to-all-start.2 = ((bf16[8,8,4608]{2,1,0:T(8,128)(2,1)}), bf16[8,8,4608]{2,1,0:T(8,128)(2,1)S(1)}, u32[]{:S(2)}, u32[]{:S(2)}) async-start(bf16[8,8,4608]{2,1,0:T(8,128)(2,1)} %bitcast.28), calls=%async_computation.2 | async-start | bytes 1179648 | tf_op jit(solution)/shard_map/all_to_all | solution.py:364
  93.1 10.8 %collective-permute-start.6 = (bf16[64,6272]{1,0:T(8,128)(2,1)}, bf16[64,6272]{1,0:T(8,128)(2,1)S(1)}, u32[]{:S(2)}, u32[]{:S(2)}) collective-permute-start(bf16[64,6272]{1,0:T(8,128)(2,1)} %pad_maximum_fusion.refs_0_), channel_id=1, source_target_pairs={{0,1},{1,0},{2,3},{3,2},{4,5},{5,4},{6,7},{7,6},{8,9},{9,8},{10,11... | collective-permute-start | bytes 2408456 | tf_op jit(solution)/shard_map/ppermute | solution.py:321
  93.9 10.0 %collective-permute-start.7 = (bf16[64,6272]{1,0:T(8,128)(2,1)}, bf16[64,6272]{1,0:T(8,128)(2,1)S(1)}, u32[]{:S(2)}, u32[]{:S(2)}) collective-permute-start(bf16[64,6272]{1,0:T(8,128)(2,1)} %copy-done.1), channel_id=1, source_target_pairs={{0,1},{1,0},{2,3},{3,2},{4,5},{5,4},{6,7},{7,6},{8,9},{9,8},{10,11... | collective-permute-start | bytes 2408456 | tf_op jit(solution)/shard_map/ppermute | solution.py:321
  102.8 2.6 %collective-permute-start.9 = (bf16[64,6272]{1,0:T(8,128)(2,1)}, bf16[64,6272]{1,0:T(8,128)(2,1)S(1)}, u32[]{:S(2)}, u32[]{:S(2)}) collective-permute-start(bf16[64,6272]{1,0:T(8,128)(2,1)} %collective-permute-done.8.refs_2_), channel_id=1, source_target_pairs={{0,1},{1,0},{2,3},{3,2},{4,5},{5,4},{6,7},{7,6},{8,9},{9,8},{10,11... | collective-permute-start | bytes 2408456 | tf_op jit(solution)/shard_map/ppermute | solution.py:321
  103.3 19.8 %collective-permute-start.11 = (bf16[64,6272]{1,0:T(8,128)(2,1)}, bf16[64,6272]{1,0:T(8,128)(2,1)}, u32[]{:S(2)}, u32[]{:S(2)}) collective-permute-start(bf16[64,6272]{1,0:T(8,128)(2,1)} %copy-done.1), channel_id=1, source_target_pairs={{0,8},{8,0},{1,9},{9,1},{2,10},{10,2},{3,11},{11,3},{4,12},{12,4},... | collective-permute-start | bytes 2408456 | tf_op jit(solution)/shard_map/ppermute | solution.py:321
  105.5 0.9 copy-start.6
  110.5 13.5 %collective-permute-start.10 = (bf16[8,3072]{1,0:T(8,128)(2,1)S(1)}, bf16[8,3072]{1,0:T(8,128)(2,1)S(1)}, u32[]{:S(2)}, u32[]{:S(2)}) collective-permute-start(bf16[8,3072]{1,0:T(8,128)(2,1)S(1)} %get-tuple-element.22), channel_id=1, source_target_pairs={{0,1},{1,0},{2,3},{3,2},{4,5},{5,4},{6,7},{7,6},{8,9},{9,8},{10,11... | collective-permute-start | bytes 147464 | tf_op jit(solution)/shard_map/ppermute | solution.py:321
  112.1 1.0 copy-start.9
  123.1 2.9 %collective-permute-start.12 = (bf16[64,6272]{1,0:T(8,128)(2,1)}, bf16[64,6272]{1,0:T(8,128)(2,1)S(1)}, u32[]{:S(2)}, u32[]{:S(2)}) collective-permute-start(bf16[64,6272]{1,0:T(8,128)(2,1)} %collective-permute-done.11.refs_3_), channel_id=1, source_target_pairs={{0,1},{1,0},{2,3},{3,2},{4,5},{5,4},{6,7},{7,6},{8,9},{9,8},{10,11... | collective-permute-start | bytes 2408456 | tf_op jit(solution)/shard_map/ppermute | solution.py:321
  126.1 1.1 copy-start.7

commit v7 on v5

--- a/solution.py
+++ b/solution.py
@@ -11,7 +11,7 @@
 CAP = 2
 AXES = ("zh", "x", "yp", "yi", "zl", "c")
 SIZES = (2, 4, 2, 2, 4, 2)
-FAR = ("zh", "x", "yp")
+FAR = ("x", "yp", "zh")
 PLANE = ("x", "yp", "yi")
 RING = ("zh", "zl")
 TOK = 6
@@ -120,7 +120,7 @@
     named_ref[:count, :4] = routes_ref[...].astype(F32).T
     routes = named_ref[...]
     column = iota((PAD, 256), 1)
-    named = named_mask(routes, (column // 16).astype(F32))
+    named = named_mask(routes, (column // 16 % 2 * 8 + column // 32).astype(F32))
     lower = jnp.where(iota((PAD, PAD), 0) > iota((PAD, PAD), 1), 1.0, 0.0)
     before = jnp.dot(lower, named, preferred_element_type=F32)
     chosen = jnp.where(before == (column // 8 % 2).astype(F32), named, 0.0)
@@ -152,7 +152,7 @@
         move = jnp.where(s == r * 8 + fold, 1.0, 0.0).astype(BF)
         piece = jnp.dot(move, rows[:, :FOLD], preferred_element_type=F32)
         out_ref[:, fold * FOLD : fold * FOLD + FOLD] = piece.astype(BF)
-    move = jnp.where((s == r // 8 * 128 + at_ref[0] * 16 + r % 8) & (r < 16), 1.0, 0.0).astype(BF)
+    move = jnp.where((s == (at_ref[0] * 2 + r // 8) * 16 + r % 8) & (r < 16), 1.0, 0.0).astype(BF)
     out_ref[:, width:] = jnp.dot(move, rows[:, FOLD:], preferred_element_type=F32).astype(BF)
 
 
@@ -261,7 +261,7 @@
 def order_kernel(own_ref, ut_ref, out_ref):
     row, column = iota((512, 512), 0), iota((512, 512), 1)
     near = (column // 128) % 2 * 16 + (column // 32) % 4 * 4 + column // 256 * 2
-    origin = column % 32 // 2 * 32 + jnp.bitwise_xor(own_ref[0], near) + column % 2
+    origin = column // 2 % 2 * 256 + column % 32 // 4 * 32 + jnp.bitwise_xor(own_ref[0], near) + column % 2
     move = jnp.where(row == origin, 1.0, 0.0).astype(BF)
     out_ref[...] = jnp.dot(ut_ref[...], move, preferred_element_type=F32).astype(BF)
 

time: 131 us -> 131 us (level)
    all_to_all x1, waiting for transfers between devices: 1.95 us -> 0.6 us  [body(): lax.all_to_all(rows.reshape(16, 16, FOLD + EXTRA), FAR, split_axis=0, con...]
where the time goes in v7:
time: 131 us; the launch traced here: 130 us
  waiting for transfers between devices  61.9 us (47%)
  starting transfers between devices  34.4 us (26%)
  Pallas kernels  25.8 us (20%)
  local copies, waits for them, and re-layouts  5.57 us (4%)
  other arithmetic  1.67 us (1%)
    ppermute x3, waiting for transfers between devices, cross(): return lax.ppermute(value, 'zl', [(i, i ^ mask) for i in range(4)])  33.9 us
    ppermute x6, waiting for transfers between devices, swap(): return lax.ppermute(value, axis, [(0, 1), (1, 0)])  27.4 us
    all_to_all x1, starting transfers between devices, body(): lax.all_to_all(rows.reshape(16, 16, FOLD + EXTRA), FAR, split_axis=0, con...  11.6 us
    all_to_all x1, starting transfers between devices, body(): lax.all_to_all(terms.reshape(16, 32, half), PLANE, split_axis=0, concat_a...  6.29 us
    ppermute x6, starting transfers between devices, swap(): return lax.ppermute(value, axis, [(0, 1), (1, 0)])  6.27 us
    pallas_call x1, Pallas kernels, weight_grad(): pl.pallas_call(functools.partial(weight_kernel, len(blocks)), grid=(width...  5.82 us
    unnamed x10, local copies, waits for them, and re-layouts  5.57 us
    ppermute x3, starting transfers between devices, cross(): return lax.ppermute(value, 'zl', [(i, i ^ mask) for i in range(4)])  5.14 us
  transfers between devices with their start and end apart: 12, of which 7 were waited for; matrix products, arithmetic and copies ran while one was open for 1% of the time, Pallas kernels for 11%

profile of v7, /device:TPU:1, one launch (start us, length us, event | category | flops | bytes accessed | tf_op | source)
XLA Modules:
  0.0 130.0 jit_solution(2078068375329394873)
XLA Ops:
  0.6 2.3 %shard_map.68 = bf16[256,896]{1,0:T(8,128)(2,1)} custom-call(bf16[6,6144]{1,0:T(8,128)(2,1)} %tokens_ref.1, s32[4,6]{1,0:T(4,128)} %bitcast.30), custom_call_target="tpu_custom_call" | custom-call | flops 1000000 | bytes 500000 | tf_op jit(solution)/shard_map/pallas_call | solution.py:138
  2.9 3.7 %shard_map.72 = bf16[336,3072]{1,0:T(8,128)(2,1)} custom-call(s32[1]{0:T(128)} %bitcast.2.core_ref, bf16[336,6144]{1,0:T(8,128)(2,1)} %bitcast.23), custom_call_target="tpu_custom_call" | custom-call | bytes 4200000 | tf_op jit(solution)/shard_map/pallas_call | solution.py:62
  6.6 3.2 %collective-permute-start.5 = (bf16[336,3072]{1,0:T(8,128)(2,1)}, bf16[336,3072]{1,0:T(8,128)(2,1)S(1)}, u32[]{:S(2)}, u32[]{:S(2)}) collective-permute-start(bf16[336,3072]{1,0:T(8,128)(2,1)} %shard_map.72), channel_id=1, source_target_pairs={{0,1},{1,0},{2,3},{3,2},{4,5},{5,4},{6,7},{7,6},{8,9},{9,8},{10,11... | collective-permute-start | bytes 6193160 | tf_op jit(solution)/shard_map/ppermute | solution.py:302
  9.8 11.6 %all-to-all-start = ((bf16[16,16,896]{2,1,0:T(8,128)(2,1)}), bf16[16,16,896]{2,1,0:T(8,128)(2,1)S(1)}, u32[]{:S(2)}, u32[]{:S(2)}) async-start(bf16[16,16,896]{2,1,0:T(8,128)(2,1)} %bitcast.7), calls=%async_computation | async-start | bytes 917504 | tf_op jit(solution)/shard_map/all_to_all | solution.py:321
  21.5 2.2 %shard_map.71 = (bf16[336,512]{1,0:T(8,128)(2,1)}, bf16[512,336]{1,0:T(8,128)(2,1)}) custom-call(bf16[336,512]{1,0:T(8,128)(2,1)} %bitcast.28, bf16[336,512]{1,0:T(8,128)(2,1)} %bitcast.29), custom_call_target="tpu_custom_call" | custom-call | flops 1000000 | bytes 1400000 | tf_op jit(solution)/shard_map/pallas_call | solution.py:43
  23.7 0.3 collective-permute-start.4
  23.9 1.6 %collective-permute-done.4.v_ref = bf16[512,336]{1,0:T(8,128)(2,1)S(1)} collective-permute-done((bf16[512,336]{1,0:T(8,128)(2,1)}, bf16[512,336]{1,0:T(8,128)(2,1)S(1)}, u32[]{:S(2)}, u32[]{:S(2)}) %collective-permute-start.4) | collective-permute-done | bytes 344096 | tf_op jit(solution)/shard_map/ppermute | solution.py:302
  25.6 0.0 collective-permute-done.5.x_ref
  25.6 0.0 copy-start
  25.6 2.2 %copy-done = bf16[1,6144,336]{1,2,0:T(8,128)(2,1)S(1)} copy-done((bf16[1,6144,336]{1,2,0:T(8,128)(2,1)S(1)}, bf16[1,6144,336]{1,2,0:T(8,128)(2,1)}, u32[]{:S(2)}) %copy-start) | copy-done | bytes 4128792
  27.8 0.0 copy-start.2
  27.8 1.0 copy-done.2
  28.8 5.0 %shard_map.73 = bf16[16,2,16,3072]{3,2,1,0:T(8,128)(2,1)} custom-call(s32[1]{0:T(128)} %bitcast.2.core_ref, bf16[512,336]{1,0:T(8,128)(2,1)S(1)} %copy-done.2, bf16[512,336]{1,0:T(8,128)(2,1)S(1)} %collective-permute-done.4.v_ref, bf16[336,6144]{1,0:T(8,128)(2,1)S(1)} %bitcast.24, bf16[336,3072]{1,0:T(8,128)(2,1)S(1)} %collective-permute-done.5.x_ref), custom_call_target="tpu_custom_call" | custom-call | flops 2113929216 | bytes 8000000 | tf_op jit(solution)/shard_map/pallas_call | solution.py:89
  33.8 0.6 all-to-all-done
  34.4 6.3 %all-to-all-start.1 = ((bf16[16,32,3072]{2,1,0:T(8,128)(2,1)}), bf16[16,32,3072]{2,1,0:T(8,128)(2,1)}, u32[]{:S(2)}, u32[]{:S(2)}) async-start(bf16[16,32,3072]{2,1,0:T(8,128)(2,1)} %bitcast.13), calls=%async_computation.1 | async-start | bytes 6291456 | tf_op jit(solution)/shard_map/all_to_all | solution.py:330
  40.7 0.7 shard_map.69
  41.4 1.7 %collective-permute-start.2 = (bf16[32,6272]{1,0:T(8,128)(2,1)S(1)}, bf16[32,6272]{1,0:T(8,128)(2,1)S(1)}, u32[]{:S(2)}, u32[]{:S(2)}) collective-permute-start(bf16[32,6272]{1,0:T(8,128)(2,1)S(1)} %shard_map.69), channel_id=1, source_target_pairs={{0,6},{2,4},{4,2},{6,0},{1,7},{3,5},{5,3},{7,1},{8,14},{10,12},{12... | collective-permute-start | bytes 1204232 | tf_op jit(solution)/shard_map/ppermute | solution.py:306
  43.1 3.4 %collective-permute-start.1 = (bf16[32,6272]{1,0:T(8,128)(2,1)S(1)}, bf16[32,6272]{1,0:T(8,128)(2,1)S(1)}, u32[]{:S(2)}, u32[]{:S(2)}) collective-permute-start(bf16[32,6272]{1,0:T(8,128)(2,1)S(1)} %shard_map.69), channel_id=1, source_target_pairs={{0,4},{2,6},{4,0},{6,2},{1,5},{3,7},{5,1},{7,3},{8,12},{10,14},{12... | collective-permute-start | bytes 1204232 | tf_op jit(solution)/shard_map/ppermute | solution.py:306
  46.5 0.0 collective-permute-start
  46.5 6.3 %collective-permute-done.2 = bf16[32,6272]{1,0:T(8,128)(2,1)S(1)} collective-permute-done((bf16[32,6272]{1,0:T(8,128)(2,1)S(1)}, bf16[32,6272]{1,0:T(8,128)(2,1)S(1)}, u32[]{:S(2)}, u32[]{:S(2)}) %collective-permute-start.2) | collective-permute-done | bytes 401440 | tf_op jit(solution)/shard_map/ppermute | solution.py:306
  52.8 27.6 %collective-permute-done.1 = bf16[32,6272]{1,0:T(8,128)(2,1)S(1)} collective-permute-done((bf16[32,6272]{1,0:T(8,128)(2,1)S(1)}, bf16[32,6272]{1,0:T(8,128)(2,1)S(1)}, u32[]{:S(2)}, u32[]{:S(2)}) %collective-permute-start.1) | collective-permute-done | bytes 401440 | tf_op jit(solution)/shard_map/ppermute | solution.py:306
  80.4 0.0 collective-permute-done
  80.4 0.1 pad_maximum_fusion.refs_0_
  80.5 0.5 collective-permute-start.3
  81.0 1.3 %collective-permute-start.7 = (bf16[128,6272]{1,0:T(8,128)(2,1)S(1)}, bf16[128,6272]{1,0:T(8,128)(2,1)}, u32[]{:S(2)}, u32[]{:S(2)}) collective-permute-start(bf16[128,6272]{1,0:T(8,128)(2,1)S(1)} %pad_maximum_fusion.refs_0_), channel_id=1, source_target_pairs={{0,8},{8,0},{1,9},{9,1},{2,10},{10,2},{3,11},{11,3},{4,12},{12,4},... | collective-permute-start | bytes 4816904 | tf_op jit(solution)/shard_map/ppermute | solution.py:302
  82.3 0.1 pad_add_fusion.at_ref
  82.4 1.7 %collective-permute-done.3.refs_1_.refs_2_ = bf16[128,6272]{1,0:T(8,128)(2,1)S(1)} collective-permute-done((bf16[128,6272]{1,0:T(8,128)(2,1)S(1)}, bf16[128,6272]{1,0:T(8,128)(2,1)S(1)}, u32[]{:S(2)}, u32[]{:S(2)}) %collective-permute-start.3) | collective-permute-done | bytes 1605664 | tf_op jit(solution)/shard_map/ppermute | solution.py:302
  84.1 1.2 shard_map.70.choice_ref
  85.3 0.0 all-to-all-done.1
  85.3 2.7 %shard_map.74 = bf16[64,4608]{1,0:T(8,128)(2,1)S(1)} custom-call(bf16[192,512]{1,0:T(8,128)(2,1)S(1)} %shard_map.70.choice_ref, bf16[512,3072]{1,0:T(8,128)(2,1)} %bitcast.14.back_ref), custom_call_target="tpu_custom_call" | custom-call | flops 603979776 | bytes 4000000 | tf_op jit(solution)/shard_map/pallas_call | solution.py:222
  88.0 0.0 copy-start.1
  88.0 0.8 copy-done.1
  88.8 5.0 %all-to-all-start.2 = ((bf16[8,8,4608]{2,1,0:T(8,128)(2,1)}), bf16[8,8,4608]{2,1,0:T(8,128)(2,1)}, u32[]{:S(2)}, u32[]{:S(2)}) async-start(bf16[8,8,4608]{2,1,0:T(8,128)(2,1)} %bitcast.25), calls=%async_computation.2 | async-start | bytes 1179648 | tf_op jit(solution)/shard_map/all_to_all | solution.py:342
  93.8 23.8 %collective-permute-done.7.refs_1_ = bf16[128,6272]{1,0:T(8,128)(2,1)} collective-permute-done((bf16[128,6272]{1,0:T(8,128)(2,1)S(1)}, bf16[128,6272]{1,0:T(8,128)(2,1)}, u32[]{:S(2)}, u32[]{:S(2)}) %collective-permute-start.7) | collective-permute-done | bytes 1605664 | tf_op jit(solution)/shard_map/ppermute | solution.py:302
  117.7 0.9 collective-permute-start.8
  118.6 0.0 all-to-all-done.2.parts_ref
  118.6 1.9 %shard_map.75 = (bf16[8,3072]{1,0:T(8,128)(2,1)S(1)}, bf16[8,3072]{1,0:T(8,128)(2,1)}) custom-call(bf16[8,8,4608]{2,1,0:T(8,128)(2,1)} %all-to-all-done.2.parts_ref), custom_call_target="tpu_custom_call" | custom-call | flops 1000 | bytes 1000 | tf_op jit(solution)/shard_map/pallas_call | solution.py:253
  120.5 0.0 copy-start.4
  120.5 0.6 copy-done.4
  121.1 0.0 collective-permute-start.6
  121.1 0.0 copy-start.3
  121.1 1.0 copy-done.3
  122.1 0.4 shard_map.76.u_ref
  122.5 0.2 collective-permute-done.6
  122.7 0.8 broadcast_select_fusion.1
  123.5 0.6 pad_maximum_fusion.1
  124.2 0.0 collective-permute-done.8.refs_3_
  124.2 5.8 %shard_map.77 = bf16[336,6144]{1,0:T(8,128)(2,1)} custom-call(bf16[336,512]{1,0:T(8,128)(2,1)S(1)} %shard_map.76.u_ref, bf16[128,6272]{1,0:T(8,128)(2,1)S(1)} %pad_maximum_fusion.refs_0_, bf16[128,6272]{1,0:T(8,128)(2,1)} %collective-permute-done.7.refs_1_, bf16[128,6272]{1,0:T(8,128)(2,1)S(1)} %collective-permute-done.3.refs_1_.refs_2_, ...), custom_call_target="tpu_custom_call" | custom-call | flops 2113929216 | bytes 10420224 | tf_op jit(solution)/shard_map/pallas_call | solution.py:288
Async XLA Ops:
  6.6 19.0 %collective-permute-start.5 = (bf16[336,3072]{1,0:T(8,128)(2,1)}, bf16[336,3072]{1,0:T(8,128)(2,1)S(1)}, u32[]{:S(2)}, u32[]{:S(2)}) collective-permute-start(bf16[336,3072]{1,0:T(8,128)(2,1)} %shard_map.72), channel_id=1, source_target_pairs={{0,1},{1,0},{2,3},{3,2},{4,5},{5,4},{6,7},{7,6},{8,9},{9,8},{10,11... | collective-permute-start | bytes 6193160 | tf_op jit(solution)/shard_map/ppermute | solution.py:302
  9.8 24.6 %all-to-all-start = ((bf16[16,16,896]{2,1,0:T(8,128)(2,1)}), bf16[16,16,896]{2,1,0:T(8,128)(2,1)S(1)}, u32[]{:S(2)}, u32[]{:S(2)}) async-start(bf16[16,16,896]{2,1,0:T(8,128)(2,1)} %bitcast.7), calls=%async_computation | async-start | bytes 917504 | tf_op jit(solution)/shard_map/all_to_all | solution.py:321
  23.7 1.9 %collective-permute-start.4 = (bf16[512,336]{1,0:T(8,128)(2,1)}, bf16[512,336]{1,0:T(8,128)(2,1)S(1)}, u32[]{:S(2)}, u32[]{:S(2)}) collective-permute-start(bf16[512,336]{1,0:T(8,128)(2,1)} %get-tuple-element.10.u_ref), channel_id=1, source_target_pairs={{0,1},{1,0},{2,3},{3,2},{4,5},{5,4},{6,7},{7,6},{8,9},{9,8},{10,11... | collective-permute-start | bytes 1032200 | tf_op jit(solution)/shard_map/ppermute | solution.py:302
  25.6 2.2 %copy-start = (bf16[1,6144,336]{1,2,0:T(8,128)(2,1)S(1)}, bf16[1,6144,336]{1,2,0:T(8,128)(2,1)}, u32[]{:S(2)}) copy-start(bf16[1,6144,336]{1,2,0:T(8,128)(2,1)} %param.7) | copy-start | bytes 12386308
  27.8 1.0 copy-start.2
  34.4 50.9 %all-to-all-start.1 = ((bf16[16,32,3072]{2,1,0:T(8,128)(2,1)}), bf16[16,32,3072]{2,1,0:T(8,128)(2,1)}, u32[]{:S(2)}, u32[]{:S(2)}) async-start(bf16[16,32,3072]{2,1,0:T(8,128)(2,1)} %bitcast.13), calls=%async_computation.1 | async-start | bytes 6291456 | tf_op jit(solution)/shard_map/all_to_all | solution.py:330
  41.4 11.4 %collective-permute-start.2 = (bf16[32,6272]{1,0:T(8,128)(2,1)S(1)}, bf16[32,6272]{1,0:T(8,128)(2,1)S(1)}, u32[]{:S(2)}, u32[]{:S(2)}) collective-permute-start(bf16[32,6272]{1,0:T(8,128)(2,1)S(1)} %shard_map.69), channel_id=1, source_target_pairs={{0,6},{2,4},{4,2},{6,0},{1,7},{3,5},{5,3},{7,1},{8,14},{10,12},{12... | collective-permute-start | bytes 1204232 | tf_op jit(solution)/shard_map/ppermute | solution.py:306
  43.1 37.3 %collective-permute-start.1 = (bf16[32,6272]{1,0:T(8,128)(2,1)S(1)}, bf16[32,6272]{1,0:T(8,128)(2,1)S(1)}, u32[]{:S(2)}, u32[]{:S(2)}) collective-permute-start(bf16[32,6272]{1,0:T(8,128)(2,1)S(1)} %shard_map.69), channel_id=1, source_target_pairs={{0,4},{2,6},{4,0},{6,2},{1,5},{3,7},{5,1},{7,3},{8,12},{10,14},{12... | collective-permute-start | bytes 1204232 | tf_op jit(solution)/shard_map/ppermute | solution.py:306
  46.5 33.9 %collective-permute-start = (bf16[32,6272]{1,0:T(8,128)(2,1)S(1)}, bf16[32,6272]{1,0:T(8,128)(2,1)S(1)}, u32[]{:S(2)}, u32[]{:S(2)}) collective-permute-start(bf16[32,6272]{1,0:T(8,128)(2,1)S(1)} %shard_map.69), channel_id=1, source_target_pairs={{0,2},{2,0},{4,6},{6,4},{1,3},{3,1},{5,7},{7,5},{8,10},{10,8},{12,... | collective-permute-start | bytes 1204232 | tf_op jit(solution)/shard_map/ppermute | solution.py:306
  80.5 3.6 %collective-permute-start.3 = (bf16[128,6272]{1,0:T(8,128)(2,1)S(1)}, bf16[128,6272]{1,0:T(8,128)(2,1)S(1)}, u32[]{:S(2)}, u32[]{:S(2)}) collective-permute-start(bf16[128,6272]{1,0:T(8,128)(2,1)S(1)} %pad_maximum_fusion.refs_0_), channel_id=1, source_target_pairs={{0,1},{1,0},{2,3},{3,2},{4,5},{5,4},{6,7},{7,6},{8,9},{9,8},{10,11... | collective-permute-start | bytes 4816904 | tf_op jit(solution)/shard_map/ppermute | solution.py:302
  81.0 36.7 %collective-permute-start.7 = (bf16[128,6272]{1,0:T(8,128)(2,1)S(1)}, bf16[128,6272]{1,0:T(8,128)(2,1)}, u32[]{:S(2)}, u32[]{:S(2)}) collective-permute-start(bf16[128,6272]{1,0:T(8,128)(2,1)S(1)} %pad_maximum_fusion.refs_0_), channel_id=1, source_target_pairs={{0,8},{8,0},{1,9},{9,1},{2,10},{10,2},{3,11},{11,3},{4,12},{12,4},... | collective-permute-start | bytes 4816904 | tf_op jit(solution)/shard_map/ppermute | solution.py:302
  88.0 0.8 copy-start.1
  88.8 29.8 %all-to-all-start.2 = ((bf16[8,8,4608]{2,1,0:T(8,128)(2,1)}), bf16[8,8,4608]{2,1,0:T(8,128)(2,1)}, u32[]{:S(2)}, u32[]{:S(2)}) async-start(bf16[8,8,4608]{2,1,0:T(8,128)(2,1)} %bitcast.25), calls=%async_computation.2 | async-start | bytes 1179648 | tf_op jit(solution)/shard_map/all_to_all | solution.py:342
  117.7 6.5 %collective-permute-start.8 = (bf16[128,6272]{1,0:T(8,128)(2,1)}, bf16[128,6272]{1,0:T(8,128)(2,1)}, u32[]{:S(2)}, u32[]{:S(2)}) collective-permute-start(bf16[128,6272]{1,0:T(8,128)(2,1)} %collective-permute-done.7.refs_1_), channel_id=1, source_target_pairs={{0,1},{1,0},{2,3},{3,2},{4,5},{5,4},{6,7},{7,6},{8,9},{9,8},{10,11... | collective-permute-start | bytes 4816904 | tf_op jit(solution)/shard_map/ppermute | solution.py:302
  120.5 0.6 copy-start.4
  121.1 1.6 %collective-permute-start.6 = (bf16[8,3072]{1,0:T(8,128)(2,1)}, bf16[8,3072]{1,0:T(8,128)(2,1)}, u32[]{:S(2)}, u32[]{:S(2)}) collective-permute-start(bf16[8,3072]{1,0:T(8,128)(2,1)} %get-tuple-element.13), channel_id=1, source_target_pairs={{0,1},{1,0},{2,3},{3,2},{4,5},{5,4},{6,7},{7,6},{8,9},{9,8},{10,11... | collective-permute-start | bytes 147464 | tf_op jit(solution)/shard_map/ppermute | solution.py:302
  121.1 1.0 copy-start.3

commit v8 on v7

--- a/solution.py
+++ b/solution.py
@@ -51,28 +51,6 @@
     )(gate_t, grad_t)
 
 
-def copy_kernel(core_ref, in_ref, out_ref):
-    out_ref[...] = in_ref[...]
-
-
-def other_half(core, weight_t):
-    hidden, width = weight_t.shape
-    block = 1024
-    steps = width // 2 // block
-    return pl.pallas_call(
-        copy_kernel,
-        grid_spec=pltpu.PrefetchScalarGridSpec(
-            num_scalar_prefetch=1,
-            grid=(steps,),
-            in_specs=[pl.BlockSpec((hidden, block), lambda i, core: (0, (1 - core[0]) * steps + i))],
-            out_specs=pl.BlockSpec((hidden, block), lambda i, core: (0, i)),
-        ),
-        out_shape=jax.ShapeDtypeStruct((hidden, width // 2), BF),
-        compiler_params=params(60),
-        cost_estimate=pl.CostEstimate(flops=0, bytes_accessed=4200000, transcendentals=0),
-    )(core, weight_t)
-
-
 def terms_kernel(core_ref, u_ref, v_ref, w_ref, x_ref, out_ref):
     term = jnp.dot(u_ref[...], w_ref[...], preferred_element_type=F32)
     term += jnp.dot(v_ref[...], x_ref[...], preferred_element_type=F32)
@@ -110,6 +88,14 @@
     for k in range(4):
         named += jnp.where(routes[:, k : k + 1] == expert, 1.0, 0.0)
     return named
+
+
+def front_kernel(core_ref, weight_ref, tokens_ref, routes_ref, give_ref, out_ref, held_ref, named_ref):
+    give_ref[...] = weight_ref[...]
+
+    @pl.when(pl.program_id(0) == 0)
+    def place():
+        place_kernel(tokens_ref, routes_ref, out_ref, held_ref, named_ref)
 
 
 def place_kernel(tokens_ref, routes_ref, out_ref, held_ref, named_ref):
@@ -134,14 +120,33 @@
     out_ref[:, FOLD:] = jnp.dot(spread, routes.astype(BF), preferred_element_type=F32).astype(BF)
 
 
-def placed_rows(tokens, routes):
-    return pl.pallas_call(
-        place_kernel,
-        out_shape=jax.ShapeDtypeStruct((256, FOLD + EXTRA), BF),
-        scratch_shapes=[pltpu.VMEM((PAD, tokens.shape[1]), F32), pltpu.VMEM((PAD, EXTRA), F32)],
+def front(core, weight_t, tokens, routes):
+    hidden, width = weight_t.shape
+    block = 1024
+    steps = width // 2 // block
+    return pl.pallas_call(
+        front_kernel,
+        grid_spec=pltpu.PrefetchScalarGridSpec(
+            num_scalar_prefetch=1,
+            grid=(steps,),
+            in_specs=[
+                pl.BlockSpec((hidden, block), lambda i, core: (0, (1 - core[0]) * steps + i)),
+                pl.BlockSpec(tokens.shape, lambda i, core: (0, 0)),
+                pl.BlockSpec(routes.shape, lambda i, core: (0, 0)),
+            ],
+            out_specs=[
+                pl.BlockSpec((hidden, block), lambda i, core: (0, i)),
+                pl.BlockSpec((256, FOLD + EXTRA), lambda i, core: (0, 0)),
+            ],
+            scratch_shapes=[pltpu.VMEM((PAD, tokens.shape[1]), F32), pltpu.VMEM((PAD, EXTRA), F32)],
+        ),
+        out_shape=(
+            jax.ShapeDtypeStruct((hidden, width // 2), BF),
+            jax.ShapeDtypeStruct((256, FOLD + EXTRA), BF),
+        ),
         compiler_params=params(60),
-        cost_estimate=pl.CostEstimate(flops=10**6, bytes_accessed=500000, transcendentals=0),
-    )(tokens, routes)
+        cost_estimate=pl.CostEstimate(flops=10**6, bytes_accessed=4700000, transcendentals=0),
+    )(core, weight_t, tokens, routes)
 
 
 def unfold_kernel(at_ref, rows_ref, out_ref):
@@ -316,13 +321,11 @@
     hidden, width = weight_t.shape
     half = width // 2
 
-    rows = placed_rows(tokens, routes.T)
-    rows, weight_t = lax.optimization_barrier((rows, weight_t))
+    give, rows = front(core[None], weight_t, tokens, routes.T)
     arrived = lax.all_to_all(
         rows.reshape(16, 16, FOLD + EXTRA), FAR, split_axis=0, concat_axis=0, tiled=True
     ).reshape(256, FOLD + EXTRA)
 
-    give = other_half(core[None], weight_t)
     other_t = swap(give, "c")
     ut, u = gated(jnp.swapaxes(gate_pre, 1, 2)[0], jnp.swapaxes(grad_hidden, 1, 2)[0])
     other_u = swap(u, "c")

time: 131 us -> 129 us (0.985)
  Pallas kernels: 25.8 us -> 24.3 us
    pallas_call x2 -> x1, Pallas kernels: 5.95 us -> 4.43 us  [front(): pl.pallas_call(front_kernel, grid_spec=pltpu.PrefetchScalarGridSpec(num_s...]
where the time goes in v8:
time: 129 us; the launch traced here: 128 us
  waiting for transfers between devices  61.8 us (48%)
  starting transfers between devices  34.4 us (27%)
  Pallas kernels  24.3 us (19%)
  local copies, waits for them, and re-layouts  5.57 us (4%)
  other arithmetic  1.67 us (1%)
    ppermute x3, waiting for transfers between devices, cross(): return lax.ppermute(value, 'zl', [(i, i ^ mask) for i in range(4)])  33.9 us
    ppermute x6, waiting for transfers between devices, swap(): return lax.ppermute(value, axis, [(0, 1), (1, 0)])  27.4 us
    all_to_all x1, starting transfers between devices, body(): lax.all_to_all(rows.reshape(16, 16, FOLD + EXTRA), FAR, split_axis=0, con...  11.6 us
    all_to_all x1, starting transfers between devices, body(): lax.all_to_all(terms.reshape(16, 32, half), PLANE, split_axis=0, concat_a...  6.31 us
    ppermute x6, starting transfers between devices, swap(): return lax.ppermute(value, axis, [(0, 1), (1, 0)])  6.28 us
    pallas_call x1, Pallas kernels, weight_grad(): pl.pallas_call(functools.partial(weight_kernel, len(blocks)), grid=(width...  5.82 us
    unnamed x10, local copies, waits for them, and re-layouts  5.57 us
    ppermute x3, starting transfers between devices, cross(): return lax.ppermute(value, 'zl', [(i, i ^ mask) for i in range(4)])  5.12 us
  transfers between devices with their start and end apart: 12, of which 7 were waited for; matrix products, arithmetic and copies ran while one was open for 1% of the time, Pallas kernels for 11%

profile of v8, /device:TPU:1, one launch (start us, length us, event | category | flops | bytes accessed | tf_op | source)
XLA Modules:
  0.0 128.5 jit_solution(10552496255446720221)
XLA Ops:
  0.6 4.4 %shard_map.68 = (bf16[336,3072]{1,0:T(8,128)(2,1)}, bf16[256,896]{1,0:T(8,128)(2,1)}) custom-call(s32[1]{0:T(128)} %bitcast.2.core_ref, bf16[336,6144]{1,0:T(8,128)(2,1)} %bitcast.23, bf16[6,6144]{1,0:T(8,128)(2,1)} %tokens_ref.1, s32[4,6]{1,0:T(4,128)} %bitcast.31), custom_call_target="tpu_custom_call" | custom-call | flops 1000000 | bytes 4700000 | tf_op jit(solution)/shard_map/pallas_call | solution.py:127
  5.1 3.2 %collective-permute-start.5 = (bf16[336,3072]{1,0:T(8,128)(2,1)}, bf16[336,3072]{1,0:T(8,128)(2,1)S(1)}, u32[]{:S(2)}, u32[]{:S(2)}) collective-permute-start(bf16[336,3072]{1,0:T(8,128)(2,1)} %get-tuple-element.11), channel_id=1, source_target_pairs={{0,1},{1,0},{2,3},{3,2},{4,5},{5,4},{6,7},{7,6},{8,9},{9,8},{10,11... | collective-permute-start | bytes 6193160 | tf_op jit(solution)/shard_map/ppermute | solution.py:307
  8.3 11.6 %all-to-all-start = ((bf16[16,16,896]{2,1,0:T(8,128)(2,1)}), bf16[16,16,896]{2,1,0:T(8,128)(2,1)S(1)}, u32[]{:S(2)}, u32[]{:S(2)}) async-start(bf16[16,16,896]{2,1,0:T(8,128)(2,1)} %bitcast.28), calls=%async_computation | async-start | bytes 917504 | tf_op jit(solution)/shard_map/all_to_all | solution.py:325
  20.0 2.2 %shard_map.71 = (bf16[336,512]{1,0:T(8,128)(2,1)}, bf16[512,336]{1,0:T(8,128)(2,1)}) custom-call(bf16[336,512]{1,0:T(8,128)(2,1)} %bitcast.29, bf16[336,512]{1,0:T(8,128)(2,1)} %bitcast.30), custom_call_target="tpu_custom_call" | custom-call | flops 1000000 | bytes 1400000 | tf_op jit(solution)/shard_map/pallas_call | solution.py:43
  22.1 0.3 collective-permute-start.4
  22.4 1.6 %collective-permute-done.4.v_ref = bf16[512,336]{1,0:T(8,128)(2,1)S(1)} collective-permute-done((bf16[512,336]{1,0:T(8,128)(2,1)}, bf16[512,336]{1,0:T(8,128)(2,1)S(1)}, u32[]{:S(2)}, u32[]{:S(2)}) %collective-permute-start.4) | collective-permute-done | bytes 344096 | tf_op jit(solution)/shard_map/ppermute | solution.py:307
  24.1 0.0 collective-permute-done.5.x_ref
  24.1 0.0 copy-start
  24.1 2.2 %copy-done = bf16[1,6144,336]{1,2,0:T(8,128)(2,1)S(1)} copy-done((bf16[1,6144,336]{1,2,0:T(8,128)(2,1)S(1)}, bf16[1,6144,336]{1,2,0:T(8,128)(2,1)}, u32[]{:S(2)}) %copy-start) | copy-done | bytes 4128792
  26.2 0.0 copy-start.2
  26.2 1.0 copy-done.2
  27.2 5.0 %shard_map.72 = bf16[16,2,16,3072]{3,2,1,0:T(8,128)(2,1)} custom-call(s32[1]{0:T(128)} %bitcast.2.core_ref, bf16[512,336]{1,0:T(8,128)(2,1)S(1)} %copy-done.2, bf16[512,336]{1,0:T(8,128)(2,1)S(1)} %collective-permute-done.4.v_ref, bf16[336,6144]{1,0:T(8,128)(2,1)S(1)} %bitcast.24, bf16[336,3072]{1,0:T(8,128)(2,1)S(1)} %collective-permute-done.5.x_ref), custom_call_target="tpu_custom_call" | custom-call | flops 2113929216 | bytes 8000000 | tf_op jit(solution)/shard_map/pallas_call | solution.py:67
  32.3 0.6 all-to-all-done
  32.9 6.3 %all-to-all-start.1 = ((bf16[16,32,3072]{2,1,0:T(8,128)(2,1)}), bf16[16,32,3072]{2,1,0:T(8,128)(2,1)}, u32[]{:S(2)}, u32[]{:S(2)}) async-start(bf16[16,32,3072]{2,1,0:T(8,128)(2,1)} %bitcast.14), calls=%async_computation.1 | async-start | bytes 6291456 | tf_op jit(solution)/shard_map/all_to_all | solution.py:333
  39.2 0.7 shard_map.69
  39.9 1.7 %collective-permute-start.2 = (bf16[32,6272]{1,0:T(8,128)(2,1)S(1)}, bf16[32,6272]{1,0:T(8,128)(2,1)S(1)}, u32[]{:S(2)}, u32[]{:S(2)}) collective-permute-start(bf16[32,6272]{1,0:T(8,128)(2,1)S(1)} %shard_map.69), channel_id=1, source_target_pairs={{0,6},{2,4},{4,2},{6,0},{1,7},{3,5},{5,3},{7,1},{8,14},{10,12},{12... | collective-permute-start | bytes 1204232 | tf_op jit(solution)/shard_map/ppermute | solution.py:311
  41.6 3.4 %collective-permute-start.1 = (bf16[32,6272]{1,0:T(8,128)(2,1)S(1)}, bf16[32,6272]{1,0:T(8,128)(2,1)S(1)}, u32[]{:S(2)}, u32[]{:S(2)}) collective-permute-start(bf16[32,6272]{1,0:T(8,128)(2,1)S(1)} %shard_map.69), channel_id=1, source_target_pairs={{0,4},{2,6},{4,0},{6,2},{1,5},{3,7},{5,1},{7,3},{8,12},{10,14},{12... | collective-permute-start | bytes 1204232 | tf_op jit(solution)/shard_map/ppermute | solution.py:311
  45.0 0.0 collective-permute-start
  45.0 6.3 %collective-permute-done.2 = bf16[32,6272]{1,0:T(8,128)(2,1)S(1)} collective-permute-done((bf16[32,6272]{1,0:T(8,128)(2,1)S(1)}, bf16[32,6272]{1,0:T(8,128)(2,1)S(1)}, u32[]{:S(2)}, u32[]{:S(2)}) %collective-permute-start.2) | collective-permute-done | bytes 401440 | tf_op jit(solution)/shard_map/ppermute | solution.py:311
  51.3 27.6 %collective-permute-done.1 = bf16[32,6272]{1,0:T(8,128)(2,1)S(1)} collective-permute-done((bf16[32,6272]{1,0:T(8,128)(2,1)S(1)}, bf16[32,6272]{1,0:T(8,128)(2,1)S(1)}, u32[]{:S(2)}, u32[]{:S(2)}) %collective-permute-start.1) | collective-permute-done | bytes 401440 | tf_op jit(solution)/shard_map/ppermute | solution.py:311
  78.9 0.0 collective-permute-done
  78.9 0.1 pad_maximum_fusion.refs_0_
  79.0 0.5 collective-permute-start.3
  79.5 1.3 %collective-permute-start.7 = (bf16[128,6272]{1,0:T(8,128)(2,1)S(1)}, bf16[128,6272]{1,0:T(8,128)(2,1)}, u32[]{:S(2)}, u32[]{:S(2)}) collective-permute-start(bf16[128,6272]{1,0:T(8,128)(2,1)S(1)} %pad_maximum_fusion.refs_0_), channel_id=1, source_target_pairs={{0,8},{8,0},{1,9},{9,1},{2,10},{10,2},{3,11},{11,3},{4,12},{12,4},... | collective-permute-start | bytes 4816904 | tf_op jit(solution)/shard_map/ppermute | solution.py:307
  80.8 0.1 pad_add_fusion.at_ref
  80.9 1.7 %collective-permute-done.3.refs_1_.refs_2_ = bf16[128,6272]{1,0:T(8,128)(2,1)S(1)} collective-permute-done((bf16[128,6272]{1,0:T(8,128)(2,1)S(1)}, bf16[128,6272]{1,0:T(8,128)(2,1)S(1)}, u32[]{:S(2)}, u32[]{:S(2)}) %collective-permute-start.3) | collective-permute-done | bytes 1605664 | tf_op jit(solution)/shard_map/ppermute | solution.py:307
  82.5 1.2 shard_map.70.choice_ref
  83.8 0.0 all-to-all-done.1
  83.8 2.7 %shard_map.73 = bf16[64,4608]{1,0:T(8,128)(2,1)S(1)} custom-call(bf16[192,512]{1,0:T(8,128)(2,1)S(1)} %shard_map.70.choice_ref, bf16[512,3072]{1,0:T(8,128)(2,1)} %bitcast.15.back_ref), custom_call_target="tpu_custom_call" | custom-call | flops 603979776 | bytes 4000000 | tf_op jit(solution)/shard_map/pallas_call | solution.py:227
  86.5 0.0 copy-start.1
  86.5 0.8 copy-done.1
  87.3 5.0 %all-to-all-start.2 = ((bf16[8,8,4608]{2,1,0:T(8,128)(2,1)}), bf16[8,8,4608]{2,1,0:T(8,128)(2,1)}, u32[]{:S(2)}, u32[]{:S(2)}) async-start(bf16[8,8,4608]{2,1,0:T(8,128)(2,1)} %bitcast.25), calls=%async_computation.2 | async-start | bytes 1179648 | tf_op jit(solution)/shard_map/all_to_all | solution.py:345
  92.3 23.8 %collective-permute-done.7.refs_1_ = bf16[128,6272]{1,0:T(8,128)(2,1)} collective-permute-done((bf16[128,6272]{1,0:T(8,128)(2,1)S(1)}, bf16[128,6272]{1,0:T(8,128)(2,1)}, u32[]{:S(2)}, u32[]{:S(2)}) %collective-permute-start.7) | collective-permute-done | bytes 1605664 | tf_op jit(solution)/shard_map/ppermute | solution.py:307
  116.1 0.9 collective-permute-start.8
  117.1 0.0 all-to-all-done.2.parts_ref
  117.1 1.9 %shard_map.74 = (bf16[8,3072]{1,0:T(8,128)(2,1)S(1)}, bf16[8,3072]{1,0:T(8,128)(2,1)}) custom-call(bf16[8,8,4608]{2,1,0:T(8,128)(2,1)} %all-to-all-done.2.parts_ref), custom_call_target="tpu_custom_call" | custom-call | flops 1000 | bytes 1000 | tf_op jit(solution)/shard_map/pallas_call | solution.py:258
  119.0 0.0 copy-start.4
  119.0 0.6 copy-done.4
  119.6 0.0 collective-permute-start.6
  119.6 0.0 copy-start.3
  119.6 1.0 copy-done.3
  120.6 0.4 shard_map.75.u_ref
  121.0 0.2 collective-permute-done.6
  121.2 0.8 broadcast_select_fusion.1
  122.0 0.6 pad_maximum_fusion.1
  122.7 0.0 collective-permute-done.8.refs_3_
  122.7 5.8 %shard_map.76 = bf16[336,6144]{1,0:T(8,128)(2,1)} custom-call(bf16[336,512]{1,0:T(8,128)(2,1)S(1)} %shard_map.75.u_ref, bf16[128,6272]{1,0:T(8,128)(2,1)S(1)} %pad_maximum_fusion.refs_0_, bf16[128,6272]{1,0:T(8,128)(2,1)} %collective-permute-done.7.refs_1_, bf16[128,6272]{1,0:T(8,128)(2,1)S(1)} %collective-permute-done.3.refs_1_.refs_2_, ...), custom_call_target="tpu_custom_call" | custom-call | flops 2113929216 | bytes 10420224 | tf_op jit(solution)/shard_map/pallas_call | solution.py:293
Async XLA Ops:
  5.1 19.0 %collective-permute-start.5 = (bf16[336,3072]{1,0:T(8,128)(2,1)}, bf16[336,3072]{1,0:T(8,128)(2,1)S(1)}, u32[]{:S(2)}, u32[]{:S(2)}) collective-permute-start(bf16[336,3072]{1,0:T(8,128)(2,1)} %get-tuple-element.11), channel_id=1, source_target_pairs={{0,1},{1,0},{2,3},{3,2},{4,5},{5,4},{6,7},{7,6},{8,9},{9,8},{10,11... | collective-permute-start | bytes 6193160 | tf_op jit(solution)/shard_map/ppermute | solution.py:307
  8.3 24.6 %all-to-all-start = ((bf16[16,16,896]{2,1,0:T(8,128)(2,1)}), bf16[16,16,896]{2,1,0:T(8,128)(2,1)S(1)}, u32[]{:S(2)}, u32[]{:S(2)}) async-start(bf16[16,16,896]{2,1,0:T(8,128)(2,1)} %bitcast.28), calls=%async_computation | async-start | bytes 917504 | tf_op jit(solution)/shard_map/all_to_all | solution.py:325
  22.1 1.9 %collective-permute-start.4 = (bf16[512,336]{1,0:T(8,128)(2,1)}, bf16[512,336]{1,0:T(8,128)(2,1)S(1)}, u32[]{:S(2)}, u32[]{:S(2)}) collective-permute-start(bf16[512,336]{1,0:T(8,128)(2,1)} %get-tuple-element.10.u_ref), channel_id=1, source_target_pairs={{0,1},{1,0},{2,3},{3,2},{4,5},{5,4},{6,7},{7,6},{8,9},{9,8},{10,11... | collective-permute-start | bytes 1032200 | tf_op jit(solution)/shard_map/ppermute | solution.py:307
  24.1 2.2 %copy-start = (bf16[1,6144,336]{1,2,0:T(8,128)(2,1)S(1)}, bf16[1,6144,336]{1,2,0:T(8,128)(2,1)}, u32[]{:S(2)}) copy-start(bf16[1,6144,336]{1,2,0:T(8,128)(2,1)} %param.7) | copy-start | bytes 12386308
  26.2 1.0 copy-start.2
  32.9 50.9 %all-to-all-start.1 = ((bf16[16,32,3072]{2,1,0:T(8,128)(2,1)}), bf16[16,32,3072]{2,1,0:T(8,128)(2,1)}, u32[]{:S(2)}, u32[]{:S(2)}) async-start(bf16[16,32,3072]{2,1,0:T(8,128)(2,1)} %bitcast.14), calls=%async_computation.1 | async-start | bytes 6291456 | tf_op jit(solution)/shard_map/all_to_all | solution.py:333
  39.9 11.4 %collective-permute-start.2 = (bf16[32,6272]{1,0:T(8,128)(2,1)S(1)}, bf16[32,6272]{1,0:T(8,128)(2,1)S(1)}, u32[]{:S(2)}, u32[]{:S(2)}) collective-permute-start(bf16[32,6272]{1,0:T(8,128)(2,1)S(1)} %shard_map.69), channel_id=1, source_target_pairs={{0,6},{2,4},{4,2},{6,0},{1,7},{3,5},{5,3},{7,1},{8,14},{10,12},{12... | collective-permute-start | bytes 1204232 | tf_op jit(solution)/shard_map/ppermute | solution.py:311
  41.6 37.3 %collective-permute-start.1 = (bf16[32,6272]{1,0:T(8,128)(2,1)S(1)}, bf16[32,6272]{1,0:T(8,128)(2,1)S(1)}, u32[]{:S(2)}, u32[]{:S(2)}) collective-permute-start(bf16[32,6272]{1,0:T(8,128)(2,1)S(1)} %shard_map.69), channel_id=1, source_target_pairs={{0,4},{2,6},{4,0},{6,2},{1,5},{3,7},{5,1},{7,3},{8,12},{10,14},{12... | collective-permute-start | bytes 1204232 | tf_op jit(solution)/shard_map/ppermute | solution.py:311
  45.0 33.9 %collective-permute-start = (bf16[32,6272]{1,0:T(8,128)(2,1)S(1)}, bf16[32,6272]{1,0:T(8,128)(2,1)S(1)}, u32[]{:S(2)}, u32[]{:S(2)}) collective-permute-start(bf16[32,6272]{1,0:T(8,128)(2,1)S(1)} %shard_map.69), channel_id=1, source_target_pairs={{0,2},{2,0},{4,6},{6,4},{1,3},{3,1},{5,7},{7,5},{8,10},{10,8},{12,... | collective-permute-start | bytes 1204232 | tf_op jit(solution)/shard_map/ppermute | solution.py:311
  79.0 3.6 %collective-permute-start.3 = (bf16[128,6272]{1,0:T(8,128)(2,1)S(1)}, bf16[128,6272]{1,0:T(8,128)(2,1)S(1)}, u32[]{:S(2)}, u32[]{:S(2)}) collective-permute-start(bf16[128,6272]{1,0:T(8,128)(2,1)S(1)} %pad_maximum_fusion.refs_0_), channel_id=1, source_target_pairs={{0,1},{1,0},{2,3},{3,2},{4,5},{5,4},{6,7},{7,6},{8,9},{9,8},{10,11... | collective-permute-start | bytes 4816904 | tf_op jit(solution)/shard_map/ppermute | solution.py:307
  79.5 36.7 %collective-permute-start.7 = (bf16[128,6272]{1,0:T(8,128)(2,1)S(1)}, bf16[128,6272]{1,0:T(8,128)(2,1)}, u32[]{:S(2)}, u32[]{:S(2)}) collective-permute-start(bf16[128,6272]{1,0:T(8,128)(2,1)S(1)} %pad_maximum_fusion.refs_0_), channel_id=1, source_target_pairs={{0,8},{8,0},{1,9},{9,1},{2,10},{10,2},{3,11},{11,3},{4,12},{12,4},... | collective-permute-start | bytes 4816904 | tf_op jit(solution)/shard_map/ppermute | solution.py:307
  86.5 0.8 copy-start.1
  87.3 29.8 %all-to-all-start.2 = ((bf16[8,8,4608]{2,1,0:T(8,128)(2,1)}), bf16[8,8,4608]{2,1,0:T(8,128)(2,1)}, u32[]{:S(2)}, u32[]{:S(2)}) async-start(bf16[8,8,4608]{2,1,0:T(8,128)(2,1)} %bitcast.25), calls=%async_computation.2 | async-start | bytes 1179648 | tf_op jit(solution)/shard_map/all_to_all | solution.py:345
  116.1 6.5 %collective-permute-start.8 = (bf16[128,6272]{1,0:T(8,128)(2,1)}, bf16[128,6272]{1,0:T(8,128)(2,1)}, u32[]{:S(2)}, u32[]{:S(2)}) collective-permute-start(bf16[128,6272]{1,0:T(8,128)(2,1)} %collective-permute-done.7.refs_1_), channel_id=1, source_target_pairs={{0,1},{1,0},{2,3},{3,2},{4,5},{5,4},{6,7},{7,6},{8,9},{9,8},{10,11... | collective-permute-start | bytes 4816904 | tf_op jit(solution)/shard_map/ppermute | solution.py:307
  119.0 0.6 copy-start.4
  119.6 1.6 %collective-permute-start.6 = (bf16[8,3072]{1,0:T(8,128)(2,1)}, bf16[8,3072]{1,0:T(8,128)(2,1)}, u32[]{:S(2)}, u32[]{:S(2)}) collective-permute-start(bf16[8,3072]{1,0:T(8,128)(2,1)} %get-tuple-element.13), channel_id=1, source_target_pairs={{0,1},{1,0},{2,3},{3,2},{4,5},{5,4},{6,7},{7,6},{8,9},{9,8},{10,11... | collective-permute-start | bytes 147464 | tf_op jit(solution)/shard_map/ppermute | solution.py:307
  119.6 1.0 copy-start.3

commit v9 on v8

--- a/solution.py
+++ b/solution.py
@@ -346,12 +346,14 @@
         sums.reshape(8, PAD, half + half // 2), RING, split_axis=0, concat_axis=0, tiled=True
     )
 
+    mine, other = totalled(parts)
+    other = swap(other, "c")
+
     pair = lax.optimization_barrier((pair, sums))[0]
+    pair, other = lax.optimization_barrier((pair, other))
     rows = [run, pair, other_run, swap(pair, "c")]
     grad = weight_grad(u_rows, rows, width, 2048)
 
-    mine, other = totalled(parts)
-    other = swap(other, "c")
     left, right = jnp.where(core == 0, mine, other), jnp.where(core == 0, other, mine)
     grad_rows = jnp.concatenate([left, right], axis=1)[:TOK]
     return (grad_rows, jnp.swapaxes(grad[None], 1, 2))

time: 129 us -> 128 us (level)
  blocking collectives: 0 us -> 23.2 us
  waiting for transfers between devices: 61.8 us -> 42.6 us
  starting transfers between devices: 34.4 us -> 30.8 us
  Pallas kernels: 24.3 us -> 22.6 us
    all_to_all x0 -> x1, blocking collectives: none -> 23.2 us  [body(): lax.all_to_all(sums.reshape(8, PAD, half + half // 2), RING, split_axis=0...]
    ppermute x6, waiting for transfers between devices: 27.4 us -> 8.08 us  [swap(): return lax.ppermute(value, axis, [(0, 1), (1, 0)])]
    all_to_all x1 -> x0, starting transfers between devices: 5.02 us -> none  [body(): lax.all_to_all(sums.reshape(8, PAD, half + half // 2), RING, split_axis=0...]
    pallas_call x1, Pallas kernels: 1.9 us -> 0.2 us  [totalled(): pl.pallas_call(total_kernel, out_shape=(like, like), compiler_params=para...]
    ppermute x6, starting transfers between devices: 6.28 us -> 7.73 us  [swap(): return lax.ppermute(value, axis, [(0, 1), (1, 0)])]
  transfers between devices with their start and end apart: 12 -> 11, of which waited for: 7 -> 7; matrix products, arithmetic and copies ran while one was open for 1% -> 1% of each run, Pallas kernels for 11% -> 10%
where the time goes in v9:
time: 128 us; the launch traced here: 127 us
  waiting for transfers between devices  42.6 us (33%)
  starting transfers between devices  30.8 us (24%)
  blocking collectives  23.2 us (18%)
  Pallas kernels  22.6 us (18%)
  local copies, waits for them, and re-layouts  5.38 us (4%)
  other arithmetic  1.67 us (1%)
    ppermute x3, waiting for transfers between devices, cross(): return lax.ppermute(value, 'zl', [(i, i ^ mask) for i in range(4)])  33.9 us
    all_to_all x1, blocking collectives, body(): lax.all_to_all(sums.reshape(8, PAD, half + half // 2), RING, split_axis=0...  23.2 us
    all_to_all x1, starting transfers between devices, body(): lax.all_to_all(rows.reshape(16, 16, FOLD + EXTRA), FAR, split_axis=0, con...  11.6 us
    ppermute x6, waiting for transfers between devices, swap(): return lax.ppermute(value, axis, [(0, 1), (1, 0)])  8.08 us
    ppermute x6, starting transfers between devices, swap(): return lax.ppermute(value, axis, [(0, 1), (1, 0)])  7.73 us
    all_to_all x1, starting transfers between devices, body(): lax.all_to_all(terms.reshape(16, 32, half), PLANE, split_axis=0, concat_a...  6.32 us
    pallas_call x1, Pallas kernels, weight_grad(): pl.pallas_call(functools.partial(weight_kernel, len(blocks)), grid=(width...  5.82 us
    unnamed x10, local copies, waits for them, and re-layouts  5.38 us
  transfers between devices with their start and end apart: 11, of which 7 were waited for; matrix products, arithmetic and copies ran while one was open for 1% of the time, Pallas kernels for 10%

profile of v9, /device:TPU:1, one launch (start us, length us, event | category | flops | bytes accessed | tf_op | source)
XLA Modules:
  0.0 127.0 jit_solution(1154212306543135255)
XLA Ops:
  0.6 4.4 %shard_map.68 = (bf16[336,3072]{1,0:T(8,128)(2,1)}, bf16[256,896]{1,0:T(8,128)(2,1)}) custom-call(s32[1]{0:T(128)} %bitcast.2.core_ref, bf16[336,6144]{1,0:T(8,128)(2,1)} %bitcast.23, bf16[6,6144]{1,0:T(8,128)(2,1)} %tokens_ref.1, s32[4,6]{1,0:T(4,128)} %bitcast.31), custom_call_target="tpu_custom_call" | custom-call | flops 1000000 | bytes 4700000 | tf_op jit(solution)/shard_map/pallas_call | solution.py:127
  5.1 3.2 %collective-permute-start.5 = (bf16[336,3072]{1,0:T(8,128)(2,1)}, bf16[336,3072]{1,0:T(8,128)(2,1)S(1)}, u32[]{:S(2)}, u32[]{:S(2)}) collective-permute-start(bf16[336,3072]{1,0:T(8,128)(2,1)} %get-tuple-element.13), channel_id=1, source_target_pairs={{0,1},{1,0},{2,3},{3,2},{4,5},{5,4},{6,7},{7,6},{8,9},{9,8},{10,11... | collective-permute-start | bytes 6193160 | tf_op jit(solution)/shard_map/ppermute | solution.py:307
  8.3 11.6 %all-to-all-start = ((bf16[16,16,896]{2,1,0:T(8,128)(2,1)}), bf16[16,16,896]{2,1,0:T(8,128)(2,1)S(1)}, u32[]{:S(2)}, u32[]{:S(2)}) async-start(bf16[16,16,896]{2,1,0:T(8,128)(2,1)} %bitcast.28), calls=%async_computation | async-start | bytes 917504 | tf_op jit(solution)/shard_map/all_to_all | solution.py:325
  20.0 2.2 %shard_map.71 = (bf16[336,512]{1,0:T(8,128)(2,1)}, bf16[512,336]{1,0:T(8,128)(2,1)}) custom-call(bf16[336,512]{1,0:T(8,128)(2,1)} %bitcast.29, bf16[336,512]{1,0:T(8,128)(2,1)} %bitcast.30), custom_call_target="tpu_custom_call" | custom-call | flops 1000000 | bytes 1400000 | tf_op jit(solution)/shard_map/pallas_call | solution.py:43
  22.1 0.3 collective-permute-start.4
  22.4 1.6 %collective-permute-done.4.v_ref = bf16[512,336]{1,0:T(8,128)(2,1)S(1)} collective-permute-done((bf16[512,336]{1,0:T(8,128)(2,1)}, bf16[512,336]{1,0:T(8,128)(2,1)S(1)}, u32[]{:S(2)}, u32[]{:S(2)}) %collective-permute-start.4) | collective-permute-done | bytes 344096 | tf_op jit(solution)/shard_map/ppermute | solution.py:307
  24.1 0.0 collective-permute-done.5.x_ref
  24.1 0.0 copy-start
  24.1 2.2 %copy-done = bf16[1,6144,336]{1,2,0:T(8,128)(2,1)S(1)} copy-done((bf16[1,6144,336]{1,2,0:T(8,128)(2,1)S(1)}, bf16[1,6144,336]{1,2,0:T(8,128)(2,1)}, u32[]{:S(2)}) %copy-start) | copy-done | bytes 4128792
  26.2 0.0 copy-start.1
  26.2 1.0 copy-done.1
  27.2 5.0 %shard_map.72 = bf16[16,2,16,3072]{3,2,1,0:T(8,128)(2,1)} custom-call(s32[1]{0:T(128)} %bitcast.2.core_ref, bf16[512,336]{1,0:T(8,128)(2,1)S(1)} %copy-done.1, bf16[512,336]{1,0:T(8,128)(2,1)S(1)} %collective-permute-done.4.v_ref, bf16[336,6144]{1,0:T(8,128)(2,1)S(1)} %bitcast.24, bf16[336,3072]{1,0:T(8,128)(2,1)S(1)} %collective-permute-done.5.x_ref), custom_call_target="tpu_custom_call" | custom-call | flops 2113929216 | bytes 8000000 | tf_op jit(solution)/shard_map/pallas_call | solution.py:67
  32.3 0.6 all-to-all-done
  32.9 6.3 %all-to-all-start.1 = ((bf16[16,32,3072]{2,1,0:T(8,128)(2,1)}), bf16[16,32,3072]{2,1,0:T(8,128)(2,1)}, u32[]{:S(2)}, u32[]{:S(2)}) async-start(bf16[16,32,3072]{2,1,0:T(8,128)(2,1)} %bitcast.14), calls=%async_computation.1 | async-start | bytes 6291456 | tf_op jit(solution)/shard_map/all_to_all | solution.py:333
  39.2 0.7 shard_map.69
  39.9 1.7 %collective-permute-start.2 = (bf16[32,6272]{1,0:T(8,128)(2,1)S(1)}, bf16[32,6272]{1,0:T(8,128)(2,1)S(1)}, u32[]{:S(2)}, u32[]{:S(2)}) collective-permute-start(bf16[32,6272]{1,0:T(8,128)(2,1)S(1)} %shard_map.69), channel_id=1, source_target_pairs={{0,6},{2,4},{4,2},{6,0},{1,7},{3,5},{5,3},{7,1},{8,14},{10,12},{12... | collective-permute-start | bytes 1204232 | tf_op jit(solution)/shard_map/ppermute | solution.py:311
  41.6 3.4 %collective-permute-start.1 = (bf16[32,6272]{1,0:T(8,128)(2,1)S(1)}, bf16[32,6272]{1,0:T(8,128)(2,1)S(1)}, u32[]{:S(2)}, u32[]{:S(2)}) collective-permute-start(bf16[32,6272]{1,0:T(8,128)(2,1)S(1)} %shard_map.69), channel_id=1, source_target_pairs={{0,4},{2,6},{4,0},{6,2},{1,5},{3,7},{5,1},{7,3},{8,12},{10,14},{12... | collective-permute-start | bytes 1204232 | tf_op jit(solution)/shard_map/ppermute | solution.py:311
  45.0 0.0 collective-permute-start
  45.0 6.3 %collective-permute-done.2 = bf16[32,6272]{1,0:T(8,128)(2,1)S(1)} collective-permute-done((bf16[32,6272]{1,0:T(8,128)(2,1)S(1)}, bf16[32,6272]{1,0:T(8,128)(2,1)S(1)}, u32[]{:S(2)}, u32[]{:S(2)}) %collective-permute-start.2) | collective-permute-done | bytes 401440 | tf_op jit(solution)/shard_map/ppermute | solution.py:311
  51.3 27.6 %collective-permute-done.1 = bf16[32,6272]{1,0:T(8,128)(2,1)S(1)} collective-permute-done((bf16[32,6272]{1,0:T(8,128)(2,1)S(1)}, bf16[32,6272]{1,0:T(8,128)(2,1)S(1)}, u32[]{:S(2)}, u32[]{:S(2)}) %collective-permute-start.1) | collective-permute-done | bytes 401440 | tf_op jit(solution)/shard_map/ppermute | solution.py:311
  78.9 0.0 collective-permute-done
  78.9 0.1 pad_maximum_fusion.refs_0_
  79.0 0.5 collective-permute-start.3
  79.5 1.3 %collective-permute-start.6 = (bf16[128,6272]{1,0:T(8,128)(2,1)S(1)}, bf16[128,6272]{1,0:T(8,128)(2,1)}, u32[]{:S(2)}, u32[]{:S(2)}) collective-permute-start(bf16[128,6272]{1,0:T(8,128)(2,1)S(1)} %pad_maximum_fusion.refs_0_), channel_id=1, source_target_pairs={{0,8},{8,0},{1,9},{9,1},{2,10},{10,2},{3,11},{11,3},{4,12},{12,4},... | collective-permute-start | bytes 4816904 | tf_op jit(solution)/shard_map/ppermute | solution.py:307
  80.8 0.1 pad_add_fusion.at_ref
  80.9 1.7 %collective-permute-done.3.refs_1_.refs_2_ = bf16[128,6272]{1,0:T(8,128)(2,1)S(1)} collective-permute-done((bf16[128,6272]{1,0:T(8,128)(2,1)S(1)}, bf16[128,6272]{1,0:T(8,128)(2,1)S(1)}, u32[]{:S(2)}, u32[]{:S(2)}) %collective-permute-start.3) | collective-permute-done | bytes 1605664 | tf_op jit(solution)/shard_map/ppermute | solution.py:307
  82.5 1.2 shard_map.70.choice_ref
  83.8 0.0 all-to-all-done.1
  83.8 2.7 %shard_map.73 = bf16[64,4608]{1,0:T(8,128)(2,1)S(1)} custom-call(bf16[192,512]{1,0:T(8,128)(2,1)S(1)} %shard_map.70.choice_ref, bf16[512,3072]{1,0:T(8,128)(2,1)} %bitcast.15.back_ref), custom_call_target="tpu_custom_call" | custom-call | flops 603979776 | bytes 4000000 | tf_op jit(solution)/shard_map/pallas_call | solution.py:227
  86.5 23.2 %all_to_all.15.parts_ref = bf16[8,8,4608]{2,1,0:T(8,128)(2,1)S(1)} all-to-all(bf16[8,8,4608]{2,1,0:T(8,128)(2,1)S(1)} %bitcast.25), channel_id=1, replica_groups=mesh['zh'=2,'x'=4,'yp'=2,'yi'=2,'zl'=4,'c'=2] {'zh','zl'}, dimensions={0} | all-to-all | bytes 1179648 | tf_op jit(solution)/shard_map/all_to_all | solution.py:345
  109.7 0.2 shard_map.74
  109.9 0.0 copy-start.3
  109.9 0.6 copy-done.3
  110.5 1.5 %collective-permute-start.7 = (bf16[8,3072]{1,0:T(8,128)(2,1)S(1)}, bf16[8,3072]{1,0:T(8,128)(2,1)S(1)}, u32[]{:S(2)}, u32[]{:S(2)}) collective-permute-start(bf16[8,3072]{1,0:T(8,128)(2,1)S(1)} %get-tuple-element.16), channel_id=1, source_target_pairs={{0,1},{1,0},{2,3},{3,2},{4,5},{5,4},{6,7},{7,6},{8,9},{9,8},{10,11... | collective-permute-start | bytes 147464 | tf_op jit(solution)/shard_map/ppermute | solution.py:307
  112.0 4.2 %collective-permute-done.6.refs_1_ = bf16[128,6272]{1,0:T(8,128)(2,1)} collective-permute-done((bf16[128,6272]{1,0:T(8,128)(2,1)S(1)}, bf16[128,6272]{1,0:T(8,128)(2,1)}, u32[]{:S(2)}, u32[]{:S(2)}) %collective-permute-start.6) | collective-permute-done | bytes 1605664 | tf_op jit(solution)/shard_map/ppermute | solution.py:307
  116.1 0.0 collective-permute-done.7
  116.1 0.0 copy-start.4
  116.1 0.6 copy-done.4
  116.8 0.9 collective-permute-start.8
  117.7 0.0 copy-start.2
  117.7 1.0 copy-done.2
  118.7 0.4 shard_map.75.u_ref
  119.1 0.8 broadcast_select_fusion.1
  119.9 0.6 pad_maximum_fusion.1
  120.5 0.6 collective-permute-done.8.refs_3_
  121.1 5.8 %shard_map.76 = bf16[336,6144]{1,0:T(8,128)(2,1)} custom-call(bf16[336,512]{1,0:T(8,128)(2,1)S(1)} %shard_map.75.u_ref, bf16[128,6272]{1,0:T(8,128)(2,1)S(1)} %pad_maximum_fusion.refs_0_, bf16[128,6272]{1,0:T(8,128)(2,1)} %collective-permute-done.6.refs_1_, bf16[128,6272]{1,0:T(8,128)(2,1)S(1)} %collective-permute-done.3.refs_1_.refs_2_, ...), custom_call_target="tpu_custom_call" | custom-call | flops 2113929216 | bytes 10420224 | tf_op jit(solution)/shard_map/pallas_call | solution.py:293
Async XLA Ops:
  5.1 19.0 %collective-permute-start.5 = (bf16[336,3072]{1,0:T(8,128)(2,1)}, bf16[336,3072]{1,0:T(8,128)(2,1)S(1)}, u32[]{:S(2)}, u32[]{:S(2)}) collective-permute-start(bf16[336,3072]{1,0:T(8,128)(2,1)} %get-tuple-element.13), channel_id=1, source_target_pairs={{0,1},{1,0},{2,3},{3,2},{4,5},{5,4},{6,7},{7,6},{8,9},{9,8},{10,11... | collective-permute-start | bytes 6193160 | tf_op jit(solution)/shard_map/ppermute | solution.py:307
  8.3 24.6 %all-to-all-start = ((bf16[16,16,896]{2,1,0:T(8,128)(2,1)}), bf16[16,16,896]{2,1,0:T(8,128)(2,1)S(1)}, u32[]{:S(2)}, u32[]{:S(2)}) async-start(bf16[16,16,896]{2,1,0:T(8,128)(2,1)} %bitcast.28), calls=%async_computation | async-start | bytes 917504 | tf_op jit(solution)/shard_map/all_to_all | solution.py:325
  22.1 1.9 %collective-permute-start.4 = (bf16[512,336]{1,0:T(8,128)(2,1)}, bf16[512,336]{1,0:T(8,128)(2,1)S(1)}, u32[]{:S(2)}, u32[]{:S(2)}) collective-permute-start(bf16[512,336]{1,0:T(8,128)(2,1)} %get-tuple-element.12.u_ref), channel_id=1, source_target_pairs={{0,1},{1,0},{2,3},{3,2},{4,5},{5,4},{6,7},{7,6},{8,9},{9,8},{10,11... | collective-permute-start | bytes 1032200 | tf_op jit(solution)/shard_map/ppermute | solution.py:307
  24.1 2.2 %copy-start = (bf16[1,6144,336]{1,2,0:T(8,128)(2,1)S(1)}, bf16[1,6144,336]{1,2,0:T(8,128)(2,1)}, u32[]{:S(2)}) copy-start(bf16[1,6144,336]{1,2,0:T(8,128)(2,1)} %param.7) | copy-start | bytes 12386308
  26.2 1.0 copy-start.1
  32.9 50.9 %all-to-all-start.1 = ((bf16[16,32,3072]{2,1,0:T(8,128)(2,1)}), bf16[16,32,3072]{2,1,0:T(8,128)(2,1)}, u32[]{:S(2)}, u32[]{:S(2)}) async-start(bf16[16,32,3072]{2,1,0:T(8,128)(2,1)} %bitcast.14), calls=%async_computation.1 | async-start | bytes 6291456 | tf_op jit(solution)/shard_map/all_to_all | solution.py:333
  39.9 11.4 %collective-permute-start.2 = (bf16[32,6272]{1,0:T(8,128)(2,1)S(1)}, bf16[32,6272]{1,0:T(8,128)(2,1)S(1)}, u32[]{:S(2)}, u32[]{:S(2)}) collective-permute-start(bf16[32,6272]{1,0:T(8,128)(2,1)S(1)} %shard_map.69), channel_id=1, source_target_pairs={{0,6},{2,4},{4,2},{6,0},{1,7},{3,5},{5,3},{7,1},{8,14},{10,12},{12... | collective-permute-start | bytes 1204232 | tf_op jit(solution)/shard_map/ppermute | solution.py:311
  41.6 37.3 %collective-permute-start.1 = (bf16[32,6272]{1,0:T(8,128)(2,1)S(1)}, bf16[32,6272]{1,0:T(8,128)(2,1)S(1)}, u32[]{:S(2)}, u32[]{:S(2)}) collective-permute-start(bf16[32,6272]{1,0:T(8,128)(2,1)S(1)} %shard_map.69), channel_id=1, source_target_pairs={{0,4},{2,6},{4,0},{6,2},{1,5},{3,7},{5,1},{7,3},{8,12},{10,14},{12... | collective-permute-start | bytes 1204232 | tf_op jit(solution)/shard_map/ppermute | solution.py:311
  45.0 33.9 %collective-permute-start = (bf16[32,6272]{1,0:T(8,128)(2,1)S(1)}, bf16[32,6272]{1,0:T(8,128)(2,1)S(1)}, u32[]{:S(2)}, u32[]{:S(2)}) collective-permute-start(bf16[32,6272]{1,0:T(8,128)(2,1)S(1)} %shard_map.69), channel_id=1, source_target_pairs={{0,2},{2,0},{4,6},{6,4},{1,3},{3,1},{5,7},{7,5},{8,10},{10,8},{12,... | collective-permute-start | bytes 1204232 | tf_op jit(solution)/shard_map/ppermute | solution.py:311
  79.0 3.6 %collective-permute-start.3 = (bf16[128,6272]{1,0:T(8,128)(2,1)S(1)}, bf16[128,6272]{1,0:T(8,128)(2,1)S(1)}, u32[]{:S(2)}, u32[]{:S(2)}) collective-permute-start(bf16[128,6272]{1,0:T(8,128)(2,1)S(1)} %pad_maximum_fusion.refs_0_), channel_id=1, source_target_pairs={{0,1},{1,0},{2,3},{3,2},{4,5},{5,4},{6,7},{7,6},{8,9},{9,8},{10,11... | collective-permute-start | bytes 4816904 | tf_op jit(solution)/shard_map/ppermute | solution.py:307
  79.5 36.7 %collective-permute-start.6 = (bf16[128,6272]{1,0:T(8,128)(2,1)S(1)}, bf16[128,6272]{1,0:T(8,128)(2,1)}, u32[]{:S(2)}, u32[]{:S(2)}) collective-permute-start(bf16[128,6272]{1,0:T(8,128)(2,1)S(1)} %pad_maximum_fusion.refs_0_), channel_id=1, source_target_pairs={{0,8},{8,0},{1,9},{9,1},{2,10},{10,2},{3,11},{11,3},{4,12},{12,4},... | collective-permute-start | bytes 4816904 | tf_op jit(solution)/shard_map/ppermute | solution.py:307
  109.9 0.6 copy-start.3
  110.5 5.6 %collective-permute-start.7 = (bf16[8,3072]{1,0:T(8,128)(2,1)S(1)}, bf16[8,3072]{1,0:T(8,128)(2,1)S(1)}, u32[]{:S(2)}, u32[]{:S(2)}) collective-permute-start(bf16[8,3072]{1,0:T(8,128)(2,1)S(1)} %get-tuple-element.16), channel_id=1, source_target_pairs={{0,1},{1,0},{2,3},{3,2},{4,5},{5,4},{6,7},{7,6},{8,9},{9,8},{10,11... | collective-permute-start | bytes 147464 | tf_op jit(solution)/shard_map/ppermute | solution.py:307
  116.1 0.6 copy-start.4
  116.8 4.4 %collective-permute-start.8 = (bf16[128,6272]{1,0:T(8,128)(2,1)}, bf16[128,6272]{1,0:T(8,128)(2,1)}, u32[]{:S(2)}, u32[]{:S(2)}) collective-permute-start(bf16[128,6272]{1,0:T(8,128)(2,1)} %collective-permute-done.6.refs_1_), channel_id=1, source_target_pairs={{0,1},{1,0},{2,3},{3,2},{4,5},{5,4},{6,7},{7,6},{8,9},{9,8},{10,11... | collective-permute-start | bytes 4816904 | tf_op jit(solution)/shard_map/ppermute | solution.py:307
  117.7 1.0 copy-start.2

commit v10 on v9

--- a/solution.py
+++ b/solution.py
@@ -12,7 +12,7 @@
 AXES = ("zh", "x", "yp", "yi", "zl", "c")
 SIZES = (2, 4, 2, 2, 4, 2)
 FAR = ("x", "yp", "zh")
-PLANE = ("x", "yp", "yi")
+PLANE = ("yp", "yi", "x")
 RING = ("zh", "zl")
 TOK = 6
 PAD = 8
@@ -55,8 +55,9 @@
     term = jnp.dot(u_ref[...], w_ref[...], preferred_element_type=F32)
     term += jnp.dot(v_ref[...], x_ref[...], preferred_element_type=F32)
     term = term.astype(BF).reshape(2, 16, 16, term.shape[1])
-    out_ref[:, 0, :, :] = term[0]
-    out_ref[:, 1, :, :] = term[1]
+    for zh in range(2):
+        for place in range(16):
+            out_ref[place % 4 * 4 + place // 4, zh, :, :] = term[zh, place]
 
 
 def terms_of(core, u, v, weight_t, other_t):
@@ -175,7 +176,7 @@
     out_ref = refs[-1]
     shape = (8 * 2 * PAD, 512)
     row, column = iota(shape, 0), iota(shape, 1)
-    expert = at_ref[0] * 8 + column // 64
+    expert = at_ref[0] * 8 + column // 32 % 4 * 2 + column // 256
     routes = jnp.concatenate([ref[...] for ref in refs[:-1]], axis=0)
     r, s = iota((128, 256), 0), iota((128, 256), 1)
     came = (r // 8) % 2 * 128 + jnp.bitwise_xor((r // 16) % 4, at_ref[1]) * 32 + r // 64 * 8 + r % 8

time: 128 us -> 130 us (1.016)
  starting transfers between devices: 30.8 us -> 32.7 us
    ppermute x6, waiting for transfers between devices: 8.08 us -> 5.7 us  [swap(): return lax.ppermute(value, axis, [(0, 1), (1, 0)])]
    ppermute x6, starting transfers between devices: 7.73 us -> 9.65 us  [swap(): return lax.ppermute(value, axis, [(0, 1), (1, 0)])]
    all_to_all x1, waiting for transfers between devices: 0.01 us -> 1.35 us  [body(): lax.all_to_all(terms.reshape(16, 32, half), PLANE, split_axis=0, concat_a...]
  transfers between devices with their start and end apart: 11 -> 11, of which waited for: 7 -> 8; matrix products, arithmetic and copies ran while one was open for 1% -> 1% of each run, Pallas kernels for 10% -> 10%
where the time goes in v10:
time: 130 us; the launch traced here: 129 us
  waiting for transfers between devices  41.4 us (32%)
  starting transfers between devices  32.7 us (25%)
  blocking collectives  24.3 us (19%)
  Pallas kernels  22.6 us (17%)
  local copies, waits for them, and re-layouts  5.38 us (4%)
  other arithmetic  1.67 us (1%)
    ppermute x3, waiting for transfers between devices, cross(): return lax.ppermute(value, 'zl', [(i, i ^ mask) for i in range(4)])  33.8 us
    all_to_all x1, blocking collectives, body(): lax.all_to_all(sums.reshape(8, PAD, half + half // 2), RING, split_axis=0...  24.3 us
    all_to_all x1, starting transfers between devices, body(): lax.all_to_all(rows.reshape(16, 16, FOLD + EXTRA), FAR, split_axis=0, con...  11.6 us
    ppermute x6, starting transfers between devices, swap(): return lax.ppermute(value, axis, [(0, 1), (1, 0)])  9.65 us
    all_to_all x1, starting transfers between devices, body(): lax.all_to_all(terms.reshape(16, 32, half), PLANE, split_axis=0, concat_a...  6.32 us
    pallas_call x1, Pallas kernels, weight_grad(): pl.pallas_call(functools.partial(weight_kernel, len(blocks)), grid=(width...  5.82 us
    ppermute x6, waiting for transfers between devices, swap(): return lax.ppermute(value, axis, [(0, 1), (1, 0)])  5.7 us
    unnamed x10, local copies, waits for them, and re-layouts  5.38 us
  transfers between devices with their start and end apart: 11, of which 8 were waited for; matrix products, arithmetic and copies ran while one was open for 1% of the time, Pallas kernels for 10%

profile of v10, /device:TPU:1, one launch (start us, length us, event | category | flops | bytes accessed | tf_op | source)
XLA Modules:
  0.0 128.8 jit_solution(3371123107402479375)
XLA Ops:
  0.6 4.4 %shard_map.68 = (bf16[336,3072]{1,0:T(8,128)(2,1)}, bf16[256,896]{1,0:T(8,128)(2,1)}) custom-call(s32[1]{0:T(128)} %bitcast.2.core_ref, bf16[336,6144]{1,0:T(8,128)(2,1)} %bitcast.23, bf16[6,6144]{1,0:T(8,128)(2,1)} %tokens_ref.1, s32[4,6]{1,0:T(4,128)} %bitcast.31), custom_call_target="tpu_custom_call" | custom-call | flops 1000000 | bytes 4700000 | tf_op jit(solution)/shard_map/pallas_call | solution.py:128
  5.1 3.2 %collective-permute-start.5 = (bf16[336,3072]{1,0:T(8,128)(2,1)}, bf16[336,3072]{1,0:T(8,128)(2,1)S(1)}, u32[]{:S(2)}, u32[]{:S(2)}) collective-permute-start(bf16[336,3072]{1,0:T(8,128)(2,1)} %get-tuple-element.13), channel_id=1, source_target_pairs={{0,1},{1,0},{2,3},{3,2},{4,5},{5,4},{6,7},{7,6},{8,9},{9,8},{10,11... | collective-permute-start | bytes 6193160 | tf_op jit(solution)/shard_map/ppermute | solution.py:308
  8.3 11.6 %all-to-all-start = ((bf16[16,16,896]{2,1,0:T(8,128)(2,1)}), bf16[16,16,896]{2,1,0:T(8,128)(2,1)S(1)}, u32[]{:S(2)}, u32[]{:S(2)}) async-start(bf16[16,16,896]{2,1,0:T(8,128)(2,1)} %bitcast.28), calls=%async_computation | async-start | bytes 917504 | tf_op jit(solution)/shard_map/all_to_all | solution.py:326
  20.0 2.2 %shard_map.71 = (bf16[336,512]{1,0:T(8,128)(2,1)}, bf16[512,336]{1,0:T(8,128)(2,1)}) custom-call(bf16[336,512]{1,0:T(8,128)(2,1)} %bitcast.29, bf16[336,512]{1,0:T(8,128)(2,1)} %bitcast.30), custom_call_target="tpu_custom_call" | custom-call | flops 1000000 | bytes 1400000 | tf_op jit(solution)/shard_map/pallas_call | solution.py:43
  22.1 0.3 collective-permute-start.4
  22.4 1.6 %collective-permute-done.4.v_ref = bf16[512,336]{1,0:T(8,128)(2,1)S(1)} collective-permute-done((bf16[512,336]{1,0:T(8,128)(2,1)}, bf16[512,336]{1,0:T(8,128)(2,1)S(1)}, u32[]{:S(2)}, u32[]{:S(2)}) %collective-permute-start.4) | collective-permute-done | bytes 344096 | tf_op jit(solution)/shard_map/ppermute | solution.py:308
  24.1 0.0 collective-permute-done.5.x_ref
  24.1 0.0 copy-start
  24.1 2.2 %copy-done = bf16[1,6144,336]{1,2,0:T(8,128)(2,1)S(1)} copy-done((bf16[1,6144,336]{1,2,0:T(8,128)(2,1)S(1)}, bf16[1,6144,336]{1,2,0:T(8,128)(2,1)}, u32[]{:S(2)}) %copy-start) | copy-done | bytes 4128792
  26.2 0.0 copy-start.1
  26.2 1.0 copy-done.1
  27.2 5.0 %shard_map.72 = bf16[16,2,16,3072]{3,2,1,0:T(8,128)(2,1)} custom-call(s32[1]{0:T(128)} %bitcast.2.core_ref, bf16[512,336]{1,0:T(8,128)(2,1)S(1)} %copy-done.1, bf16[512,336]{1,0:T(8,128)(2,1)S(1)} %collective-permute-done.4.v_ref, bf16[336,6144]{1,0:T(8,128)(2,1)S(1)} %bitcast.24, bf16[336,3072]{1,0:T(8,128)(2,1)S(1)} %collective-permute-done.5.x_ref), custom_call_target="tpu_custom_call" | custom-call | flops 2113929216 | bytes 8000000 | tf_op jit(solution)/shard_map/pallas_call | solution.py:68
  32.3 0.6 all-to-all-done
  32.9 6.3 %all-to-all-start.1 = ((bf16[16,32,3072]{2,1,0:T(8,128)(2,1)}), bf16[16,32,3072]{2,1,0:T(8,128)(2,1)}, u32[]{:S(2)}, u32[]{:S(2)}) async-start(bf16[16,32,3072]{2,1,0:T(8,128)(2,1)} %bitcast.14), calls=%async_computation.1 | async-start | bytes 6291456 | tf_op jit(solution)/shard_map/all_to_all | solution.py:334
  39.2 0.7 shard_map.69
  39.9 1.7 %collective-permute-start.2 = (bf16[32,6272]{1,0:T(8,128)(2,1)S(1)}, bf16[32,6272]{1,0:T(8,128)(2,1)S(1)}, u32[]{:S(2)}, u32[]{:S(2)}) collective-permute-start(bf16[32,6272]{1,0:T(8,128)(2,1)S(1)} %shard_map.69), channel_id=1, source_target_pairs={{0,6},{2,4},{4,2},{6,0},{1,7},{3,5},{5,3},{7,1},{8,14},{10,12},{12... | collective-permute-start | bytes 1204232 | tf_op jit(solution)/shard_map/ppermute | solution.py:312
  41.6 3.4 %collective-permute-start.1 = (bf16[32,6272]{1,0:T(8,128)(2,1)S(1)}, bf16[32,6272]{1,0:T(8,128)(2,1)S(1)}, u32[]{:S(2)}, u32[]{:S(2)}) collective-permute-start(bf16[32,6272]{1,0:T(8,128)(2,1)S(1)} %shard_map.69), channel_id=1, source_target_pairs={{0,4},{2,6},{4,0},{6,2},{1,5},{3,7},{5,1},{7,3},{8,12},{10,14},{12... | collective-permute-start | bytes 1204232 | tf_op jit(solution)/shard_map/ppermute | solution.py:312
  45.0 0.0 collective-permute-start
  45.0 6.4 %collective-permute-done.2 = bf16[32,6272]{1,0:T(8,128)(2,1)S(1)} collective-permute-done((bf16[32,6272]{1,0:T(8,128)(2,1)S(1)}, bf16[32,6272]{1,0:T(8,128)(2,1)S(1)}, u32[]{:S(2)}, u32[]{:S(2)}) %collective-permute-start.2) | collective-permute-done | bytes 401440 | tf_op jit(solution)/shard_map/ppermute | solution.py:312
  51.4 27.3 %collective-permute-done.1 = bf16[32,6272]{1,0:T(8,128)(2,1)S(1)} collective-permute-done((bf16[32,6272]{1,0:T(8,128)(2,1)S(1)}, bf16[32,6272]{1,0:T(8,128)(2,1)S(1)}, u32[]{:S(2)}, u32[]{:S(2)}) %collective-permute-start.1) | collective-permute-done | bytes 401440 | tf_op jit(solution)/shard_map/ppermute | solution.py:312
  78.8 0.0 collective-permute-done
  78.8 0.1 pad_maximum_fusion.refs_0_
  78.9 0.6 collective-permute-start.3
  79.5 1.3 %collective-permute-start.6 = (bf16[128,6272]{1,0:T(8,128)(2,1)S(1)}, bf16[128,6272]{1,0:T(8,128)(2,1)}, u32[]{:S(2)}, u32[]{:S(2)}) collective-permute-start(bf16[128,6272]{1,0:T(8,128)(2,1)S(1)} %pad_maximum_fusion.refs_0_), channel_id=1, source_target_pairs={{0,8},{8,0},{1,9},{9,1},{2,10},{10,2},{3,11},{11,3},{4,12},{12,4},... | collective-permute-start | bytes 4816904 | tf_op jit(solution)/shard_map/ppermute | solution.py:308
  80.8 0.1 pad_add_fusion.at_ref
  80.9 1.7 %collective-permute-done.3.refs_1_.refs_2_ = bf16[128,6272]{1,0:T(8,128)(2,1)S(1)} collective-permute-done((bf16[128,6272]{1,0:T(8,128)(2,1)S(1)}, bf16[128,6272]{1,0:T(8,128)(2,1)S(1)}, u32[]{:S(2)}, u32[]{:S(2)}) %collective-permute-start.3) | collective-permute-done | bytes 1605664 | tf_op jit(solution)/shard_map/ppermute | solution.py:308
  82.5 1.2 shard_map.70.choice_ref
  83.8 1.3 %all-to-all-done.1 = bf16[16,32,3072]{2,1,0:T(8,128)(2,1)} async-done(((bf16[16,32,3072]{2,1,0:T(8,128)(2,1)}), bf16[16,32,3072]{2,1,0:T(8,128)(2,1)}, u32[]{:S(2)}, u32[]{:S(2)}) %all-to-all-start.1) | async-done | bytes 3145760 | tf_op jit(solution)/shard_map/all_to_all | solution.py:334
  85.1 2.7 %shard_map.73 = bf16[64,4608]{1,0:T(8,128)(2,1)S(1)} custom-call(bf16[192,512]{1,0:T(8,128)(2,1)S(1)} %shard_map.70.choice_ref, bf16[512,3072]{1,0:T(8,128)(2,1)} %bitcast.15.back_ref), custom_call_target="tpu_custom_call" | custom-call | flops 603979776 | bytes 4000000 | tf_op jit(solution)/shard_map/pallas_call | solution.py:228
  87.8 24.3 %all_to_all.15.parts_ref = bf16[8,8,4608]{2,1,0:T(8,128)(2,1)S(1)} all-to-all(bf16[8,8,4608]{2,1,0:T(8,128)(2,1)S(1)} %bitcast.25), channel_id=1, replica_groups=mesh['zh'=2,'x'=4,'yp'=2,'yi'=2,'zl'=4,'c'=2] {'zh','zl'}, dimensions={0} | all-to-all | bytes 1179648 | tf_op jit(solution)/shard_map/all_to_all | solution.py:346
  112.1 0.2 shard_map.74
  112.3 0.0 copy-start.3
  112.3 0.6 copy-done.3
  112.9 3.5 %collective-permute-start.7 = (bf16[8,3072]{1,0:T(8,128)(2,1)S(1)}, bf16[8,3072]{1,0:T(8,128)(2,1)S(1)}, u32[]{:S(2)}, u32[]{:S(2)}) collective-permute-start(bf16[8,3072]{1,0:T(8,128)(2,1)S(1)} %get-tuple-element.16), channel_id=1, source_target_pairs={{0,1},{1,0},{2,3},{3,2},{4,5},{5,4},{6,7},{7,6},{8,9},{9,8},{10,11... | collective-permute-start | bytes 147464 | tf_op jit(solution)/shard_map/ppermute | solution.py:308
  116.4 1.8 %collective-permute-done.6.refs_1_ = bf16[128,6272]{1,0:T(8,128)(2,1)} collective-permute-done((bf16[128,6272]{1,0:T(8,128)(2,1)S(1)}, bf16[128,6272]{1,0:T(8,128)(2,1)}, u32[]{:S(2)}, u32[]{:S(2)}) %collective-permute-start.6) | collective-permute-done | bytes 1605664 | tf_op jit(solution)/shard_map/ppermute | solution.py:308
  118.2 0.0 collective-permute-done.7
  118.2 0.0 copy-start.4
  118.2 0.6 copy-done.4
  118.8 0.7 collective-permute-start.8
  119.5 0.0 copy-start.2
  119.5 1.0 copy-done.2
  120.5 0.4 shard_map.75.u_ref
  120.9 0.8 broadcast_select_fusion.1
  121.7 0.6 pad_maximum_fusion.1
  122.3 0.6 collective-permute-done.8.refs_3_
  122.9 5.8 %shard_map.76 = bf16[336,6144]{1,0:T(8,128)(2,1)} custom-call(bf16[336,512]{1,0:T(8,128)(2,1)S(1)} %shard_map.75.u_ref, bf16[128,6272]{1,0:T(8,128)(2,1)S(1)} %pad_maximum_fusion.refs_0_, bf16[128,6272]{1,0:T(8,128)(2,1)} %collective-permute-done.6.refs_1_, bf16[128,6272]{1,0:T(8,128)(2,1)S(1)} %collective-permute-done.3.refs_1_.refs_2_, ...), custom_call_target="tpu_custom_call" | custom-call | flops 2113929216 | bytes 10420224 | tf_op jit(solution)/shard_map/pallas_call | solution.py:294
Async XLA Ops:
  5.1 19.0 %collective-permute-start.5 = (bf16[336,3072]{1,0:T(8,128)(2,1)}, bf16[336,3072]{1,0:T(8,128)(2,1)S(1)}, u32[]{:S(2)}, u32[]{:S(2)}) collective-permute-start(bf16[336,3072]{1,0:T(8,128)(2,1)} %get-tuple-element.13), channel_id=1, source_target_pairs={{0,1},{1,0},{2,3},{3,2},{4,5},{5,4},{6,7},{7,6},{8,9},{9,8},{10,11... | collective-permute-start | bytes 6193160 | tf_op jit(solution)/shard_map/ppermute | solution.py:308
  8.3 24.6 %all-to-all-start = ((bf16[16,16,896]{2,1,0:T(8,128)(2,1)}), bf16[16,16,896]{2,1,0:T(8,128)(2,1)S(1)}, u32[]{:S(2)}, u32[]{:S(2)}) async-start(bf16[16,16,896]{2,1,0:T(8,128)(2,1)} %bitcast.28), calls=%async_computation | async-start | bytes 917504 | tf_op jit(solution)/shard_map/all_to_all | solution.py:326
  22.1 1.9 %collective-permute-start.4 = (bf16[512,336]{1,0:T(8,128)(2,1)}, bf16[512,336]{1,0:T(8,128)(2,1)S(1)}, u32[]{:S(2)}, u32[]{:S(2)}) collective-permute-start(bf16[512,336]{1,0:T(8,128)(2,1)} %get-tuple-element.12.u_ref), channel_id=1, source_target_pairs={{0,1},{1,0},{2,3},{3,2},{4,5},{5,4},{6,7},{7,6},{8,9},{9,8},{10,11... | collective-permute-start | bytes 1032200 | tf_op jit(solution)/shard_map/ppermute | solution.py:308
  24.1 2.2 %copy-start = (bf16[1,6144,336]{1,2,0:T(8,128)(2,1)S(1)}, bf16[1,6144,336]{1,2,0:T(8,128)(2,1)}, u32[]{:S(2)}) copy-start(bf16[1,6144,336]{1,2,0:T(8,128)(2,1)} %param.7) | copy-start | bytes 12386308
  26.2 1.0 copy-start.1
  32.9 52.2 %all-to-all-start.1 = ((bf16[16,32,3072]{2,1,0:T(8,128)(2,1)}), bf16[16,32,3072]{2,1,0:T(8,128)(2,1)}, u32[]{:S(2)}, u32[]{:S(2)}) async-start(bf16[16,32,3072]{2,1,0:T(8,128)(2,1)} %bitcast.14), calls=%async_computation.1 | async-start | bytes 6291456 | tf_op jit(solution)/shard_map/all_to_all | solution.py:334
  39.9 11.5 %collective-permute-start.2 = (bf16[32,6272]{1,0:T(8,128)(2,1)S(1)}, bf16[32,6272]{1,0:T(8,128)(2,1)S(1)}, u32[]{:S(2)}, u32[]{:S(2)}) collective-permute-start(bf16[32,6272]{1,0:T(8,128)(2,1)S(1)} %shard_map.69), channel_id=1, source_target_pairs={{0,6},{2,4},{4,2},{6,0},{1,7},{3,5},{5,3},{7,1},{8,14},{10,12},{12... | collective-permute-start | bytes 1204232 | tf_op jit(solution)/shard_map/ppermute | solution.py:312
  41.6 37.2 %collective-permute-start.1 = (bf16[32,6272]{1,0:T(8,128)(2,1)S(1)}, bf16[32,6272]{1,0:T(8,128)(2,1)S(1)}, u32[]{:S(2)}, u32[]{:S(2)}) collective-permute-start(bf16[32,6272]{1,0:T(8,128)(2,1)S(1)} %shard_map.69), channel_id=1, source_target_pairs={{0,4},{2,6},{4,0},{6,2},{1,5},{3,7},{5,1},{7,3},{8,12},{10,14},{12... | collective-permute-start | bytes 1204232 | tf_op jit(solution)/shard_map/ppermute | solution.py:312
  45.0 33.8 %collective-permute-start = (bf16[32,6272]{1,0:T(8,128)(2,1)S(1)}, bf16[32,6272]{1,0:T(8,128)(2,1)S(1)}, u32[]{:S(2)}, u32[]{:S(2)}) collective-permute-start(bf16[32,6272]{1,0:T(8,128)(2,1)S(1)} %shard_map.69), channel_id=1, source_target_pairs={{0,2},{2,0},{4,6},{6,4},{1,3},{3,1},{5,7},{7,5},{8,10},{10,8},{12,... | collective-permute-start | bytes 1204232 | tf_op jit(solution)/shard_map/ppermute | solution.py:312
  78.9 3.7 %collective-permute-start.3 = (bf16[128,6272]{1,0:T(8,128)(2,1)S(1)}, bf16[128,6272]{1,0:T(8,128)(2,1)S(1)}, u32[]{:S(2)}, u32[]{:S(2)}) collective-permute-start(bf16[128,6272]{1,0:T(8,128)(2,1)S(1)} %pad_maximum_fusion.refs_0_), channel_id=1, source_target_pairs={{0,1},{1,0},{2,3},{3,2},{4,5},{5,4},{6,7},{7,6},{8,9},{9,8},{10,11... | collective-permute-start | bytes 4816904 | tf_op jit(solution)/shard_map/ppermute | solution.py:308
  79.5 38.7 %collective-permute-start.6 = (bf16[128,6272]{1,0:T(8,128)(2,1)S(1)}, bf16[128,6272]{1,0:T(8,128)(2,1)}, u32[]{:S(2)}, u32[]{:S(2)}) collective-permute-start(bf16[128,6272]{1,0:T(8,128)(2,1)S(1)} %pad_maximum_fusion.refs_0_), channel_id=1, source_target_pairs={{0,8},{8,0},{1,9},{9,1},{2,10},{10,2},{3,11},{11,3},{4,12},{12,4},... | collective-permute-start | bytes 4816904 | tf_op jit(solution)/shard_map/ppermute | solution.py:308
  112.3 0.6 copy-start.3
  112.9 5.3 %collective-permute-start.7 = (bf16[8,3072]{1,0:T(8,128)(2,1)S(1)}, bf16[8,3072]{1,0:T(8,128)(2,1)S(1)}, u32[]{:S(2)}, u32[]{:S(2)}) collective-permute-start(bf16[8,3072]{1,0:T(8,128)(2,1)S(1)} %get-tuple-element.16), channel_id=1, source_target_pairs={{0,1},{1,0},{2,3},{3,2},{4,5},{5,4},{6,7},{7,6},{8,9},{9,8},{10,11... | collective-permute-start | bytes 147464 | tf_op jit(solution)/shard_map/ppermute | solution.py:308
  118.2 0.6 copy-start.4
  118.8 4.1 %collective-permute-start.8 = (bf16[128,6272]{1,0:T(8,128)(2,1)}, bf16[128,6272]{1,0:T(8,128)(2,1)}, u32[]{:S(2)}, u32[]{:S(2)}) collective-permute-start(bf16[128,6272]{1,0:T(8,128)(2,1)} %collective-permute-done.6.refs_1_), channel_id=1, source_target_pairs={{0,1},{1,0},{2,3},{3,2},{4,5},{5,4},{6,7},{7,6},{8,9},{9,8},{10,11... | collective-permute-start | bytes 4816904 | tf_op jit(solution)/shard_map/ppermute | solution.py:308
  119.5 1.0 copy-start.2
